TPU v7x, 32 devices: a whole 2x2x4 slice. The times are simulated.
32 devices in a mesh: dp: 4 (over y, core), fsdp: 8 (over z, x).
Axes of the slice: x: 2, y: 2, z: 4, core: 2. Of those that a mesh axis runs over, the one named last changes fastest.
Arguments:
- frames: bfloat16 [81920, 512], P(('dp', 'fsdp')), may hold values from -6 to 6
- memory: bfloat16 [16384, 512], P(('dp', 'fsdp')), may hold values from -6 to 6
- left_keys: bfloat16 [122880, 512], P(('dp', 'fsdp')), may hold values from -6 to 6
- left_values: bfloat16 [122880, 512], P(('dp', 'fsdp')), may hold values from -6 to 6
- lengths: int32 [4096], P(('dp', 'fsdp')), may hold values from 4 to 16
- cotangent: bfloat16 [81920, 512], P(('dp', 'fsdp')), may hold values from -6 to 6
- attn_w: float32 [4, 512, 512], P(None, 'fsdp'), as said below
- ffn_in: float32 [512, 2048], P('fsdp'), may hold values from -0.25 to 0.25
- ffn_out: float32 [2048, 512], P('fsdp'), may hold values from -0.125 to 0.125
- norm_params: float32 [4, 512], P(None, 'fsdp'), as said below
- attn_m: float32 [4, 512, 512], P(None, 'fsdp'), as said below
- attn_v: float32 [4, 512, 512], P(None, 'fsdp'), as said below
- ffn_in_m: float32 [512, 2048], P('fsdp'), as said below
- ffn_in_v: float32 [512, 2048], P('fsdp'), as said below
- ffn_out_m: float32 [2048, 512], P('fsdp'), as said below
- ffn_out_v: float32 [2048, 512], P('fsdp'), as said below
- norm_m: float32 [4, 512], P(None, 'fsdp'), as said below
- norm_v: float32 [4, 512], P(None, 'fsdp'), as said below
Outputs:
- output: bfloat16 [81920, 512], P(('dp', 'fsdp'))
- input_grad: float32 [81920, 512], P(('dp', 'fsdp'))
- attn_grad: float32 [4, 512, 512], P(None, 'fsdp')
- attn_first: float32 [4, 512, 512], P(None, 'fsdp')
- attn_second: float32 [4, 512, 512], P(None, 'fsdp')
- attn_new: float32 [4, 512, 512], P(None, 'fsdp')
- attn_copy: bfloat16 [4, 512, 512], P(None, 'fsdp')
- in_grad: float32 [512, 2048], P('fsdp')
- in_first: float32 [512, 2048], P('fsdp')
- in_second: float32 [512, 2048], P('fsdp')
- in_new: float32 [512, 2048], P('fsdp')
- in_copy: bfloat16 [512, 2048], P('fsdp')
- out_grad: float32 [2048, 512], P('fsdp')
- out_first: float32 [2048, 512], P('fsdp')
- out_second: float32 [2048, 512], P('fsdp')
- out_new: float32 [2048, 512], P('fsdp')
- out_copy: bfloat16 [2048, 512], P('fsdp')
- norm_grad: float32 [4, 512], P(None, 'fsdp')
- norm_first: float32 [4, 512], P(None, 'fsdp')
- norm_second: float32 [4, 512], P(None, 'fsdp')
- norm_new: float32 [4, 512], P(None, 'fsdp')
- norm_copy: bfloat16 [4, 512], P(None, 'fsdp')
Inputs may be any that keep to these rules, and one draw needn't show every extreme that they name: attn_w holds four independent 512 x 512 matrices of entries. `norm_params`: gains near 1, shifts near 0. `attn_v`: positive entries. `ffn_in_v`: positive entries. `ffn_out_v`: positive entries. `norm_v`: positive entries. `attn_m`: entries of both signs. `ffn_in_m`: entries of both signs. `ffn_out_m`: entries of both signs. `norm_m`: entries of both signs.
All inputs are finite; a program needn't handle non-finite values.
Results may differ from a plain program's by a relative error of at most 0.024.
Values may be sent and summed in bfloat16 or wider, within the bound.
No kernel may reach another device: no remote copies, remote signals or barrier semaphores. Data moves between devices by JAX's collectives and lax.ppermute only.
A program may use at most 320 MiB of HBM per device.

v0:
```python
import functools
import math

import jax
import jax.numpy as jnp
import numpy as np
from jax import lax
from jax.experimental import pallas as pl
from jax.experimental.pallas import tpu as pltpu
from jax.sharding import PartitionSpec as P

D = 512
FF = 2048
HEADS = 8
SEG = 16
LEFT = 30
MEM = 4
STEP = 5
ROWS_SPAN = 20
GROUP = 4
QROWS = GROUP * ROWS_SPAN
MROWS = GROUP * MEM
LROWS = GROUP * LEFT
LWIN = 128
KPAD = 256
HALF = 256
PAIR = 128
NORM_ROWS = 16

F32 = jnp.float32
BF16 = jnp.bfloat16
BLOCKED = -1e9
EPS_NORM = 1e-05
BETA_FIRST = 0.5
BETA_SECOND = 0.5
WEIGHT_DECAY = 0.01
EPS_ADAM = 1e-08
RATES_ATTENTION = (0.04, 0.04, 0.04, 0.25)
RATE_FFN_IN = 0.04
RATE_FFN_OUT = 0.02
RATE_NORM = 0.2
VMEM_LIMIT = 56 * 2**20


def dot(a, b):
    return lax.dot_general(a, b, (((1,), (0,)), ((), ())), preferred_element_type=F32)


def dot_last(a, b):
    return lax.dot_general(a, b, (((1,), (1,)), ((), ())), preferred_element_type=F32)


def dot_rows(a, b):
    return lax.dot_general(a, b, (((0,), (0,)), ((), ())), preferred_element_type=F32)


def normalize(x):
    mean = jnp.mean(x, axis=1, keepdims=True)
    centred = x - mean
    variance = jnp.mean(centred * centred, axis=1, keepdims=True)
    scale = lax.rsqrt(variance + EPS_NORM)
    return centred * scale, scale


def norm_back(grad, normed, scale, gain):
    grad = grad * gain
    first = jnp.mean(grad, axis=1, keepdims=True)
    second = jnp.mean(grad * normed, axis=1, keepdims=True)
    return scale * (grad - first - normed * second)


def gelu_parts(x):
    c = math.sqrt(2.0 / math.pi)
    square = x * x
    t = jnp.tanh(x * (c + (c * 0.044715) * square))
    half = 0.5 * x
    value = half + half * t
    slope = 0.5 + 0.5 * t + half * (1.0 - t * t) * (c + (3.0 * c * 0.044715) * square)
    return value, slope


def spread_pair(x):
    lane = lax.broadcasted_iota(jnp.int32, x.shape, 1)
    zero = jnp.zeros_like(x)
    return jnp.concatenate([jnp.where(lane < 64, x, zero), jnp.where(lane < 64, zero, x)], axis=0)


def join_pair(x):
    rows = x.shape[0] // 2
    lane = lax.broadcasted_iota(jnp.int32, (rows, PAIR), 1)
    return jnp.where(lane < 64, x[:rows], x[rows:])


def left_start(g):
    return LROWS * g - (8 if g % 2 else 0)


def span_masks():
    query_span = np.arange(2 * QROWS) % QROWS // ROWS_SPAN
    masks = np.full((2, 2 * QROWS, KPAD), BLOCKED, np.float32)
    for odd in range(2):
        span = np.full(KPAD, -1)
        span[:MROWS] = np.arange(MROWS) // MEM
        span[MROWS : MROWS + QROWS] = np.arange(QROWS) // ROWS_SPAN
        start = MROWS + QROWS + (8 if odd else 0)
        span[start : start + LROWS] = np.arange(LROWS) // LEFT
        masks[odd][query_span[:, None] == span[None, :]] = 0.0
    return masks


def length_bias(lengths):
    groups = lengths.shape[0] // GROUP
    key = np.arange(KPAD)
    is_frame = (key >= MROWS) & (key < MROWS + QROWS)
    place = np.where(is_frame, (key - MROWS) % ROWS_SPAN, 0)
    span = np.where(is_frame, (key - MROWS) // ROWS_SPAN, 0)
    own = lengths.reshape(groups, GROUP)
    length = jnp.zeros((groups, KPAD), jnp.int32)
    for s in range(GROUP):
        length = jnp.where(jnp.asarray(span == s)[None, :], own[:, s : s + 1], length)
    dead = jnp.asarray(is_frame & (place < SEG))[None, :] & (jnp.asarray(place)[None, :] >= length)
    return jnp.where(dead, BLOCKED, 0.0).astype(F32).reshape(groups, 1, KPAD)


def adamw(weight, grad, first_old, second_old, rate):
    first = BETA_FIRST * first_old + (1.0 - BETA_FIRST) * grad
    second = BETA_SECOND * second_old + (1.0 - BETA_SECOND) * grad * grad
    first_hat = first / (1.0 - BETA_FIRST**STEP)
    second_hat = second / (1.0 - BETA_SECOND**STEP)
    new = weight - rate * (first_hat / (jnp.sqrt(second_hat) + EPS_ADAM) + WEIGHT_DECAY * weight)
    return first, second, new


class Places:
    def __init__(self, mesh):
        self.n = mesh.shape["fsdp"]
        self.dp = mesh.shape["dp"]
        power = max(int(math.log2(self.n)) - 1, 0) // 2
        self.X = 2**power
        self.Z = self.n // self.X
        self.C = 2
        self.Y = self.dp // self.C

    def me(self):
        f = lax.axis_index("fsdp")
        d = lax.axis_index("dp")
        return jnp.stack([f // self.X, f % self.X, d % self.C, d // self.C]).astype(jnp.int32)

    def slot_to(self, me_ref, f):
        dz = lax.rem(f // self.X + self.Z - me_ref[0], self.Z)
        dx = lax.rem(f % self.X + self.X - me_ref[1], self.X)
        return dx * self.Z + dz

    def slot_from(self, me_ref, f):
        dz = lax.rem(me_ref[0] + self.Z - f // self.X, self.Z)
        dx = lax.rem(me_ref[1] + self.X - f % self.X, self.X)
        return dx * self.Z + dz

    def shift(self, value, dz, dx):
        X, Z = self.X, self.Z
        perm = [
            (z * X + x, (z + dz) % Z * X + (x + dx) % X) for z in range(Z) for x in range(X)
        ]
        return lax.ppermute(value, "fsdp", perm)

    def y_joined(self, me_ref, ref):
        slots = [lax.rem(me_ref[3] + self.Y - y, self.Y) for y in range(self.Y)]
        return jnp.concatenate([ref[slot] for slot in slots], axis=0)

    def y_slot_to(self, me_ref, y):
        return lax.rem(y + self.Y - me_ref[3], self.Y)

    def shift_y(self, value, dy):
        dp = self.dp
        return lax.ppermute(value, "dp", [(d, (d + 2 * dy) % dp) for d in range(dp)])

    def other_core(self, value):
        return lax.ppermute(value, "dp", [(d, d ^ 1) for d in range(self.dp)])

    def sum_over_y(self, value):
        step = 1
        while step < self.Y:
            got = lax.ppermute(value, "dp", [(d, d ^ (2 * step)) for d in range(self.dp)])
            value = (value.astype(F32) + got.astype(F32)).astype(BF16)
            step *= 2
        return value


def call(kernel, me, grid, ins, outs, scratch, name, flops=0, moved=0, aliases=None):
    def spec(block, index):
        if block is None:
            return pl.BlockSpec(memory_space=pl.ANY)
        return pl.BlockSpec(block, lambda *a: index(*a[:-1]))

    return pl.pallas_call(
        kernel,
        grid_spec=pltpu.PrefetchScalarGridSpec(
            num_scalar_prefetch=1,
            grid=grid,
            in_specs=[spec(b, f) for _, b, f in ins],
            out_specs=[spec(b, f) for _, _, b, f in outs],
            scratch_shapes=scratch,
        ),
        out_shape=[jax.ShapeDtypeStruct(s, d) for s, d, _, _ in outs],
        compiler_params=pltpu.CompilerParams(vmem_limit_bytes=VMEM_LIMIT),
        cost_estimate=pl.CostEstimate(flops=flops, bytes_accessed=moved, transcendentals=0),
        input_output_aliases=aliases or {},
        name=name,
    )(me, *[a for a, _, _ in ins])


def whole(shape):
    return shape, lambda i: (0,) * len(shape)


def rows_of(shape, column=0):
    return shape, lambda i: (i, column)


def pack_first(me, attn_w, norm_params, places):
    r = D // places.n
    h = r // 2

    def kernel(me_ref, w_ref, n_ref, out_ref, scratch):
        lower = me_ref[2] == 0
        for k in range(3):
            w = w_ref[k]
            out_ref[k * h : (k + 1) * h, :] = jnp.where(lower, w[:h], w[h:]).astype(BF16)
        scratch[...] = jnp.zeros_like(scratch)
        scratch[0:4, 0:r] = n_ref[...]
        out_ref[3 * h :, :] = scratch[...].astype(BF16)

    (out,) = call(
        kernel,
        me,
        (1,),
        [
            (attn_w, (3, r, HALF), lambda i: (0, 0, 0)),
            (norm_params, *whole((4, r))),
        ],
        [((3 * h + NORM_ROWS, HALF), BF16, *whole((3 * h + NORM_ROWS, HALF)))],
        [pltpu.VMEM((NORM_ROWS, HALF), F32)],
        "pack_first",
        moved=4 * 3 * r * HALF,
    )
    return out


def pack_rest(me, attn_w, ffn_in, ffn_out, places):
    r, r2 = D // places.n, FF // places.n
    h, q = r // 2, r2 // places.dp

    def kernel(me_ref, w_ref, in_ref, out_w_ref, second_ref, up_ref):
        lower = me_ref[2] == 0
        for k in range(3):
            w = w_ref[k, :, HALF:]
            second_ref[k * h : (k + 1) * h, :] = jnp.where(lower, w[:h], w[h:]).astype(BF16)
        member = me_ref[3] * 2 + me_ref[2]
        w = out_w_ref[pl.ds(pl.multiple_of(member * q, q), q), :].astype(BF16)
        second_ref[3 * h : 3 * h + q, :] = w[:, :HALF]
        second_ref[3 * h + q :, :] = w[:, HALF:]
        half = FF // 2
        for k in range(4):
            up_ref[k * r : (k + 1) * r, :] = jnp.where(
                lower,
                in_ref[:, k * HALF : (k + 1) * HALF],
                in_ref[:, half + k * HALF : half + (k + 1) * HALF],
            ).astype(BF16)
        w = w_ref[3]
        up_ref[4 * r :, :] = jnp.where(lower, w[:, :HALF], w[:, HALF:]).astype(BF16)

    shapes = (3 * h + 2 * q, HALF), (5 * r, HALF)
    return call(
        kernel,
        me,
        (1,),
        [
            (attn_w, *whole((4, r, D))),
            (ffn_in, *whole((r, FF))),
            (ffn_out, *whole((r2, D))),
        ],
        [(shape, BF16, *whole(shape)) for shape in shapes],
        [],
        "pack_rest",
        moved=4 * (4 * r * D + r * FF + r2 * D),
    )


def attention_forward(me, half, x, memory, left_keys, left_values, bias, masks, own, other, places):
    first = half == 0
    spans = memory.shape[0] // MEM
    step_spans = 32 if spans % 32 == 0 else 16
    groups = step_spans // GROUP
    rows = step_spans * ROWS_SPAN
    n, r = places.n, D // places.n
    h = r // 2

    def kernel(me_ref, x_ref, mem_ref, lk_ref, lv_ref, bias_ref, mask_ref, own_ref, other_ref, *rest):
        qkv_ref, kvm_ref, att_ref, p_ref, w_ref, *rest = rest
        if first:
            hid_ref, xhat_ref, memt_ref, norm_ref, *rest = rest
        ks, vs = rest

        @pl.when(pl.program_id(0) == 0)
        def _():
            ks[...] = jnp.zeros_like(ks)
            vs[...] = jnp.zeros_like(vs)
            lower = me_ref[2] == 0
            if first:
                norm_ref[...] = jnp.zeros_like(norm_ref)
            for f in range(n):
                slot = places.slot_from(me_ref, f)
                mine, sib = own_ref[slot], other_ref[slot]
                for at, part in (
                    (slice(f * r, f * r + h), jnp.where(lower, mine, sib)),
                    (slice(f * r + h, (f + 1) * r), jnp.where(lower, sib, mine)),
                ):
                    for k in range(3):
                        w_ref[at, k * HALF : (k + 1) * HALF] = part[k * h : (k + 1) * h]
                if first:
                    tail = mine[3 * h :, :].astype(F32)
                    norm_ref[:, f * r : (f + 1) * r] = tail[0:8, 0:r]

        w = w_ref[...]
        if first:
            xhat, _ = normalize(x_ref[...].astype(F32))
            xhat_ref[...] = xhat.astype(BF16).T
            memt_ref[...] = mem_ref[...].T
            hidden = (xhat * norm_ref[0:1, :] + norm_ref[1:2, :]).astype(BF16)
            hid_ref[...] = hidden
        else:
            hidden = x_ref[...]
        qkv = dot(hidden, w).astype(BF16)
        query = qkv[:, :HALF] * jnp.asarray(0.125, BF16)
        qkv_ref[:, :HALF] = query
        qkv_ref[:, HALF:] = qkv[:, HALF:]
        kvm = dot(mem_ref[...], w[:, HALF:]).astype(BF16)
        kvm_ref[...] = kvm
        for g in range(groups):
            ls = left_start(g)
            for dest, low, src in ((ks, 0, lk_ref), (vs, HALF, lv_ref)):
                dest[g, 0:MROWS, :] = kvm[MROWS * g : MROWS * (g + 1), low : low + HALF]
                dest[g, MROWS : MROWS + QROWS, :] = qkv[
                    QROWS * g : QROWS * (g + 1), HALF + low : 2 * HALF + low
                ]
                dest[g, MROWS + QROWS : MROWS + QROWS + LWIN, :] = src[ls : ls + LWIN, :]
        for g0 in range(0, groups, 4):
            work = {}
            units = [(g, p) for g in range(g0, g0 + 4) for p in range(2)]
            for g, p in units:
                s = slice(p * PAIR, (p + 1) * PAIR)
                work[g, p] = dot_last(spread_pair(query[QROWS * g : QROWS * (g + 1), s]), ks[g, :, s])
            for g, p in units:
                scores = work[g, p] + (mask_ref[g % 2] + bias_ref[g])
                work[g, p] = jnp.exp(scores - jnp.max(scores, axis=1, keepdims=True))
            for g, p in units:
                s = slice(p * PAIR, (p + 1) * PAIR)
                e = work[g, p]
                right = jnp.concatenate([vs[g, :, s], jnp.ones((KPAD, PAIR), BF16)], axis=1)
                work[g, p] = e, dot(e.astype(BF16), right)
            for g, p in units:
                s = slice(p * PAIR, (p + 1) * PAIR)
                e, mixed = work[g, p]
                scale = 1.0 / mixed[:, PAIR:]
                at = slice(2 * QROWS * g, 2 * QROWS * (g + 1))
                p_ref[p, at, :PAIR] = (e[:, :PAIR] * scale).astype(BF16)
                p_ref[p, at, PAIR:] = (e[:, PAIR:] * scale).astype(BF16)
                att_ref[QROWS * g : QROWS * (g + 1), s] = join_pair(mixed[:, :PAIR] * scale).astype(BF16)

    count = x.shape[0]
    wide = 3 * HALF
    ins = [
        (x, *rows_of((rows, D))),
        (memory, *rows_of((step_spans * MEM, D))),
        (left_keys, *rows_of((step_spans * LEFT, HALF), half)),
        (left_values, *rows_of((step_spans * LEFT, HALF), half)),
        (bias, (groups, 1, KPAD), lambda i: (i, 0, 0)),
        (masks, *whole((2, 2 * QROWS, KPAD))),
        (own, *whole(own.shape)),
        (other, *whole(other.shape)),
    ]
    outs = [
        ((count, wide), BF16, *rows_of((rows, wide))),
        ((spans * MEM, 2 * HALF), BF16, *rows_of((step_spans * MEM, 2 * HALF))),
        ((count, HALF), BF16, *rows_of((rows, HALF))),
        ((2, 2 * count, KPAD), BF16, (2, 2 * rows, KPAD), lambda i: (0, i, 0)),
        ((D, wide), BF16, *whole((D, wide))),
    ]
    if first:
        columns = lambda i: (0, i)
        outs += [
            ((count, D), BF16, *rows_of((rows, D))),
            ((D, count), BF16, (D, rows), columns),
            ((D, spans * MEM), BF16, (D, step_spans * MEM), columns),
            ((8, D), F32, *whole((8, D))),
        ]
    return call(
        kernel,
        me,
        (spans // step_spans,),
        ins,
        outs,
        [pltpu.VMEM((groups, KPAD, HALF), BF16)] * 2,
        f"attention_forward_{half}",
        flops=2 * count * D * wide * 4,
        moved=2 * (count * D * 3 + spans * LEFT * D + spans * 4 * ROWS_SPAN * KPAD),
    )


def feed_forward(me, attended_halves, frames, cotangent, norm, up, down, places):
    count = frames.shape[0]
    rows = 512
    steps = count // rows
    chunk = 256
    n, r, r2 = places.n, D // places.n, FF // places.n
    X, Y, Z = places.X, places.Y, places.Z
    q, part_rows = r2 // places.dp, (r + r2) // Y

    def kernel(me_ref, a0, a1, fr_ref, cot_ref, norm_ref, *rest):
        up_refs, other_up_refs, rest = rest[:X], rest[X : 2 * X], rest[2 * X :]
        down_refs, other_down_refs, rest = rest[:Y], rest[Y : 2 * Y], rest[2 * Y :]
        out_ref, res_ref, gatt_ref, gn_ref, keep_up, send_up, keep_down, send_down, *rest = rest
        w1, w2, wo, acc1, acc2, acco = rest
        i = pl.program_id(0)
        lower = me_ref[2] == 0

        @pl.when(i == 0)
        def _():
            acc1[...] = jnp.zeros_like(acc1)
            acc2[...] = jnp.zeros_like(acc2)
            acco[...] = jnp.zeros_like(acco)
            gn_ref[...] = jnp.zeros_like(gn_ref)
            for dx in range(X):
                xx = lax.rem(me_ref[1] + X - dx, X)
                for dz in range(Z):
                    zz = lax.rem(me_ref[0] + Z - dz, Z)
                    f = zz * X + xx

                    def halves(mine, sib):
                        return jnp.where(lower, mine, sib), jnp.where(lower, sib, mine)

                    low, high = halves(up_refs[dx][dz], other_up_refs[dx][dz])
                    at = pl.ds(pl.multiple_of(f * r, r), r)
                    for k in range(4):
                        w1[at, k * HALF : (k + 1) * HALF] = low[k * r : (k + 1) * r]
                        w1[at, FF // 2 + k * HALF : FF // 2 + (k + 1) * HALF] = high[k * r : (k + 1) * r]
                    wo[at, :HALF] = low[4 * r :]
                    wo[at, HALF:] = high[4 * r :]
                    for dy in range(Y):
                        yy = lax.rem(me_ref[3] + Y - dy, Y)
                        for core, part in enumerate(
                            halves(down_refs[dy][dx, dz], other_down_refs[dy][dx, dz])
                        ):
                            at = pl.ds(pl.multiple_of(f * r2 + (yy * 2 + core) * q, q), q)
                            w2[at, :HALF] = part[:q]
                            w2[at, HALF:] = part[q:]

        attended = jnp.concatenate([a0[...], a1[...]], axis=1)
        residual = fr_ref[...].astype(F32) + dot(attended, wo[...])
        normed, scale = normalize(residual)
        gain = norm_ref[2:3, :]
        hidden = (normed * gain + norm_ref[3:4, :]).astype(BF16)
        cot = cot_ref[...]
        output = residual
        grad = None
        slices = [slice(j * chunk, (j + 1) * chunk) for j in range(FF // chunk)]
        late = None
        for j, s in enumerate(slices):
            inner, grad_act = dot(hidden, w1[:, s]), dot_last(cot, w2[s, :])
            if late is not None:
                u, active, grad_inner = late
                output = output + dot(active, w2[u, :])
                part = dot_last(grad_inner, w1[:, u])
                grad = part if grad is None else grad + part
                acc1[:, u] += dot_rows(hidden, grad_inner)
                acc2[:, u] += dot_rows(cot, active)
            value, slope = gelu_parts(inner)
            late = s, value.astype(BF16), (grad_act * slope).astype(BF16)
        u, active, grad_inner = late
        output = output + dot(active, w2[u, :])
        grad = grad + dot_last(grad_inner, w1[:, u])
        acc1[:, u] += dot_rows(hidden, grad_inner)
        acc2[:, u] += dot_rows(cot, active)
        out_ref[...] = output.astype(BF16)
        gn_ref[0:1, :] += jnp.sum(grad * normed, axis=0, keepdims=True)
        gn_ref[1:2, :] += jnp.sum(grad, axis=0, keepdims=True)
        grad_residual = cot.astype(F32) + norm_back(grad, normed, scale, gain)
        res_ref[...] = grad_residual
        grad_low = grad_residual.astype(BF16)
        gatt_ref[...] = dot_last(grad_low, wo[...]).astype(BF16)
        acco[...] += dot_rows(attended, grad_low)

        @pl.when(i == steps - 1)
        def _():
            for f in range(n):
                slot = places.slot_to(me_ref, f)

                def sides(low, high):
                    low, high = low.astype(BF16), high.astype(BF16)
                    return jnp.where(lower, low, high), jnp.where(lower, high, low)

                here = slice(f * r, (f + 1) * r)
                for k in range(4):
                    at = slice(k * r, (k + 1) * r)
                    keep_up[slot, at, :], send_up[slot, at, :] = sides(
                        acc1[here, k * HALF : (k + 1) * HALF],
                        acc1[here, FF // 2 + k * HALF : FF // 2 + (k + 1) * HALF],
                    )
                turned = acc2[:, f * r2 : (f + 1) * r2].T
                low = jnp.concatenate([acco[here, :HALF], turned[:, :HALF]], axis=0)
                high = jnp.concatenate([acco[here, HALF:], turned[:, HALF:]], axis=0)
                for y in range(Y):
                    at = slice(y * part_rows, (y + 1) * part_rows)
                    to = places.y_slot_to(me_ref, y)
                    keep_down[to, slot], send_down[to, slot] = sides(low[at], high[at])

    wires = [(n, 4 * r, HALF)] * 2 + [(Y, n, part_rows, HALF)] * 2
    return call(
        kernel,
        me,
        (steps,),
        [(a, *rows_of((rows, HALF))) for a in attended_halves]
        + [
            (frames, *rows_of((rows, D))),
            (cotangent, *rows_of((rows, D))),
            (norm, *whole((8, D))),
        ]
        + [(a, *whole(a.shape)) for a in (*up[0], *up[1], *down[0], *down[1])],
        [
            ((count, D), BF16, *rows_of((rows, D))),
            ((count, D), F32, *rows_of((rows, D))),
            ((count, D), BF16, *rows_of((rows, D))),
            ((8, D), F32, *whole((8, D))),
        ]
        + [(wire, BF16, *whole(wire)) for wire in wires],
        [
            pltpu.VMEM((D, FF), BF16),
            pltpu.VMEM((FF, D), BF16),
            pltpu.VMEM((D, D), BF16),
            pltpu.VMEM((D, FF), F32),
            pltpu.VMEM((D, FF), F32),
            pltpu.VMEM((D, D), F32),
        ],
        "feed_forward",
        flops=2 * count * D * (6 * FF + 3 * D) * 2,
        moved=2 * count * D * 8,
    )


def attention_backward(me, half, xhat, memory_t, left_keys, left_values, saved, grad_att, norm, norm_parts, places):
    last = norm_parts is not None
    qkv, kvm, probs, weights, attended = saved
    spans = memory_t.shape[1] // MEM
    step_spans = 32 if spans % 32 == 0 else 16
    steps = spans // step_spans
    groups = step_spans // GROUP
    rows = step_spans * ROWS_SPAN
    n, r = places.n, D // places.n
    h = r // 2
    m = 3 * h + (NORM_ROWS if last else 0)
    wide = 3 * HALF
    parts = norm_parts if last else []

    def kernel(me_ref, xhat_ref, mem_ref, lk_ref, lv_ref, qkv_ref, kvm_ref, p_ref, da_ref, att_ref, w_ref, norm_ref, *rest):
        part_refs = rest[: len(parts)]
        d_ref, keep_ref, send_ref, gn_ref, ks, vs, dm, acc, accm, sums = rest[len(parts) :]
        i = pl.program_id(0)

        @pl.when(i == 0)
        def _():
            ks[...] = jnp.zeros_like(ks)
            vs[...] = jnp.zeros_like(vs)
            acc[...] = jnp.zeros_like(acc)
            accm[...] = jnp.zeros_like(accm)
            sums[...] = jnp.zeros_like(sums)

        for g in range(groups):
            ls = left_start(g)
            for dest, low, src in ((ks, 0, lk_ref), (vs, HALF, lv_ref)):
                dest[g, 0:MROWS, :] = kvm_ref[MROWS * g : MROWS * (g + 1), low : low + HALF]
                dest[g, MROWS : MROWS + QROWS, :] = qkv_ref[
                    QROWS * g : QROWS * (g + 1), HALF + low : 2 * HALF + low
                ]
                dest[g, MROWS + QROWS : MROWS + QROWS + LWIN, :] = src[ls : ls + LWIN, :]
        negative = jnp.full((KPAD, PAIR), -1.0, BF16)
        for g0 in range(0, groups, 4):
            work = {}
            units = [(g, k) for g in range(g0, g0 + 4) for k in range(2)]
            for g, k in units:
                here = slice(QROWS * g, QROWS * (g + 1))
                s = slice(k * PAIR, (k + 1) * PAIR)
                grad = da_ref[here, s]
                product = (grad.astype(F32) * att_ref[here, s].astype(F32)).astype(BF16)
                da = spread_pair(grad)
                left = jnp.concatenate([da, spread_pair(product)], axis=1)
                right = jnp.concatenate([vs[g, :, s], negative], axis=1)
                work[g, k] = da, dot_last(left, right)
            for g, k in units:
                da, centred = work[g, k]
                p = p_ref[k, 2 * QROWS * g : 2 * QROWS * (g + 1), :]
                work[g, k] = da, p, (p.astype(F32) * centred).astype(BF16)
            for g, k in units:
                here = slice(QROWS * g, QROWS * (g + 1))
                s = slice(k * PAIR, (k + 1) * PAIR)
                d_ref[here, s] = (join_pair(dot(work[g, k][2], ks[g, :, s])) * 0.125).astype(BF16)
            for g, k in units:
                here = slice(QROWS * g, QROWS * (g + 1))
                there = slice(MROWS * g, MROWS * (g + 1))
                s = slice(k * PAIR, (k + 1) * PAIR)
                at = k * PAIR
                da, p, ds = work[g, k]
                q = spread_pair(qkv_ref[here, s])
                dk = dot_rows(ds[:, :PAIR], q).astype(BF16)
                dv = dot_rows(p[:, :PAIR], da).astype(BF16)
                d_ref[here, HALF + at : HALF + at + PAIR] = dk[MROWS : MROWS + QROWS]
                d_ref[here, 2 * HALF + at : 2 * HALF + at + PAIR] = dv[MROWS : MROWS + QROWS]
                dm[there, at : at + PAIR] = dk[:MROWS]
                dm[there, HALF + at : HALF + at + PAIR] = dv[:MROWS]
        d = d_ref[...]
        acc[...] += dot(xhat_ref[...], d)
        accm[...] += dot(mem_ref[...], dm[...])
        sums[0:1, :] += jnp.sum(d.astype(F32), axis=0, keepdims=True)

        @pl.when(i == steps - 1)
        def _():
            lower = me_ref[2] == 0
            w = w_ref[...].astype(F32)
            total = acc[...]
            row_sum = sums[0:1, :]
            lane = lax.broadcasted_iota(jnp.int32, (D, PAIR), 1)
            gain_grad = jnp.sum(total * w, axis=1, keepdims=True)
            shift_grad = jnp.sum(row_sum * w, axis=1, keepdims=True)
            turned = jnp.where(lane == 0, gain_grad, jnp.where(lane == 1, shift_grad, 0.0)).T[0:8, :]
            gn_ref[...] = turned
            line = lax.broadcasted_iota(jnp.int32, (PAIR, D), 0)
            columns = jnp.where(line == 0, norm_ref[0:1, :], jnp.where(line == 1, norm_ref[1:2, :], 0.0)).T
            grads = total * columns[:, 0:1] + columns[:, 1:2] * row_sum
            gq = grads[:, :HALF]
            gk = grads[:, HALF : 2 * HALF] + accm[:, :HALF]
            gv = grads[:, 2 * HALF :] + accm[:, HALF:]
            if last:
                first_norm = turned
                for ref in part_refs[1:]:
                    first_norm = first_norm + ref[...]
                norm_grad = jnp.concatenate([first_norm[0:2], part_refs[0][0:2, :], jnp.zeros((12, D), F32)], axis=0)
                gn_ref[...] = norm_grad[0:8]
            for f in range(n):
                slot = places.slot_to(me_ref, f)
                for k, grad in enumerate((gq, gk, gv)):
                    low = grad[f * r : f * r + h].astype(BF16)
                    high = grad[f * r + h : (f + 1) * r].astype(BF16)
                    keep_ref[slot, k * h : (k + 1) * h, :] = jnp.where(lower, low, high)
                    send_ref[slot, k * h : (k + 1) * h, :] = jnp.where(lower, high, low)
                if last:
                    piece = norm_grad[:, f * r : (f + 1) * r].astype(BF16)
                    for ref in (keep_ref, send_ref):
                        ref[slot, 3 * h :, :] = jnp.zeros((NORM_ROWS, HALF), BF16)
                        ref[slot, 3 * h :, 0:r] = piece

    count = xhat.shape[1]
    wire = (n, m, HALF)
    return call(
        kernel,
        me,
        (steps,),
        [
            (xhat, (D, rows), lambda i: (0, i)),
            (memory_t, (D, step_spans * MEM), lambda i: (0, i)),
            (left_keys, *rows_of((step_spans * LEFT, HALF), half)),
            (left_values, *rows_of((step_spans * LEFT, HALF), half)),
            (qkv, *rows_of((rows, wide))),
            (kvm, *rows_of((step_spans * MEM, 2 * HALF))),
            (probs, (2, 2 * rows, KPAD), lambda i: (0, i, 0)),
            (grad_att, *rows_of((rows, HALF), half)),
            (attended, *rows_of((rows, HALF))),
            (weights, *whole((D, wide))),
            (norm, *whole((8, D))),
        ]
        + [(a, *whole((8, D))) for a in parts],
        [
            ((count, wide), BF16, *rows_of((rows, wide))),
            (wire, BF16, *whole(wire)),
            (wire, BF16, *whole(wire)),
            ((8, D), F32, *whole((8, D))),
        ],
        [pltpu.VMEM((groups, KPAD, HALF), BF16)] * 2
        + [
            pltpu.VMEM((step_spans * MEM, 2 * HALF), BF16),
            pltpu.VMEM((D, wide), F32),
            pltpu.VMEM((D, 2 * HALF), F32),
            pltpu.VMEM((8, wide), F32),
        ],
        f"attention_backward_{half}",
        flops=2 * count * D * wide * 8,
        moved=2 * (count * D * 5 + spans * LEFT * D + spans * 4 * ROWS_SPAN * KPAD),
    )


def frames_gradient(me, frames, grad_residual, grads, weights, norm, part, before):
    count = frames.shape[0]
    rows = 256
    steps = count // rows // 2
    start = part * steps

    def kernel(me_ref, fr_ref, res_ref, d0, d1, w0_ref, w1_ref, norm_ref, *rest):
        out_ref = rest[-1]
        grad = dot_last(d0[...], w0_ref[...]) + dot_last(d1[...], w1_ref[...])
        xhat, scale = normalize(fr_ref[...].astype(F32))
        out_ref[...] = res_ref[...] + norm_back(grad, xhat, scale, norm_ref[0:1, :])

    def block(shape):
        return shape, lambda i: (start + i, 0)

    ins = [(frames, *block((rows, D))), (grad_residual, *block((rows, D)))]
    ins += [(d, *block((rows, 3 * HALF))) for d in grads]
    ins += [(w, *whole((D, 3 * HALF))) for w in weights]
    ins += [(norm, *whole((8, D)))]
    if part:
        ins += [(before, None, None)]
    (out,) = call(
        kernel,
        me,
        (steps,),
        ins,
        [((count, D), F32, *block((rows, D)))],
        [],
        f"frames_gradient_{part}",
        flops=count * D * 3 * D,
        moved=count * D * 8,
        aliases={len(ins): 0} if part else None,
    )
    return out


def after(value, *others):
    return lax.optimization_barrier((value, *others))[0]


def add(a, b):
    return a.astype(F32) + b.astype(F32)


def update_ffn(me, up, down, ffn_in, ffn_in_m, ffn_in_v, ffn_out, ffn_out_m, ffn_out_v, places):
    r, r2 = D // places.n, FF // places.n
    half = FF // 2

    def kernel(me_ref, own_ref, other_ref, own_down, other_down, wi, mi, vi, wo, mo, vo, *outs):
        lower = me_ref[2] == 0

        def halves(mine, sib):
            return jnp.where(lower, mine, sib).astype(F32), jnp.where(lower, sib, mine).astype(F32)

        def put(refs, at, grad, w, m, v, rate):
            g_ref, f_ref, s_ref, n_ref, c_ref = refs
            first, second, new = adamw(w[:, at], grad, m[:, at], v[:, at], rate)
            g_ref[:, at] = grad
            f_ref[:, at] = first
            s_ref[:, at] = second
            n_ref[:, at] = new
            c_ref[:, at] = new.astype(BF16)

        low, high = halves(own_ref[...], other_ref[...])
        for k in range(4):
            for base, part in ((0, low), (half, high)):
                at = slice(base + k * HALF, base + (k + 1) * HALF)
                put(outs[:5], at, part[k * r : (k + 1) * r], wi, mi, vi, RATE_FFN_IN)
        low, high = halves(places.y_joined(me_ref, own_down), places.y_joined(me_ref, other_down))
        for at, part in ((slice(0, HALF), low), (slice(HALF, D), high)):
            put(outs[5:], at, part[r:], wo, mo, vo, RATE_FFN_OUT)

    si, so = (r, FF), (r2, D)
    return call(
        kernel,
        me,
        (1,),
        [(a, *whole(a.shape)) for a in (*up, *down, ffn_in, ffn_in_m, ffn_in_v, ffn_out, ffn_out_m, ffn_out_v)],
        [(s, t, *whole(s)) for s in (si, so) for t in (F32, F32, F32, F32, BF16)],
        [],
        "update_ffn",
        moved=4 * 8 * (r * FF + r2 * D),
    )


def update_attention(me, rest, sums, attn_w, attn_m, attn_v, norm_params, norm_m, norm_v, places):
    r, r2 = D // places.n, FF // places.n
    h = r // 2
    sums = [*rest, *sums]

    def kernel(me_ref, *refs):
        sum_refs = refs[: len(sums)]
        w, m, v, nw, nm, nv = refs[len(sums) : len(sums) + 6]
        outs = refs[len(sums) + 6 : len(sums) + 11]
        norm_outs = refs[len(sums) + 11 :]
        lower = me_ref[2] == 0

        def put(k, at, columns, grad):
            rate = RATES_ATTENTION[k]
            first, second, new = adamw(w[k, at, columns], grad, m[k, at, columns], v[k, at, columns], rate)
            for ref, value in zip(outs, (grad, first, second, new, new.astype(BF16))):
                ref[k, at, columns] = value

        def halves(mine, sib):
            return jnp.where(lower, mine, sib).astype(F32), jnp.where(lower, sib, mine).astype(F32)

        low, high = halves(*[places.y_joined(me_ref, ref)[:r] for ref in sum_refs[:2]])
        put(3, slice(0, r), slice(0, HALF), low)
        put(3, slice(0, r), slice(HALF, D), high)
        for p in range(2):
            columns = slice(p * HALF, (p + 1) * HALF)
            for k in range(3):
                at = p * 3 * h + k * h
                low, high = halves(*[ref[at : at + h, :] for ref in sum_refs[2:]])
                put(k, slice(0, h), columns, low)
                put(k, slice(h, r), columns, high)
        grad = sum_refs[2][6 * h :, :].astype(F32)[0:4, 0:r]
        first, second, new = adamw(nw[...], grad, nm[...], nv[...], RATE_NORM)
        for ref, value in zip(norm_outs, (grad, first, second, new, new.astype(BF16))):
            ref[...] = value

    shape, small = (4, r, D), (4, r)
    ins = (*sums, attn_w, attn_m, attn_v, norm_params, norm_m, norm_v)
    return call(
        kernel,
        me,
        (1,),
        [(a, *whole(a.shape)) for a in ins],
        [(s, t, *whole(s)) for s in (shape, small) for t in (F32, F32, F32, F32, BF16)],
        [],
        "update_attention",
        moved=4 * 8 * 4 * r * D,
    )


def shards(
    places,
    frames,
    memory,
    left_keys,
    left_values,
    lengths,
    cotangent,
    attn_w,
    ffn_in,
    ffn_out,
    norm_params,
    attn_m,
    attn_v,
    ffn_in_m,
    ffn_in_v,
    ffn_out_m,
    ffn_out_v,
    norm_m,
    norm_v,
):
    X, Z = places.X, places.Z
    tie = lax.optimization_barrier
    me = places.me()
    bias = length_bias(lengths)
    masks = jnp.asarray(span_masks())

    def direct(value):
        return [
            value if dx == dz == 0 else places.shift(value, dz, dx)
            for dx in range(X)
            for dz in range(Z)
        ]

    def along_z(value):
        return [value if dz == 0 else places.shift(value, dz, 0) for dz in range(Z)]

    def along_x(value):
        return [value if dx == 0 else places.shift(value, 0, dx) for dx in range(X)]

    def split(total):
        return total.reshape((X, Z) + total.shape[1:])

    def send_x(total):
        return [places.shift(total[dx].astype(BF16), 0, dx) for dx in range(1, X)]

    def send_z(column):
        return [places.shift(column[dz].astype(BF16), dz, 0) for dz in range(1, Z)]

    def collect(mine, got):
        for part in got:
            mine = add(mine, part)
        return mine

    first_wire = pack_first(me, attn_w, norm_params, places)
    mixed, up_wire = pack_rest(me, attn_w, ffn_in, ffn_out, places)
    first = direct(first_wire)
    mixed = jnp.stack(along_z(mixed))
    up_wire, first = tie((up_wire, first))
    first = jnp.stack(first)
    mixed = along_x(mixed)
    up = along_z(up_wire)
    me, first = tie((me, first))

    def forward(token, half, x, own, other):
        return attention_forward(
            token, half, x, memory, left_keys, left_values, bias, masks, own, other, places
        )

    qkv0, kvm0, att0, p0, w_low, hidden, xhat, memory_t, norm = forward(
        me, 0, frames, first, places.other_core(first)
    )
    me, att0, mixed, up = tie((me, att0, mixed, up))
    h3 = 3 * (D // places.n) // 2
    second = jnp.concatenate([part[:, :h3] for part in mixed], axis=0)
    down = jnp.stack([part[:, h3:] for part in mixed])
    down = [down if dy == 0 else places.shift_y(down, dy) for dy in range(places.Y)]
    up = along_x(jnp.stack(up))
    qkv1, kvm1, att1, p1, w_high = forward(me, 1, hidden, second, places.other_core(second))
    me, att1, up, down = tie((me, att1, up, down))
    up = up, [places.other_core(part) for part in up]
    down = down, [places.other_core(part) for part in down]
    output, grad_residual, grad_att, norm_two, keep_up, send_up, keep_down, send_down = feed_forward(
        me, (att0, att1), frames, cotangent, norm, up, down, places
    )

    def backward(token, half, saved, norm_parts=None):
        return attention_backward(
            token, half, xhat, memory_t, left_keys, left_values, saved, grad_att, norm, norm_parts, places
        )

    def send_y(total):
        return [places.shift_y(total[dy].astype(BF16), dy) for dy in range(1, places.Y)]

    up = split(add(keep_up, places.other_core(send_up)))
    down = add(keep_down, places.other_core(send_down))
    got_up, got_down = send_x(up), send_y(down)
    me, up, down = tie((me, up, down))
    d0, keep0, send0, n0 = backward(me, 0, (qkv0, kvm0, p0, w_low, att0))
    me, d0, got_up, got_down = tie((me, d0, got_up, got_down))
    up, down = collect(up[0], got_up), split(collect(down[0], got_down))
    got_up, got_down = send_z(up), send_x(down)
    got0 = places.other_core(send0)
    d1, keep1, send1, n1 = backward(me, 1, (qkv1, kvm1, p1, w_high, att1), [norm_two, n0])
    me, d1, got0, got_up, got_down = tie((me, d1, got0, got_up, got_down))
    got1 = places.other_core(send1)
    up, down = collect(up[0], got_up).astype(BF16), collect(down[0], got_down)
    attn = split(jnp.concatenate([add(keep0, got0), add(keep1, got1)], axis=1))
    got = send_x(attn)
    got_down = send_z(down)
    up = places.sum_over_y(up)
    frames_part = functools.partial(
        frames_gradient, frames=frames, grad_residual=grad_residual, grads=(d0, d1),
        weights=(w_low, w_high), norm=norm,
    )
    me, attn = tie((me, attn))
    input_grad = frames_part(me, part=0, before=None)
    me, input_grad, up, got, got_down = tie((me, input_grad, up, got, got_down))
    attn = collect(attn[0], got)
    got = send_z(attn)
    up = up, places.other_core(up)
    down = collect(down[0], got_down).astype(BF16)
    down = jnp.stack([down if dy == 0 else places.shift_y(down, dy) for dy in range(places.Y)])
    input_grad = frames_part(me, part=1, before=input_grad)
    me, input_grad, up, down, got = tie((me, input_grad, up, down, got))
    down = down, places.other_core(down)
    attn = places.sum_over_y(collect(attn[0], got).astype(BF16))
    ffn = update_ffn(me, up, down, ffn_in, ffn_in_m, ffn_in_v, ffn_out, ffn_out_m, ffn_out_v, places)
    attn = attn, places.other_core(attn)
    attention = update_attention(
        me, down, attn, attn_w, attn_m, attn_v, norm_params, norm_m, norm_v, places
    )
    return (output, input_grad, *attention[:5], *ffn, *attention[5:])


def solution(mesh):
    rows = P(("dp", "fsdp"), None)
    attn, ffn, norm = P(None, "fsdp", None), P("fsdp", None), P(None, "fsdp")
    return jax.shard_map(
        functools.partial(shards, Places(mesh)),
        mesh=mesh,
        in_specs=(rows,) * 4
        + (P(("dp", "fsdp")), rows, attn, ffn, ffn, norm)
        + (attn, attn, ffn, ffn, ffn, ffn, norm, norm),
        out_specs=(rows, rows) + (attn,) * 5 + (ffn,) * 10 + (norm,) * 5,
        check_vma=False,
    )
```

profile of v0, /device:TPU:0, one launch (start us, length us, event | category | flops | bytes accessed | tf_op | source)
XLA Modules:
  0.0 225.3 jit_solution(17186557673548877937)
XLA Ops:
  3.6 3.0 %collective-permute-start = (bf16[112,256]{1,0:T(8,128)(2,1)}, bf16[112,256]{1,0:T(8,128)(2,1)S(1)}, u32[]{:S(2)}, u32[]{:S(2)}) collective-permute-start(bf16[112,256]{1,0:T(8,128)(2,1)} %pack_first.1), channel_id=1, source_target_pairs={{0,2},{1,3},{2,4},{3,5},{4,6},{5,7},{6,0},{7,1},{8,10},{9,11},{10,... | collective-permute-start | bytes 172040 | tf_op jit(solution)/shard_map/ppermute | solution.py:164
  6.6 2.6 %collective-permute-start.1 = (bf16[112,256]{1,0:T(8,128)(2,1)}, bf16[112,256]{1,0:T(8,128)(2,1)S(1)}, u32[]{:S(2)}, u32[]{:S(2)}) collective-permute-start(bf16[112,256]{1,0:T(8,128)(2,1)} %pack_first.1), channel_id=1, source_target_pairs={{0,4},{1,5},{2,6},{3,7},{4,0},{5,1},{6,2},{7,3},{8,12},{9,13},{10,... | collective-permute-start | bytes 172040 | tf_op jit(solution)/shard_map/ppermute | solution.py:164
  14.0 3.0 %collective-permute-start.6 = (bf16[112,256]{1,0:T(8,128)(2,1)}, bf16[112,256]{1,0:T(8,128)(2,1)S(1)}, u32[]{:S(2)}, u32[]{:S(2)}) collective-permute-start(bf16[112,256]{1,0:T(8,128)(2,1)} %pack_first.1), channel_id=1, source_target_pairs={{0,7},{1,6},{2,1},{3,0},{4,3},{5,2},{6,5},{7,4},{8,15},{9,14},{10,... | collective-permute-start | bytes 172040 | tf_op jit(solution)/shard_map/ppermute | solution.py:164
  17.7 2.7 %pack_rest.1 = (bf16[224,256]{1,0:T(8,128)(2,1)}, bf16[320,256]{1,0:T(8,128)(2,1)}) custom-call(s32[4]{0:T(128)} %pad_add_fusion.me_ref, f32[4,64,512]{2,1,0:T(8,128)} %refs_4_.1, f32[64,2048]{1,0:T(8,128)} %wi.1, f32[256,512]{1,0:T(8,128)} %wo.1), custom_call_target="tpu_custom_call" | custom-call | bytes 1572864 | tf_op jit(solution)/shard_map/pack_rest/pallas_call | solution.py:195
  22.3 2.9 %collective-permute-start.10 = (bf16[224,256]{1,0:T(8,128)(2,1)}, bf16[224,256]{1,0:T(8,128)(2,1)S(1)}, u32[]{:S(2)}, u32[]{:S(2)}) collective-permute-start(bf16[224,256]{1,0:T(8,128)(2,1)} %get-tuple-element.141), channel_id=1, source_target_pairs={{0,6},{1,7},{2,0},{3,1},{4,2},{5,3},{6,4},{7,5},{8,14},{9,15},{10,... | collective-permute-start | bytes 344072 | tf_op jit(solution)/shard_map/ppermute | solution.py:164
  28.2 3.3 %collective-permute-start.13 = (bf16[320,256]{1,0:T(8,128)(2,1)}, bf16[320,256]{1,0:T(8,128)(2,1)S(1)}, u32[]{:S(2)}, u32[]{:S(2)}) collective-permute-start(bf16[320,256]{1,0:T(8,128)(2,1)} %get-tuple-element.148), channel_id=1, source_target_pairs={{0,4},{1,5},{2,6},{3,7},{4,0},{5,1},{6,2},{7,3},{8,12},{9,13},{10,... | collective-permute-start | bytes 491528 | tf_op jit(solution)/shard_map/ppermute | solution.py:164
  31.6 3.1 %collective-permute-start.14 = (bf16[320,256]{1,0:T(8,128)(2,1)}, bf16[320,256]{1,0:T(8,128)(2,1)S(1)}, u32[]{:S(2)}, u32[]{:S(2)}) collective-permute-start(bf16[320,256]{1,0:T(8,128)(2,1)} %get-tuple-element.148), channel_id=1, source_target_pairs={{0,6},{1,7},{2,0},{3,1},{4,2},{5,3},{6,4},{7,5},{8,14},{9,15},{10,... | collective-permute-start | bytes 491528 | tf_op jit(solution)/shard_map/ppermute | solution.py:164
  38.5 14.7 %attention_forward_0.1 = (bf16[2560,768]{1,0:T(8,128)(2,1)}, bf16[512,512]{1,0:T(8,128)(2,1)}, bf16[2560,256]{1,0:T(8,128)(2,1)}, bf16[2,5120,256]{2,1,0:T(8,128...) custom-call(s32[4]{0:T(128)} %pad_add_fusion.me_ref, ...), custom_call_target="tpu_custom_call" | custom-call | flops 8053063680 | bytes 17039360 | tf_op jit(solution)/shard_map/attention_forward_0/pallas_call | solution.py:195
  56.1 12.0 %attention_forward_1.1 = (bf16[2560,768]{1,0:T(8,128)(2,1)}, bf16[512,512]{1,0:T(8,128)(2,1)}, bf16[2560,256]{1,0:T(8,128)(2,1)}, bf16[2,5120,256]{2,1,0:T(8,128)(2,1)}, bf16[512,768]{1,0:T(8,128)(2,1)}) custom-call(s32[4]{0:T(128)} %pad_add_fusion.me_ref, bf16[2560,512]{1,0:T(8,128)(2,1)} %get-tuple-element.144.x_ref, bf16[512,512]{1,0:T(8,128)(2,1)} %mem_ref.3, ...), custom_call_target="tpu_custom_call" | custom-call | flops 8053063680 | bytes 17039360 | tf_op jit(solution)/shard_map/attention_forward_1/pallas_call | solution.py:195
  68.2 3.9 %collective-permute-done.16.rest_1_ = bf16[4,320,256]{2,1,0:T(8,128)(2,1)S(1)} collective-permute-done((bf16[4,320,256]{2,1,0:T(8,128)(2,1)S(1)}, bf16[4,320,256]{2,1,0:T(8,128)(2,1)S(1)}, u32[]{:S(2)}, u32[]{:S(2)}) %collective-permute-start.16) | collective-permute-done | bytes 655392 | tf_op jit(solution)/shard_map/ppermute | solution.py:164
  73.1 2.8 %collective-permute-done.20.rest_6_ = bf16[2,4,128,256]{3,2,1,0:T(8,128)(2,1)S(1)} collective-permute-done((bf16[2,4,128,256]{3,2,1,0:T(8,128)(2,1)S(1)}, bf16[2,4,128,256]{3,2,1,0:T(8,128)(2,1)S(1)}, u32[]{:S(2)}, u32[]{:S(2)}) %collective-permute-start.20) | collective-permute-done | bytes 524320 | tf_op jit(solution)/shard_map/ppermute | solution.py:178
  77.9 50.8 %feed_forward.1 = (bf16[2560,512]{1,0:T(8,128)(2,1)}, f32[2560,512]{1,0:T(8,128)}, bf16[2560,512]{1,0:T(8,128)(2,1)}, f32[8,512]{1,0:T(8,128)}, bf16[8,256,256]{...) custom-call(s32[4]{0:T(128)} %pad_add_fusion.me_ref, ...), custom_call_target="tpu_custom_call" | custom-call | flops 72477573120 | bytes 20971520 | tf_op jit(solution)/shard_map/feed_forward/pallas_call | solution.py:195
  129.3 2.4 %collective-permute-done.22 = bf16[8,256,256]{2,1,0:T(8,128)(2,1)S(1)} collective-permute-done((bf16[8,256,256]{2,1,0:T(8,128)(2,1)}, bf16[8,256,256]{2,1,0:T(8,128)(2,1)S(1)}, u32[]{:S(2)}, u32[]{:S(2)}) %collective-permute-start.22) | collective-permute-done | bytes 1048608 | tf_op jit(solution)/shard_map/ppermute | solution.py:178
  134.6 16.7 %attention_backward_0.1 = (bf16[2560,768]{1,0:T(8,128)(2,1)}, bf16[8,96,256]{2,1,0:T(8,128)(2,1)}, bf16[8,96,256]{2,1,0:T(8,128)(2,1)}, f32[8,512]{1,0:T(8,128)}) custom-call(s32[4]{0:T(128)} %pad_add_fusion.me_ref, bf16[512,2560]{1,0:T(8,128)(2,1)} %get-tuple-element.166.xhat_ref, bf16[512,512]{1,0:T(8,128)(2,1)} %get-tuple-element.167.mem_ref, ...), custom_call_target="tpu_custom_call" | custom-call | flops 16106127360 | bytes 22282240 | tf_op jit(solution)/shard_map/attention_backward_0/pallas_call | solution.py:195
  153.5 4.2 %collective-permute-start.27 = (bf16[256,256]{1,0:T(8,128)(2,1)S(1)}, bf16[256,256]{1,0:T(8,128)(2,1)S(1)}, u32[]{:S(2)}, u32[]{:S(2)}) collective-permute-start(bf16[256,256]{1,0:T(8,128)(2,1)S(1)} %get-tuple-element.248), channel_id=1, source_target_pairs={{0,2},{1,3},{2,4},{3,5},{4,6},{5,7},{6,0},{7,1},{8,10},{9,11},{10,... | collective-permute-start | bytes 393224 | tf_op jit(solution)/shard_map/ppermute | solution.py:164
  157.7 2.4 %collective-permute-start.29 = (bf16[256,256]{1,0:T(8,128)(2,1)S(1)}, bf16[256,256]{1,0:T(8,128)(2,1)S(1)}, u32[]{:S(2)}, u32[]{:S(2)}) collective-permute-start(bf16[256,256]{1,0:T(8,128)(2,1)S(1)} %get-tuple-element.246), channel_id=1, source_target_pairs={{0,6},{1,7},{2,0},{3,1},{4,2},{5,3},{6,4},{7,5},{8,14},{9,15},{10,... | collective-permute-start | bytes 393224 | tf_op jit(solution)/shard_map/ppermute | solution.py:164
  160.2 16.5 %attention_backward_1.1 = (bf16[2560,768]{1,0:T(8,128)(2,1)}, bf16[8,112,256]{2,1,0:T(8,128)(2,1)}, bf16[8,112,256]{2,1,0:T(8,128)(2,1)}, f32[8,512]{1,0:T(8,128)}) custom-call(s32[4]{0:T(128)} %pad_add_fusion.me_ref, bf16[512,2560]{1,0:T(8,128)(2,1)} %get-tuple-element.166.xhat_ref, bf16[512,512]{1,0:T(8,128)(2,1)} %get-tuple-element.167.mem_ref, ...), custom_call_target="tpu_custom_call" | custom-call | flops 16106127360 | bytes 22282240 | tf_op jit(solution)/shard_map/attention_backward_1/pallas_call | solution.py:195
  177.0 2.5 %collective-permute-start.35 = (bf16[160,256]{1,0:T(8,128)(2,1)S(1)}, bf16[160,256]{1,0:T(8,128)(2,1)S(1)}, u32[]{:S(2)}, u32[]{:S(2)}) collective-permute-start(bf16[160,256]{1,0:T(8,128)(2,1)S(1)} %get-tuple-element.253), channel_id=1, source_target_pairs={{0,4},{1,5},{2,6},{3,7},{4,0},{5,1},{6,2},{7,3},{8,12},{9,13},{10,... | collective-permute-start | bytes 245768 | tf_op jit(solution)/shard_map/ppermute | solution.py:164
  184.7 8.8 %frames_gradient_0.1.rest_0_ = f32[2560,512]{1,0:T(8,128)} custom-call(s32[4]{0:T(128)} %pad_add_fusion.me_ref, bf16[2560,512]{1,0:T(8,128)(2,1)} %fr_ref.5, f32[2560,512]{1,0:T(8,128)} %get-tuple-element.193.res_ref, bf16[2560,768]{1,0:T(8,128)(2,1)} %get-tuple-element.194.d0, bf16[2560,768]{1,0:T(8,128)(2,1)} %get-tuple-element.195.d1, ...), custom_call_target="tpu_custom_call" | custom-call | flops 2013265920 | bytes 10485760 | tf_op jit(solution)/shard_map/frames_gradient_0/pallas_call | solution.py:195
  196.2 2.8 %collective-permute-start.41 = (bf16[208,256]{1,0:T(8,128)(2,1)S(1)}, bf16[208,256]{1,0:T(8,128)(2,1)S(1)}, u32[]{:S(2)}, u32[]{:S(2)}) collective-permute-start(bf16[208,256]{1,0:T(8,128)(2,1)S(1)} %get-tuple-element.249), channel_id=1, source_target_pairs={{0,6},{1,7},{2,0},{3,1},{4,2},{5,3},{6,4},{7,5},{8,14},{9,15},{10,... | collective-permute-start | bytes 319496 | tf_op jit(solution)/shard_map/ppermute | solution.py:164
  199.7 9.1 %frames_gradient_1.1 = f32[2560,512]{1,0:T(8,128)} custom-call(s32[4]{0:T(128)} %pad_add_fusion.me_ref, bf16[2560,512]{1,0:T(8,128)(2,1)} %fr_ref.5, f32[2560,512]{1,0:T(8,128)} %get-tuple-element.193.res_ref, bf16[2560,768]{1,0:T(8,128)(2,1)} %get-tuple-element.194.d0, bf16[2560,768]{1,0:T(8,128)(2,1)} %get-tuple-element.195.d1, ...), custom_call_target="tpu_custom_call", output_to_operand_aliasing={{}: (8, {})} | custom-call | flops 2013265920 | bytes 10485760 | tf_op jit(solution)/shard_map/frames_gradient_1/pallas_call | solution.py:195
  210.7 3.6 %collective-permute-done.43 = bf16[208,256]{1,0:T(8,128)(2,1)S(1)} collective-permute-done((bf16[208,256]{1,0:T(8,128)(2,1)S(1)}, bf16[208,256]{1,0:T(8,128)(2,1)S(1)}, u32[]{:S(2)}, u32[]{:S(2)}) %collective-permute-start.43) | collective-permute-done | bytes 106528 | tf_op jit(solution)/shard_map/ppermute | solution.py:183
  215.2 5.2 %update_ffn.1 = (f32[64,2048]{1,0:T(8,128)}, f32[64,2048]{1,0:T(8,128)}, f32[64,2048]{1,0:T(8,128)}, f32[64,2048]{1,0:T(8,128)}, bf16[64,2048]{1,0:T(8,128)(2,1)...) custom-call(s32[4]{0:T(128)} %pad_add_fusion.me_ref, ...), custom_call_target="tpu_custom_call" | custom-call | bytes 8388608 | tf_op jit(solution)/shard_map/update_ffn/pallas_call | solution.py:195
  221.1 4.0 %update_attention.1 = (f32[4,64,512]{2,1,0:T(8,128)}, f32[4,64,512]{2,1,0:T(8,128)}, f32[4,64,512]{2,1,0:T(8,128)}, f32[4,64,512]{2,1,0:T(8,128)}, bf16[4,64,512...) custom-call(s32[4]{0:T(128)} %pad_add_fusion.me_ref, ...), custom_call_target="tpu_custom_call" | custom-call | bytes 4194304 | tf_op jit(solution)/shard_map/update_attention/pallas_call | solution.py:195
  (174 shorter events, 40.5 us)
Async XLA Ops:
  12.7 12.5 %collective-permute-start.5 = (bf16[112,256]{1,0:T(8,128)(2,1)}, bf16[112,256]{1,0:T(8,128)(2,1)S(1)}, u32[]{:S(2)}, u32[]{:S(2)}) collective-permute-start(bf16[112,256]{1,0:T(8,128)(2,1)} %pack_first.1), channel_id=1, source_target_pairs={{0,5},{1,4},{2,7},{3,6},{4,1},{5,0},{6,3},{7,2},{8,13},{9,12},{10,... | collective-permute-start | bytes 172040 | tf_op jit(solution)/shard_map/ppermute | solution.py:164
  22.3 12.3 %collective-permute-start.10 = (bf16[224,256]{1,0:T(8,128)(2,1)}, bf16[224,256]{1,0:T(8,128)(2,1)S(1)}, u32[]{:S(2)}, u32[]{:S(2)}) collective-permute-start(bf16[224,256]{1,0:T(8,128)(2,1)} %get-tuple-element.141), channel_id=1, source_target_pairs={{0,6},{1,7},{2,0},{3,1},{4,2},{5,3},{6,4},{7,5},{8,14},{9,15},{10,... | collective-permute-start | bytes 344072 | tf_op jit(solution)/shard_map/ppermute | solution.py:164
  26.1 11.6 %collective-permute-start.7 = (bf16[8,112,256]{2,1,0:T(8,128)(2,1)S(1)}, bf16[8,112,256]{2,1,0:T(8,128)(2,1)S(1)}, u32[]{:S(2)}, u32[]{:S(2)}) collective-permute-start(bf16[8,112,256]{2,1,0:T(8,128)(2,1)S(1)} %bitcast_dynamic-update-slice_fusion.own_ref), channel_id=1, source_target_pairs={{0,8},{8,0},{16,24},{24,16},{1,9},{9,1},{17,25},{25,17},{2,10},{10... | collective-permute-start | bytes 1376264 | tf_op jit(solution)/shard_map/ppermute | solution.py:178
  27.3 25.8 %collective-permute-start.12 = (bf16[320,256]{1,0:T(8,128)(2,1)}, bf16[320,256]{1,0:T(8,128)(2,1)S(1)}, u32[]{:S(2)}, u32[]{:S(2)}) collective-permute-start(bf16[320,256]{1,0:T(8,128)(2,1)} %get-tuple-element.148), channel_id=1, source_target_pairs={{0,2},{1,3},{2,4},{3,5},{4,6},{5,7},{6,0},{7,1},{8,10},{9,11},{10,... | collective-permute-start | bytes 491528 | tf_op jit(solution)/shard_map/ppermute | solution.py:164
  28.2 25.0 %collective-permute-start.13 = (bf16[320,256]{1,0:T(8,128)(2,1)}, bf16[320,256]{1,0:T(8,128)(2,1)S(1)}, u32[]{:S(2)}, u32[]{:S(2)}) collective-permute-start(bf16[320,256]{1,0:T(8,128)(2,1)} %get-tuple-element.148), channel_id=1, source_target_pairs={{0,4},{1,5},{2,6},{3,7},{4,0},{5,1},{6,2},{7,3},{8,12},{9,13},{10,... | collective-permute-start | bytes 491528 | tf_op jit(solution)/shard_map/ppermute | solution.py:164
  31.6 21.6 %collective-permute-start.14 = (bf16[320,256]{1,0:T(8,128)(2,1)}, bf16[320,256]{1,0:T(8,128)(2,1)S(1)}, u32[]{:S(2)}, u32[]{:S(2)}) collective-permute-start(bf16[320,256]{1,0:T(8,128)(2,1)} %get-tuple-element.148), channel_id=1, source_target_pairs={{0,6},{1,7},{2,0},{3,1},{4,2},{5,3},{6,4},{7,5},{8,14},{9,15},{10,... | collective-permute-start | bytes 491528 | tf_op jit(solution)/shard_map/ppermute | solution.py:164
  35.6 17.6 %collective-permute-start.11 = (bf16[4,224,256]{2,1,0:T(8,128)(2,1)S(1)}, bf16[4,224,256]{2,1,0:T(8,128)(2,1)S(1)}, u32[]{:S(2)}, u32[]{:S(2)}) collective-permute-start(bf16[4,224,256]{2,1,0:T(8,128)(2,1)S(1)} %pad_maximum_fusion.3), channel_id=1, source_target_pairs={{0,1},{1,0},{2,3},{3,2},{4,5},{5,4},{6,7},{7,6},{8,9},{9,8},{10,11... | collective-permute-start | bytes 1376264 | tf_op jit(solution)/shard_map/ppermute | solution.py:164
  53.5 14.7 %collective-permute-start.17 = (bf16[2,4,128,256]{3,2,1,0:T(8,128)(2,1)S(1)}, bf16[2,4,128,256]{3,2,1,0:T(8,128)(2,1)S(1)}, u32[]{:S(2)}, u32[]{:S(2)}) collective-permute-start(bf16[2,4,128,256]{3,2,1,0:T(8,128)(2,1)S(1)} %pad_maximum_fusion.2.rest_4_), channel_id=1, source_target_pairs={{0,16},{8,24},{16,0},{24,8},{1,17},{9,25},{17,1},{25,9},{2,18},{10... | collective-permute-start | bytes 1572872 | tf_op jit(solution)/shard_map/ppermute | solution.py:175
  55.2 16.9 %collective-permute-start.16 = (bf16[4,320,256]{2,1,0:T(8,128)(2,1)S(1)}, bf16[4,320,256]{2,1,0:T(8,128)(2,1)S(1)}, u32[]{:S(2)}, u32[]{:S(2)}) collective-permute-start(bf16[4,320,256]{2,1,0:T(8,128)(2,1)S(1)} %pad_maximum_fusion.1.rest_0_), channel_id=1, source_target_pairs={{0,1},{1,0},{2,3},{3,2},{4,5},{5,4},{6,7},{7,6},{8,9},{9,8},{10,11... | collective-permute-start | bytes 1966088 | tf_op jit(solution)/shard_map/ppermute | solution.py:164
  133.3 18.0 %collective-permute-start.24 = (bf16[4,256,256]{2,1,0:T(8,128)(2,1)S(1)}, bf16[4,256,256]{2,1,0:T(8,128)(2,1)S(1)}, u32[]{:S(2)}, u32[]{:S(2)}) collective-permute-start(bf16[4,256,256]{2,1,0:T(8,128)(2,1)S(1)} %slice.222), channel_id=1, source_target_pairs={{0,1},{1,0},{2,3},{3,2},{4,5},{5,4},{6,7},{7,6},{8,9},{9,8},{10,11... | collective-permute-start | bytes 1572872 | tf_op jit(solution)/shard_map/ppermute | solution.py:164
  134.0 17.3 %collective-permute-start.25 = (bf16[8,160,256]{2,1,0:T(8,128)(2,1)S(1)}, bf16[8,160,256]{2,1,0:T(8,128)(2,1)S(1)}, u32[]{:S(2)}, u32[]{:S(2)}) collective-permute-start(bf16[8,160,256]{2,1,0:T(8,128)(2,1)S(1)} %fusion.2), channel_id=1, source_target_pairs={{0,16},{8,24},{16,0},{24,8},{1,17},{9,25},{17,1},{25,9},{2,18},{10... | collective-permute-start | bytes 1966088 | tf_op jit(solution)/shard_map/ppermute | solution.py:175
  151.2 25.5 %collective-permute-start.26 = (bf16[8,96,256]{2,1,0:T(8,128)(2,1)}, bf16[8,96,256]{2,1,0:T(8,128)(2,1)S(1)}, u32[]{:S(2)}, u32[]{:S(2)}) collective-permute-start(bf16[8,96,256]{2,1,0:T(8,128)(2,1)} %get-tuple-element.182), channel_id=1, source_target_pairs={{0,8},{8,0},{16,24},{24,16},{1,9},{9,1},{17,25},{25,17},{2,10},{10... | collective-permute-start | bytes 1179656 | tf_op jit(solution)/shard_map/ppermute | solution.py:178
  151.5 25.3 %collective-permute-start.30 = (bf16[4,160,256]{2,1,0:T(8,128)(2,1)S(1)}, bf16[4,160,256]{2,1,0:T(8,128)(2,1)S(1)}, u32[]{:S(2)}, u32[]{:S(2)}) collective-permute-start(bf16[4,160,256]{2,1,0:T(8,128)(2,1)S(1)} %slice.223), channel_id=1, source_target_pairs={{0,1},{1,0},{2,3},{3,2},{4,5},{5,4},{6,7},{7,6},{8,9},{9,8},{10,11... | collective-permute-start | bytes 983048 | tf_op jit(solution)/shard_map/ppermute | solution.py:164
  153.5 23.3 %collective-permute-start.27 = (bf16[256,256]{1,0:T(8,128)(2,1)S(1)}, bf16[256,256]{1,0:T(8,128)(2,1)S(1)}, u32[]{:S(2)}, u32[]{:S(2)}) collective-permute-start(bf16[256,256]{1,0:T(8,128)(2,1)S(1)} %get-tuple-element.248), channel_id=1, source_target_pairs={{0,2},{1,3},{2,4},{3,5},{4,6},{5,7},{6,0},{7,1},{8,10},{9,11},{10,... | collective-permute-start | bytes 393224 | tf_op jit(solution)/shard_map/ppermute | solution.py:164
  157.7 19.1 %collective-permute-start.28 = (bf16[256,256]{1,0:T(8,128)(2,1)S(1)}, bf16[256,256]{1,0:T(8,128)(2,1)S(1)}, u32[]{:S(2)}, u32[]{:S(2)}) collective-permute-start(bf16[256,256]{1,0:T(8,128)(2,1)S(1)} %get-tuple-element.247), channel_id=1, source_target_pairs={{0,4},{1,5},{2,6},{3,7},{4,0},{5,1},{6,2},{7,3},{8,12},{9,13},{10,... | collective-permute-start | bytes 393224 | tf_op jit(solution)/shard_map/ppermute | solution.py:164
  157.7 19.1 %collective-permute-start.29 = (bf16[256,256]{1,0:T(8,128)(2,1)S(1)}, bf16[256,256]{1,0:T(8,128)(2,1)S(1)}, u32[]{:S(2)}, u32[]{:S(2)}) collective-permute-start(bf16[256,256]{1,0:T(8,128)(2,1)S(1)} %get-tuple-element.246), channel_id=1, source_target_pairs={{0,6},{1,7},{2,0},{3,1},{4,2},{5,3},{6,4},{7,5},{8,14},{9,15},{10,... | collective-permute-start | bytes 393224 | tf_op jit(solution)/shard_map/ppermute | solution.py:164
  177.0 16.6 %collective-permute-start.34 = (bf16[160,256]{1,0:T(8,128)(2,1)S(1)}, bf16[160,256]{1,0:T(8,128)(2,1)S(1)}, u32[]{:S(2)}, u32[]{:S(2)}) collective-permute-start(bf16[160,256]{1,0:T(8,128)(2,1)S(1)} %get-tuple-element.254), channel_id=1, source_target_pairs={{0,2},{1,3},{2,4},{3,5},{4,6},{5,7},{6,0},{7,1},{8,10},{9,11},{10,... | collective-permute-start | bytes 245768 | tf_op jit(solution)/shard_map/ppermute | solution.py:164
  177.0 16.5 %collective-permute-start.35 = (bf16[160,256]{1,0:T(8,128)(2,1)S(1)}, bf16[160,256]{1,0:T(8,128)(2,1)S(1)}, u32[]{:S(2)}, u32[]{:S(2)}) collective-permute-start(bf16[160,256]{1,0:T(8,128)(2,1)S(1)} %get-tuple-element.253), channel_id=1, source_target_pairs={{0,4},{1,5},{2,6},{3,7},{4,0},{5,1},{6,2},{7,3},{8,12},{9,13},{10,... | collective-permute-start | bytes 245768 | tf_op jit(solution)/shard_map/ppermute | solution.py:164
  179.5 14.0 %collective-permute-start.36 = (bf16[160,256]{1,0:T(8,128)(2,1)S(1)}, bf16[160,256]{1,0:T(8,128)(2,1)S(1)}, u32[]{:S(2)}, u32[]{:S(2)}) collective-permute-start(bf16[160,256]{1,0:T(8,128)(2,1)S(1)} %get-tuple-element.252), channel_id=1, source_target_pairs={{0,6},{1,7},{2,0},{3,1},{4,2},{5,3},{6,4},{7,5},{8,14},{9,15},{10,... | collective-permute-start | bytes 245768 | tf_op jit(solution)/shard_map/ppermute | solution.py:164
  180.9 12.6 %collective-permute-start.32 = (bf16[256,256]{1,0:T(8,128)(2,1)S(1)}, bf16[256,256]{1,0:T(8,128)(2,1)S(1)}, u32[]{:S(2)}, u32[]{:S(2)}) collective-permute-start(bf16[256,256]{1,0:T(8,128)(2,1)S(1)} %fusion.6), channel_id=1, source_target_pairs={{0,16},{8,24},{16,0},{24,8},{1,17},{9,25},{17,1},{25,9},{2,18},{10... | collective-permute-start | bytes 393224 | tf_op jit(solution)/shard_map/ppermute | solution.py:183
  182.8 11.4 %collective-permute-start.33 = (bf16[4,208,256]{2,1,0:T(8,128)(2,1)S(1)}, bf16[4,208,256]{2,1,0:T(8,128)(2,1)S(1)}, u32[]{:S(2)}, u32[]{:S(2)}) collective-permute-start(bf16[4,208,256]{2,1,0:T(8,128)(2,1)S(1)} %fusion.1), channel_id=1, source_target_pairs={{0,1},{1,0},{2,3},{3,2},{4,5},{5,4},{6,7},{7,6},{8,9},{9,8},{10,11... | collective-permute-start | bytes 1277960 | tf_op jit(solution)/shard_map/ppermute | solution.py:164
  194.3 14.4 %collective-permute-start.39 = (bf16[208,256]{1,0:T(8,128)(2,1)S(1)}, bf16[208,256]{1,0:T(8,128)(2,1)S(1)}, u32[]{:S(2)}, u32[]{:S(2)}) collective-permute-start(bf16[208,256]{1,0:T(8,128)(2,1)S(1)} %get-tuple-element.251), channel_id=1, source_target_pairs={{0,2},{1,3},{2,4},{3,5},{4,6},{5,7},{6,0},{7,1},{8,10},{9,11},{10,... | collective-permute-start | bytes 319496 | tf_op jit(solution)/shard_map/ppermute | solution.py:164
  195.0 13.8 %collective-permute-start.40 = (bf16[208,256]{1,0:T(8,128)(2,1)S(1)}, bf16[208,256]{1,0:T(8,128)(2,1)S(1)}, u32[]{:S(2)}, u32[]{:S(2)}) collective-permute-start(bf16[208,256]{1,0:T(8,128)(2,1)S(1)} %get-tuple-element.250), channel_id=1, source_target_pairs={{0,4},{1,5},{2,6},{3,7},{4,0},{5,1},{6,2},{7,3},{8,12},{9,13},{10,... | collective-permute-start | bytes 319496 | tf_op jit(solution)/shard_map/ppermute | solution.py:164
  196.2 12.6 %collective-permute-start.41 = (bf16[208,256]{1,0:T(8,128)(2,1)S(1)}, bf16[208,256]{1,0:T(8,128)(2,1)S(1)}, u32[]{:S(2)}, u32[]{:S(2)}) collective-permute-start(bf16[208,256]{1,0:T(8,128)(2,1)S(1)} %get-tuple-element.249), channel_id=1, source_target_pairs={{0,6},{1,7},{2,0},{3,1},{4,2},{5,3},{6,4},{7,5},{8,14},{9,15},{10,... | collective-permute-start | bytes 319496 | tf_op jit(solution)/shard_map/ppermute | solution.py:164
  (49 other events, 416.5 us)
where the time goes:
time: 226 us; the launch traced here: 225 us
  Pallas kernels  143 us (63%)
  starting transfers between devices  54 us (24%)
  waiting for transfers between devices  15 us (7%)
  local copies, waits for them, and re-layouts  6.36 us (3%)
  other arithmetic  5.46 us (2%)
    pallas_call x11, Pallas kernels, call(): pl.pallas_call(kernel, grid_spec=pltpu.PrefetchScalarGridSpec(num_scalar_...  143 us
    ppermute x27, starting transfers between devices, shift(): return lax.ppermute(value, 'fsdp', perm)  45.9 us
    ppermute x13, waiting for transfers between devices, other_core(): return lax.ppermute(value, 'dp', [(d, d ^ 1) for d in range(self.dp)])  5.89 us
    ppermute x27, waiting for transfers between devices, shift(): return lax.ppermute(value, 'fsdp', perm)  5.46 us
    unnamed x63, local copies, waits for them, and re-layouts  5.09 us
  transfers between devices with their start and end apart: 45, of which 7 were waited for; matrix products, arithmetic and copies ran while one was open for 3% of the time, Pallas kernels for 38%

commit v1 on v0

--- a/solution.py
+++ b/solution.py
@@ -39,7 +39,6 @@
 RATE_FFN_IN = 0.04
 RATE_FFN_OUT = 0.02
 RATE_NORM = 0.2
-VMEM_LIMIT = 56 * 2**20
 
 
 def dot(a, b):
@@ -108,18 +107,15 @@
     return masks
 
 
-def length_bias(lengths):
-    groups = lengths.shape[0] // GROUP
-    key = np.arange(KPAD)
-    is_frame = (key >= MROWS) & (key < MROWS + QROWS)
-    place = np.where(is_frame, (key - MROWS) % ROWS_SPAN, 0)
-    span = np.where(is_frame, (key - MROWS) // ROWS_SPAN, 0)
-    own = lengths.reshape(groups, GROUP)
-    length = jnp.zeros((groups, KPAD), jnp.int32)
+def dead_keys(lengths_ref, group):
+    key = lax.broadcasted_iota(jnp.int32, (1, KPAD), 1) - MROWS
+    length = jnp.full((1, KPAD), ROWS_SPAN, jnp.int32)
+    place = jnp.zeros((1, KPAD), jnp.int32)
     for s in range(GROUP):
-        length = jnp.where(jnp.asarray(span == s)[None, :], own[:, s : s + 1], length)
-    dead = jnp.asarray(is_frame & (place < SEG))[None, :] & (jnp.asarray(place)[None, :] >= length)
-    return jnp.where(dead, BLOCKED, 0.0).astype(F32).reshape(groups, 1, KPAD)
+        inside = (key >= s * ROWS_SPAN) & (key < s * ROWS_SPAN + SEG)
+        length = jnp.where(inside, lengths_ref[group * GROUP + s], length)
+        place = jnp.where(inside, key - s * ROWS_SPAN, place)
+    return jnp.where(place >= length, BLOCKED, 0.0)
 
 
 def adamw(weight, grad, first_old, second_old, rate):
@@ -186,10 +182,10 @@
         return value
 
 
-def call(kernel, me, grid, ins, outs, scratch, name, flops=0, moved=0, aliases=None):
+def call(kernel, me, grid, ins, outs, scratch, name, flops=0, moved=0, aliases=None, limit=32):
     def spec(block, index):
         if block is None:
-            return pl.BlockSpec(memory_space=pl.ANY)
+            return pl.BlockSpec(memory_space=pltpu.VMEM if index is None else pl.ANY)
         return pl.BlockSpec(block, lambda *a: index(*a[:-1]))
 
     return pl.pallas_call(
@@ -202,13 +198,17 @@
             scratch_shapes=scratch,
         ),
         out_shape=[jax.ShapeDtypeStruct(s, d) for s, d, _, _ in outs],
-        compiler_params=pltpu.CompilerParams(vmem_limit_bytes=VMEM_LIMIT),
+        compiler_params=pltpu.CompilerParams(vmem_limit_bytes=limit * 2**20),
         cost_estimate=pl.CostEstimate(flops=flops, bytes_accessed=moved, transcendentals=0),
         input_output_aliases=aliases or {},
         name=name,
     )(me, *[a for a, _, _ in ins])
 
 
+def resident(array):
+    return array, None, None
+
+
 def whole(shape):
     return shape, lambda i: (0,) * len(shape)
 
@@ -217,33 +217,13 @@
     return shape, lambda i: (i, column)
 
 
-def pack_first(me, attn_w, norm_params, places):
+def pack_first(attn_w, norm_params, places):
     r = D // places.n
     h = r // 2
-
-    def kernel(me_ref, w_ref, n_ref, out_ref, scratch):
-        lower = me_ref[2] == 0
-        for k in range(3):
-            w = w_ref[k]
-            out_ref[k * h : (k + 1) * h, :] = jnp.where(lower, w[:h], w[h:]).astype(BF16)
-        scratch[...] = jnp.zeros_like(scratch)
-        scratch[0:4, 0:r] = n_ref[...]
-        out_ref[3 * h :, :] = scratch[...].astype(BF16)
-
-    (out,) = call(
-        kernel,
-        me,
-        (1,),
-        [
-            (attn_w, (3, r, HALF), lambda i: (0, 0, 0)),
-            (norm_params, *whole((4, r))),
-        ],
-        [((3 * h + NORM_ROWS, HALF), BF16, *whole((3 * h + NORM_ROWS, HALF)))],
-        [pltpu.VMEM((NORM_ROWS, HALF), F32)],
-        "pack_first",
-        moved=4 * 3 * r * HALF,
-    )
-    return out
+    start = lax.axis_index("dp") % 2 * h
+    rows = lax.dynamic_slice(attn_w[:3, :, :HALF], (0, start, 0), (3, h, HALF)).reshape(3 * h, HALF)
+    norms = jnp.pad(norm_params, ((0, NORM_ROWS - 4), (0, HALF - r)))
+    return jnp.concatenate([rows, norms], axis=0).astype(BF16)
 
 
 def pack_rest(me, attn_w, ffn_in, ffn_out, places):
@@ -282,12 +262,14 @@
         [(shape, BF16, *whole(shape)) for shape in shapes],
         [],
         "pack_rest",
+        limit=58,
         moved=4 * (4 * r * D + r * FF + r2 * D),
     )
 
 
-def attention_forward(me, half, x, memory, left_keys, left_values, bias, masks, own, other, places):
+def attention_forward(me, half, x, memory, left_keys, left_values, masks, weights, places, part=0, parts=1, before=None):
     first = half == 0
+    fresh = before is None
     spans = memory.shape[0] // MEM
     step_spans = 32 if spans % 32 == 0 else 16
     groups = step_spans // GROUP
@@ -295,10 +277,24 @@
     n, r = places.n, D // places.n
     h = r // 2
 
-    def kernel(me_ref, x_ref, mem_ref, lk_ref, lv_ref, bias_ref, mask_ref, own_ref, other_ref, *rest):
-        qkv_ref, kvm_ref, att_ref, p_ref, w_ref, *rest = rest
+    steps = spans // step_spans // parts
+    start = part * steps
+
+    def kernel(me_ref, x_ref, mem_ref, lk_ref, lv_ref, mask_ref, *rest):
+        if fresh:
+            own_ref, other_ref, *rest = rest
+        else:
+            w_ref, *rest = rest
+            if first:
+                norm_ref, *rest = rest
+            rest = rest[len(aliased) :]
+        qkv_ref, kvm_ref, att_ref, p_ref, *rest = rest
         if first:
-            hid_ref, xhat_ref, memt_ref, norm_ref, *rest = rest
+            hid_ref, xhat_ref, memt_ref, *rest = rest
+        if fresh:
+            w_ref, *rest = rest
+            if first:
+                norm_ref, *rest = rest
         ks, vs = rest
 
         @pl.when(pl.program_id(0) == 0)
@@ -306,9 +302,9 @@
             ks[...] = jnp.zeros_like(ks)
             vs[...] = jnp.zeros_like(vs)
             lower = me_ref[2] == 0
-            if first:
+            if first and fresh:
                 norm_ref[...] = jnp.zeros_like(norm_ref)
-            for f in range(n):
+            for f in range(n) if fresh else ():
                 slot = places.slot_from(me_ref, f)
                 mine, sib = own_ref[slot], other_ref[slot]
                 for at, part in (
@@ -347,11 +343,15 @@
         for g0 in range(0, groups, 4):
             work = {}
             units = [(g, p) for g in range(g0, g0 + 4) for p in range(2)]
+            dead = {
+                g: mask_ref[g % 2] + dead_keys(me_ref, (start + pl.program_id(0)) * groups + g + 1)
+                for g in range(g0, g0 + 4)
+            }
             for g, p in units:
                 s = slice(p * PAIR, (p + 1) * PAIR)
                 work[g, p] = dot_last(spread_pair(query[QROWS * g : QROWS * (g + 1), s]), ks[g, :, s])
             for g, p in units:
-                scores = work[g, p] + (mask_ref[g % 2] + bias_ref[g])
+                scores = work[g, p] + dead[g]
                 work[g, p] = jnp.exp(scores - jnp.max(scores, axis=1, keepdims=True))
             for g, p in units:
                 s = slice(p * PAIR, (p + 1) * PAIR)
@@ -369,42 +369,52 @@
 
     count = x.shape[0]
     wide = 3 * HALF
+
+    def some(shape, column=0):
+        return shape, lambda i: (start + i, column)
+
     ins = [
-        (x, *rows_of((rows, D))),
-        (memory, *rows_of((step_spans * MEM, D))),
-        (left_keys, *rows_of((step_spans * LEFT, HALF), half)),
-        (left_values, *rows_of((step_spans * LEFT, HALF), half)),
-        (bias, (groups, 1, KPAD), lambda i: (i, 0, 0)),
+        (x, *some((rows, D))),
+        (memory, *some((step_spans * MEM, D))),
+        (left_keys, *some((step_spans * LEFT, HALF), half)),
+        (left_values, *some((step_spans * LEFT, HALF), half)),
         (masks, *whole((2, 2 * QROWS, KPAD))),
-        (own, *whole(own.shape)),
-        (other, *whole(other.shape)),
     ]
     outs = [
-        ((count, wide), BF16, *rows_of((rows, wide))),
-        ((spans * MEM, 2 * HALF), BF16, *rows_of((step_spans * MEM, 2 * HALF))),
-        ((count, HALF), BF16, *rows_of((rows, HALF))),
-        ((2, 2 * count, KPAD), BF16, (2, 2 * rows, KPAD), lambda i: (0, i, 0)),
-        ((D, wide), BF16, *whole((D, wide))),
+        ((count, wide), BF16, *some((rows, wide))),
+        ((spans * MEM, 2 * HALF), BF16, *some((step_spans * MEM, 2 * HALF))),
+        ((count, HALF), BF16, *some((rows, HALF))),
+        ((2, 2 * count, KPAD), BF16, (2, 2 * rows, KPAD), lambda i: (0, start + i, 0)),
     ]
     if first:
-        columns = lambda i: (0, i)
+        columns = lambda i: (0, start + i)
         outs += [
-            ((count, D), BF16, *rows_of((rows, D))),
+            ((count, D), BF16, *some((rows, D))),
             ((D, count), BF16, (D, rows), columns),
             ((D, spans * MEM), BF16, (D, step_spans * MEM), columns),
-            ((8, D), F32, *whole((8, D))),
         ]
-    return call(
+    shared = 2 if first else 1
+    if fresh:
+        aliased = []
+        ins += [resident(a) for a in weights]
+        outs += [((D, wide), BF16, *whole((D, wide))), ((8, D), F32, *whole((8, D)))][:shared]
+    else:
+        aliased, kept = before[:-shared], before[-shared:]
+        ins += [(a, *whole(a.shape)) for a in kept] + [(a, None, 0) for a in aliased]
+    result = call(
         kernel,
         me,
-        (spans // step_spans,),
+        (steps,),
         ins,
         outs,
         [pltpu.VMEM((groups, KPAD, HALF), BF16)] * 2,
-        f"attention_forward_{half}",
-        flops=2 * count * D * wide * 4,
-        moved=2 * (count * D * 3 + spans * LEFT * D + spans * 4 * ROWS_SPAN * KPAD),
+        f"attention_forward_{half}_{part}",
+        limit=58,
+        flops=2 * count * D * wide * 4 // parts,
+        moved=2 * (count * D * 3 + spans * LEFT * D + spans * 4 * ROWS_SPAN * KPAD) // parts,
+        aliases={1 + len(ins) - len(aliased) + k: k for k in range(len(aliased))},
     )
+    return list(result) if fresh else [*result, *kept]
 
 
 def feed_forward(me, attended_halves, frames, cotangent, norm, up, down, places):
@@ -525,7 +535,7 @@
             (cotangent, *rows_of((rows, D))),
             (norm, *whole((8, D))),
         ]
-        + [(a, *whole(a.shape)) for a in (*up[0], *up[1], *down[0], *down[1])],
+        + [resident(a) for a in (*up[0], *up[1], *down[0], *down[1])],
         [
             ((count, D), BF16, *rows_of((rows, D))),
             ((count, D), F32, *rows_of((rows, D))),
@@ -542,6 +552,7 @@
             pltpu.VMEM((D, D), F32),
         ],
         "feed_forward",
+        limit=46,
         flops=2 * count * D * (6 * FF + 3 * D) * 2,
         moved=2 * count * D * 8,
     )
@@ -691,6 +702,7 @@
             pltpu.VMEM((8, wide), F32),
         ],
         f"attention_backward_{half}",
+        limit=58,
         flops=2 * count * D * wide * 8,
         moved=2 * (count * D * 5 + spans * LEFT * D + spans * 4 * ROWS_SPAN * KPAD),
     )
@@ -716,7 +728,7 @@
     ins += [(w, *whole((D, 3 * HALF))) for w in weights]
     ins += [(norm, *whole((8, D)))]
     if part:
-        ins += [(before, None, None)]
+        ins += [(before, None, 0)]
     (out,) = call(
         kernel,
         me,
@@ -773,7 +785,8 @@
         kernel,
         me,
         (1,),
-        [(a, *whole(a.shape)) for a in (*up, *down, ffn_in, ffn_in_m, ffn_in_v, ffn_out, ffn_out_m, ffn_out_v)],
+        [resident(a) for a in (*up, *down)]
+        + [(a, *whole(a.shape)) for a in (ffn_in, ffn_in_m, ffn_in_v, ffn_out, ffn_out_m, ffn_out_v)],
         [(s, t, *whole(s)) for s in (si, so) for t in (F32, F32, F32, F32, BF16)],
         [],
         "update_ffn",
@@ -792,39 +805,51 @@
         outs = refs[len(sums) + 6 : len(sums) + 11]
         norm_outs = refs[len(sums) + 11 :]
         lower = me_ref[2] == 0
-
-        def put(k, at, columns, grad):
-            rate = RATES_ATTENTION[k]
-            first, second, new = adamw(w[k, at, columns], grad, m[k, at, columns], v[k, at, columns], rate)
+        step = pl.program_id(0)
+
+        def put(rate, at, columns, grad):
+            first, second, new = adamw(w[0, at, columns], grad, m[0, at, columns], v[0, at, columns], rate)
             for ref, value in zip(outs, (grad, first, second, new, new.astype(BF16))):
-                ref[k, at, columns] = value
+                ref[0, at, columns] = value
 
         def halves(mine, sib):
             return jnp.where(lower, mine, sib).astype(F32), jnp.where(lower, sib, mine).astype(F32)
 
-        low, high = halves(*[places.y_joined(me_ref, ref)[:r] for ref in sum_refs[:2]])
-        put(3, slice(0, r), slice(0, HALF), low)
-        put(3, slice(0, r), slice(HALF, D), high)
-        for p in range(2):
-            columns = slice(p * HALF, (p + 1) * HALF)
-            for k in range(3):
-                at = p * 3 * h + k * h
-                low, high = halves(*[ref[at : at + h, :] for ref in sum_refs[2:]])
-                put(k, slice(0, h), columns, low)
-                put(k, slice(h, r), columns, high)
-        grad = sum_refs[2][6 * h :, :].astype(F32)[0:4, 0:r]
-        first, second, new = adamw(nw[...], grad, nm[...], nv[...], RATE_NORM)
-        for ref, value in zip(norm_outs, (grad, first, second, new, new.astype(BF16))):
-            ref[...] = value
+        for k in range(3):
+
+            @pl.when(step == k)
+            def _(k=k):
+                for p in range(2):
+                    columns = slice(p * HALF, (p + 1) * HALF)
+                    at = p * 3 * h + k * h
+                    low, high = halves(*[ref[at : at + h, :] for ref in sum_refs[2:]])
+                    put(RATES_ATTENTION[k], slice(0, h), columns, low)
+                    put(RATES_ATTENTION[k], slice(h, r), columns, high)
+
+        @pl.when(step == 3)
+        def _():
+            low, high = halves(*[places.y_joined(me_ref, ref)[:r] for ref in sum_refs[:2]])
+            put(RATES_ATTENTION[3], slice(0, r), slice(0, HALF), low)
+            put(RATES_ATTENTION[3], slice(0, r), slice(HALF, D), high)
+
+        @pl.when(step == 0)
+        def _():
+            grad = sum_refs[2][6 * h :, :].astype(F32)[0:4, 0:r]
+            first, second, new = adamw(nw[...], grad, nm[...], nv[...], RATE_NORM)
+            for ref, value in zip(norm_outs, (grad, first, second, new, new.astype(BF16))):
+                ref[...] = value
 
     shape, small = (4, r, D), (4, r)
-    ins = (*sums, attn_w, attn_m, attn_v, norm_params, norm_m, norm_v)
+    block = (1, r, D), lambda i: (i, 0, 0)
+    kinds = (F32, F32, F32, F32, BF16)
     return call(
         kernel,
         me,
-        (1,),
-        [(a, *whole(a.shape)) for a in ins],
-        [(s, t, *whole(s)) for s in (shape, small) for t in (F32, F32, F32, F32, BF16)],
+        (4,),
+        [resident(a) for a in sums]
+        + [(a, *block) for a in (attn_w, attn_m, attn_v)]
+        + [(a, *whole(small)) for a in (norm_params, norm_m, norm_v)],
+        [(shape, t, *block) for t in kinds] + [(small, t, *whole(small)) for t in kinds],
         [],
         "update_attention",
         moved=4 * 8 * 4 * r * D,
@@ -854,8 +879,7 @@
 ):
     X, Z = places.X, places.Z
     tie = lax.optimization_barrier
-    me = places.me()
-    bias = length_bias(lengths)
+    me = jnp.concatenate([places.me(), lengths])
     masks = jnp.asarray(span_masks())
 
     def direct(value):
@@ -885,34 +909,36 @@
             mine = add(mine, part)
         return mine
 
-    first_wire = pack_first(me, attn_w, norm_params, places)
+    first_wire = pack_first(attn_w, norm_params, places)
     mixed, up_wire = pack_rest(me, attn_w, ffn_in, ffn_out, places)
     first = direct(first_wire)
-    mixed = jnp.stack(along_z(mixed))
+    mixed = along_z(mixed)
     up_wire, first = tie((up_wire, first))
     first = jnp.stack(first)
-    mixed = along_x(mixed)
     up = along_z(up_wire)
     me, first = tie((me, first))
 
-    def forward(token, half, x, own, other):
+    def forward(token, half, x, weights, **part):
         return attention_forward(
-            token, half, x, memory, left_keys, left_values, bias, masks, own, other, places
+            token, half, x, memory, left_keys, left_values, masks, weights, places, **part
         )
 
-    qkv0, kvm0, att0, p0, w_low, hidden, xhat, memory_t, norm = forward(
-        me, 0, frames, first, places.other_core(first)
-    )
-    me, att0, mixed, up = tie((me, att0, mixed, up))
+    low = forward(me, 0, frames, (first, places.other_core(first)), parts=2)
+    me, low, mixed = tie((me, low, mixed))
+    mixed = along_x(jnp.stack(mixed))
+    low = forward(me, 0, frames, None, parts=2, part=1, before=low)
+    me, low, mixed, up = tie((me, low, mixed, up))
+    qkv0, kvm0, att0, p0, hidden, xhat, memory_t, w_low, norm = low
     h3 = 3 * (D // places.n) // 2
     second = jnp.concatenate([part[:, :h3] for part in mixed], axis=0)
     down = jnp.stack([part[:, h3:] for part in mixed])
     down = [down if dy == 0 else places.shift_y(down, dy) for dy in range(places.Y)]
     up = along_x(jnp.stack(up))
-    qkv1, kvm1, att1, p1, w_high = forward(me, 1, hidden, second, places.other_core(second))
-    me, att1, up, down = tie((me, att1, up, down))
-    up = up, [places.other_core(part) for part in up]
-    down = down, [places.other_core(part) for part in down]
+    early = places.other_core(up[0]), places.other_core(down[0])
+    qkv1, kvm1, att1, p1, w_high = forward(me, 1, hidden, (second, places.other_core(second)))
+    me, att1, up, down, early = tie((me, att1, up, down, early))
+    up = up, [early[0]] + [places.other_core(part) for part in up[1:]]
+    down = down, [early[1]] + [places.other_core(part) for part in down[1:]]
     output, grad_residual, grad_att, norm_two, keep_up, send_up, keep_down, send_down = feed_forward(
         me, (att0, att1), frames, cotangent, norm, up, down, places
     )

time: 226 us -> 214 us (0.947)
  Pallas kernels: 143 us -> 130 us
  starting transfers between devices: 54 us -> 49.2 us
  waiting for transfers between devices: 15 us -> 18.1 us
    pallas_call x11, Pallas kernels: 143 us -> 130 us  [call(): pl.pallas_call(kernel, grid_spec=pltpu.PrefetchScalarGridSpec(num_scalar_...]
    ppermute x27, starting transfers between devices: 45.9 us -> 41.4 us  [shift(): return lax.ppermute(value, 'fsdp', perm)]
    ppermute x27, waiting for transfers between devices: 5.46 us -> 8.92 us  [shift(): return lax.ppermute(value, 'fsdp', perm)]
    unnamed x63 -> x75, local copies, waits for them, and re-layouts: 5.09 us -> 3.21 us
  transfers between devices with their start and end apart: 45 -> 45, of which waited for: 7 -> 8; matrix products, arithmetic and copies ran while one was open for 3% -> 4% of each run, Pallas kernels for 38% -> 37%
where the time goes in v1:
time: 214 us
  Pallas kernels  130 us (61%)
  starting transfers between devices  49.2 us (23%)
  waiting for transfers between devices  18.1 us (8%)
  local copies, waits for them, and re-layouts  7.2 us (3%)
  other arithmetic  7.14 us (3%)
    pallas_call x11, Pallas kernels, call(): pl.pallas_call(kernel, grid_spec=pltpu.PrefetchScalarGridSpec(num_scalar_...  130 us
    ppermute x27, starting transfers between devices, shift(): return lax.ppermute(value, 'fsdp', perm)  41.4 us
    ppermute x27, waiting for transfers between devices, shift(): return lax.ppermute(value, 'fsdp', perm)  8.92 us
    ppermute x13, waiting for transfers between devices, other_core(): return lax.ppermute(value, 'dp', [(d, d ^ 1) for d in range(self.dp)])  5.56 us
  transfers between devices with their start and end apart: 45, of which 8 were waited for; matrix products, arithmetic and copies ran while one was open for 4% of the time, Pallas kernels for 37%

profile of v1, /device:TPU:0, one launch (start us, length us, event | category | flops | bytes accessed | tf_op | source)
XLA Modules:
  0.0 213.6 jit_solution(5748810019331523763)
XLA Ops:
  2.3 3.1 %collective-permute-start = (bf16[112,256]{1,0:T(8,128)(2,1)S(1)}, bf16[112,256]{1,0:T(8,128)(2,1)S(1)}, u32[]{:S(2)}, u32[]{:S(2)}) collective-permute-start(bf16[112,256]{1,0:T(8,128)(2,1)S(1)} %fusion.16), channel_id=1, source_target_pairs={{0,2},{1,3},{2,4},{3,5},{4,6},{5,7},{6,0},{7,1},{8,10},{9,11},{10,... | collective-permute-start | bytes 172040 | tf_op jit(solution)/shard_map/ppermute | solution.py:160
  5.4 2.6 %collective-permute-start.1 = (bf16[112,256]{1,0:T(8,128)(2,1)S(1)}, bf16[112,256]{1,0:T(8,128)(2,1)S(1)}, u32[]{:S(2)}, u32[]{:S(2)}) collective-permute-start(bf16[112,256]{1,0:T(8,128)(2,1)S(1)} %fusion.16), channel_id=1, source_target_pairs={{0,4},{1,5},{2,6},{3,7},{4,0},{5,1},{6,2},{7,3},{8,12},{9,13},{10,... | collective-permute-start | bytes 172040 | tf_op jit(solution)/shard_map/ppermute | solution.py:160
  12.7 2.9 %collective-permute-start.6 = (bf16[112,256]{1,0:T(8,128)(2,1)S(1)}, bf16[112,256]{1,0:T(8,128)(2,1)S(1)}, u32[]{:S(2)}, u32[]{:S(2)}) collective-permute-start(bf16[112,256]{1,0:T(8,128)(2,1)S(1)} %fusion.16), channel_id=1, source_target_pairs={{0,7},{1,6},{2,1},{3,0},{4,3},{5,2},{6,5},{7,4},{8,15},{9,14},{10,... | collective-permute-start | bytes 172040 | tf_op jit(solution)/shard_map/ppermute | solution.py:160
  17.0 2.8 %pack_rest.1 = (bf16[224,256]{1,0:T(8,128)(2,1)}, bf16[320,256]{1,0:T(8,128)(2,1)}) custom-call(s32[132]{0:T(256)} %concatenate.13.me_ref, f32[4,64,512]{2,1,0:T(8,128)} %refs_4_.1, f32[64,2048]{1,0:T(8,128)} %wi.1, f32[256,512]{1,0:T(8,128)} %wo.1), custom_call_target="tpu_custom_call" | custom-call | bytes 1572864 | tf_op jit(solution)/shard_map/pack_rest/pallas_call | solution.py:191
  20.0 2.1 collective-permute-start.10
  24.7 9.2 %attention_forward_0_0.1 = (bf16[2560,768]{1,0:T(8,128)(2,1)}, bf16[512,512]{1,0:T(8,128)(2,1)}, bf16[2560,256]{1,0:T(8,128)(2,1)}, bf16[2,5120,256]{2,1,0:T(8,1...) custom-call(s32[132]{0:T(256)} %concatenate.13.me_ref, ...), custom_call_target="tpu_custom_call" | custom-call | flops 4026531840 | bytes 8519680 | tf_op jit(solution)/shard_map/attention_forward_0_0/pallas_call | solution.py:191
  35.6 2.3 %collective-permute-start.12 = (bf16[320,256]{1,0:T(8,128)(2,1)S(1)}, bf16[320,256]{1,0:T(8,128)(2,1)S(1)}, u32[]{:S(2)}, u32[]{:S(2)}) collective-permute-start(bf16[320,256]{1,0:T(8,128)(2,1)S(1)} %copy-done.27), channel_id=1, source_target_pairs={{0,2},{1,3},{2,4},{3,5},{4,6},{5,7},{6,0},{7,1},{8,10},{9,11},{10,... | collective-permute-start | bytes 491528 | tf_op jit(solution)/shard_map/ppermute | solution.py:160
  38.1 2.2 %collective-permute-start.14 = (bf16[320,256]{1,0:T(8,128)(2,1)S(1)}, bf16[320,256]{1,0:T(8,128)(2,1)S(1)}, u32[]{:S(2)}, u32[]{:S(2)}) collective-permute-start(bf16[320,256]{1,0:T(8,128)(2,1)S(1)} %copy-done.27), channel_id=1, source_target_pairs={{0,6},{1,7},{2,0},{3,1},{4,2},{5,3},{6,4},{7,5},{8,14},{9,15},{10,... | collective-permute-start | bytes 491528 | tf_op jit(solution)/shard_map/ppermute | solution.py:160
  40.2 9.0 %attention_forward_0_1.1 = (bf16[2560,768]{1,0:T(8,128)(2,1)}, bf16[512,512]{1,0:T(8,128)(2,1)}, bf16[2560,256]{1,0:T(8,128)(2,1)}, bf16[2,5120,256]{2,1,0:T(8,1...) custom-call(s32[132]{0:T(256)} %concatenate.13.me_ref, ...), custom_call_target="tpu_custom_call", output_to_operand_aliasing={{0}: (8, {}), {1}: (9, {}), {2}: (10, {}), {3}: (11, {}), {... | custom-call | flops 4026531840 | bytes 8519680 | tf_op jit(solution)/shard_map/attention_forward_0_1/pallas_call | solution.py:191
  53.6 11.6 %attention_forward_1_0.1 = (bf16[2560,768]{1,0:T(8,128)(2,1)}, bf16[512,512]{1,0:T(8,128)(2,1)}, bf16[2560,256]{1,0:T(8,128)(2,1)}, bf16[2,5120,256]{2,1,0:T(8,128)(2,1)}, bf16[512,768]{1,0:T(8,128)(2,1)}) custom-call(s32[132]{0:T(256)} %concatenate.13.me_ref, bf16[2560,512]{1,0:T(8,128)(2,1)} %get-tuple-element.204.x_ref, bf16[512,512]{1,0:T(8,128)(2,1)} %mem_ref.5, ...), custom_call_target="tpu_custom_call" | custom-call | flops 8053063680 | bytes 17039360 | tf_op jit(solution)/shard_map/attention_forward_1_0/pallas_call | solution.py:191
  65.2 4.0 %collective-permute-done.16.rest_1_ = bf16[4,320,256]{2,1,0:T(8,128)(2,1)S(1)} collective-permute-done((bf16[4,320,256]{2,1,0:T(8,128)(2,1)S(1)}, bf16[4,320,256]{2,1,0:T(8,128)(2,1)S(1)}, u32[]{:S(2)}, u32[]{:S(2)}) %collective-permute-start.16) | collective-permute-done | bytes 655392 | tf_op jit(solution)/shard_map/ppermute | solution.py:160
  69.6 2.3 %collective-permute-done.21.rest_7_ = bf16[2,4,128,256]{3,2,1,0:T(8,128)(2,1)S(1)} collective-permute-done((bf16[2,4,128,256]{3,2,1,0:T(8,128)(2,1)S(1)}, bf16[2,4,128,256]{3,2,1,0:T(8,128)(2,1)S(1)}, u32[]{:S(2)}, u32[]{:S(2)}) %collective-permute-start.21) | collective-permute-done | bytes 524320 | tf_op jit(solution)/shard_map/ppermute | solution.py:174
  72.0 48.1 %feed_forward.1 = (bf16[2560,512]{1,0:T(8,128)(2,1)}, f32[2560,512]{1,0:T(8,128)}, bf16[2560,512]{1,0:T(8,128)(2,1)}, f32[8,512]{1,0:T(8,128)S(1)}, bf16[8,256,2...) custom-call(s32[132]{0:T(256)S(1)} %copy-done.16, ...), custom_call_target="tpu_custom_call" | custom-call | flops 72477573120 | bytes 20971520 | tf_op jit(solution)/shard_map/feed_forward/pallas_call | solution.py:191
  120.6 2.3 %collective-permute-done.22 = bf16[8,256,256]{2,1,0:T(8,128)(2,1)S(1)} collective-permute-done((bf16[8,256,256]{2,1,0:T(8,128)(2,1)S(1)}, bf16[8,256,256]{2,1,0:T(8,128)(2,1)S(1)}, u32[]{:S(2)}, u32[]{:S(2)}) %collective-permute-start.22) | collective-permute-done | bytes 1048608 | tf_op jit(solution)/shard_map/ppermute | solution.py:174
  125.9 16.7 %attention_backward_0.1 = (bf16[2560,768]{1,0:T(8,128)(2,1)}, bf16[8,96,256]{2,1,0:T(8,128)(2,1)}, bf16[8,96,256]{2,1,0:T(8,128)(2,1)}, f32[8,512]{1,0:T(8,128)}) custom-call(s32[132]{0:T(256)} %concatenate.13.me_ref, bf16[512,2560]{1,0:T(8,128)(2,1)} %get-tuple-element.228.xhat_ref, bf16[512,512]{1,0:T(8,128)(2,1)} %get-tuple-element.229.mem_ref, ...), custom_call_target="tpu_custom_call" | custom-call | flops 16106127360 | bytes 22282240 | tf_op jit(solution)/shard_map/attention_backward_0/pallas_call | solution.py:191
  146.7 4.0 %collective-permute-start.27 = (bf16[256,256]{1,0:T(8,128)(2,1)}, bf16[256,256]{1,0:T(8,128)(2,1)S(1)}, u32[]{:S(2)}, u32[]{:S(2)}) collective-permute-start(bf16[256,256]{1,0:T(8,128)(2,1)} %get-tuple-element.306), channel_id=1, source_target_pairs={{0,2},{1,3},{2,4},{3,5},{4,6},{5,7},{6,0},{7,1},{8,10},{9,11},{10,... | collective-permute-start | bytes 393224 | tf_op jit(solution)/shard_map/ppermute | solution.py:160
  153.0 16.7 %attention_backward_1.1 = (bf16[2560,768]{1,0:T(8,128)(2,1)}, bf16[8,112,256]{2,1,0:T(8,128)(2,1)}, bf16[8,112,256]{2,1,0:T(8,128)(2,1)}, f32[8,512]{1,0:T(8,128)}) custom-call(s32[132]{0:T(256)} %concatenate.13.me_ref, bf16[512,2560]{1,0:T(8,128)(2,1)} %get-tuple-element.228.xhat_ref, bf16[512,512]{1,0:T(8,128)(2,1)} %get-tuple-element.229.mem_ref, ...), custom_call_target="tpu_custom_call" | custom-call | flops 16106127360 | bytes 22282240 | tf_op jit(solution)/shard_map/attention_backward_1/pallas_call | solution.py:191
  181.4 5.1 %frames_gradient_0.1.rest_0_ = f32[2560,512]{1,0:T(8,128)} custom-call(s32[132]{0:T(256)S(1)} %copy-done.17, bf16[2560,512]{1,0:T(8,128)(2,1)S(1)} %copy-done, f32[2560,512]{1,0:T(8,128)S(1)} %bitcast.96, bf16[2560,768]{1,0:T(8,128)(2,1)S(1)} %copy-done.1, bf16[2560,768]{1,0:T(8,128)(2,1)S(1)} %copy-done.2, bf16[512,768]{1,0:T(8,128)(2,1)S(1)} %copy-done.3, ...), custom_call_target="tpu_custom_call" | custom-call | flops 2013265920 | bytes 10485760 | tf_op jit(solution)/shard_map/frames_gradient_0/pallas_call | solution.py:191
  186.6 4.2 %collective-permute-done.33 = bf16[4,208,256]{2,1,0:T(8,128)(2,1)S(1)} collective-permute-done((bf16[4,208,256]{2,1,0:T(8,128)(2,1)S(1)}, bf16[4,208,256]{2,1,0:T(8,128)(2,1)S(1)}, u32[]{:S(2)}, u32[]{:S(2)}) %collective-permute-start.33) | collective-permute-done | bytes 426016 | tf_op jit(solution)/shard_map/ppermute | solution.py:160
  192.8 2.8 %collective-permute-start.41 = (bf16[208,256]{1,0:T(8,128)(2,1)S(1)}, bf16[208,256]{1,0:T(8,128)(2,1)S(1)}, u32[]{:S(2)}, u32[]{:S(2)}) collective-permute-start(bf16[208,256]{1,0:T(8,128)(2,1)S(1)} %get-tuple-element.307), channel_id=1, source_target_pairs={{0,6},{1,7},{2,0},{3,1},{4,2},{5,3},{6,4},{7,5},{8,14},{9,15},{10,... | collective-permute-start | bytes 319496 | tf_op jit(solution)/shard_map/ppermute | solution.py:160
  196.3 5.4 %frames_gradient_1.1 = f32[2560,512]{1,0:T(8,128)} custom-call(s32[132]{0:T(256)S(1)} %copy-done.17, bf16[2560,512]{1,0:T(8,128)(2,1)S(1)} %copy-done, f32[2560,512]{1,0:T(8,128)S(1)} %bitcast.96, bf16[2560,768]{1,0:T(8,128)(2,1)S(1)} %copy-done.1, bf16[2560,768]{1,0:T(8,128)(2,1)S(1)} %copy-done.2, ...), custom_call_target="tpu_custom_call", output_to_operand_aliasing={{}: (8, {})} | custom-call | flops 2013265920 | bytes 10485760 | tf_op jit(solution)/shard_map/frames_gradient_1/pallas_call | solution.py:191
  203.7 3.6 %collective-permute-done.43 = bf16[208,256]{1,0:T(8,128)(2,1)S(1)} collective-permute-done((bf16[208,256]{1,0:T(8,128)(2,1)S(1)}, bf16[208,256]{1,0:T(8,128)(2,1)S(1)}, u32[]{:S(2)}, u32[]{:S(2)}) %collective-permute-start.43) | collective-permute-done | bytes 106528 | tf_op jit(solution)/shard_map/ppermute | solution.py:179
  207.5 3.1 %update_ffn.1 = (f32[64,2048]{1,0:T(8,128)}, f32[64,2048]{1,0:T(8,128)}, f32[64,2048]{1,0:T(8,128)}, f32[64,2048]{1,0:T(8,128)}, bf16[64,2048]{1,0:T(8,128)(2,1)...) custom-call(s32[132]{0:T(256)S(1)} %copy-done.17, ...), custom_call_target="tpu_custom_call" | custom-call | bytes 8388608 | tf_op jit(solution)/shard_map/update_ffn/pallas_call | solution.py:191
  210.7 2.7 %update_attention.1 = (f32[4,64,512]{2,1,0:T(8,128)}, f32[4,64,512]{2,1,0:T(8,128)}, f32[4,64,512]{2,1,0:T(8,128)}, f32[4,64,512]{2,1,0:T(8,128)}, bf16[4,64,512...) custom-call(s32[132]{0:T(256)S(1)} %copy-done.17, ...), custom_call_target="tpu_custom_call" | custom-call | bytes 4194304 | tf_op jit(solution)/shard_map/update_attention/pallas_call | solution.py:191
  (188 shorter events, 43.2 us)
Async XLA Ops:
  8.0 11.8 %collective-permute-start.2 = (bf16[112,256]{1,0:T(8,128)(2,1)S(1)}, bf16[112,256]{1,0:T(8,128)(2,1)S(1)}, u32[]{:S(2)}, u32[]{:S(2)}) collective-permute-start(bf16[112,256]{1,0:T(8,128)(2,1)S(1)} %fusion.16), channel_id=1, source_target_pairs={{0,6},{1,7},{2,0},{3,1},{4,2},{5,3},{6,4},{7,5},{8,14},{9,15},{10,... | collective-permute-start | bytes 172040 | tf_op jit(solution)/shard_map/ppermute | solution.py:160
  20.0 13.9 %collective-permute-start.10 = (bf16[224,256]{1,0:T(8,128)(2,1)}, bf16[224,256]{1,0:T(8,128)(2,1)S(1)}, u32[]{:S(2)}, u32[]{:S(2)}) collective-permute-start(bf16[224,256]{1,0:T(8,128)(2,1)} %get-tuple-element.198), channel_id=1, source_target_pairs={{0,6},{1,7},{2,0},{3,1},{4,2},{5,3},{6,4},{7,5},{8,14},{9,15},{10,... | collective-permute-start | bytes 344072 | tf_op jit(solution)/shard_map/ppermute | solution.py:160
  22.1 11.8 %collective-permute-start.8 = (bf16[224,256]{1,0:T(8,128)(2,1)}, bf16[224,256]{1,0:T(8,128)(2,1)S(1)}, u32[]{:S(2)}, u32[]{:S(2)}) collective-permute-start(bf16[224,256]{1,0:T(8,128)(2,1)} %get-tuple-element.198), channel_id=1, source_target_pairs={{0,2},{1,3},{2,4},{3,5},{4,6},{5,7},{6,0},{7,1},{8,10},{9,11},{10,... | collective-permute-start | bytes 344072 | tf_op jit(solution)/shard_map/ppermute | solution.py:160
  22.1 11.8 %collective-permute-start.9 = (bf16[224,256]{1,0:T(8,128)(2,1)}, bf16[224,256]{1,0:T(8,128)(2,1)S(1)}, u32[]{:S(2)}, u32[]{:S(2)}) collective-permute-start(bf16[224,256]{1,0:T(8,128)(2,1)} %get-tuple-element.198), channel_id=1, source_target_pairs={{0,4},{1,5},{2,6},{3,7},{4,0},{5,1},{6,2},{7,3},{8,12},{9,13},{10,... | collective-permute-start | bytes 344072 | tf_op jit(solution)/shard_map/ppermute | solution.py:160
  34.0 15.9 %collective-permute-start.11 = (bf16[4,224,256]{2,1,0:T(8,128)(2,1)S(1)}, bf16[4,224,256]{2,1,0:T(8,128)(2,1)S(1)}, u32[]{:S(2)}, u32[]{:S(2)}) collective-permute-start(bf16[4,224,256]{2,1,0:T(8,128)(2,1)S(1)} %pad_maximum_fusion.3), channel_id=1, source_target_pairs={{0,1},{1,0},{2,3},{3,2},{4,5},{5,4},{6,7},{7,6},{8,9},{9,8},{10,11... | collective-permute-start | bytes 1376264 | tf_op jit(solution)/shard_map/ppermute | solution.py:160
  35.6 13.7 %collective-permute-start.12 = (bf16[320,256]{1,0:T(8,128)(2,1)S(1)}, bf16[320,256]{1,0:T(8,128)(2,1)S(1)}, u32[]{:S(2)}, u32[]{:S(2)}) collective-permute-start(bf16[320,256]{1,0:T(8,128)(2,1)S(1)} %copy-done.27), channel_id=1, source_target_pairs={{0,2},{1,3},{2,4},{3,5},{4,6},{5,7},{6,0},{7,1},{8,10},{9,11},{10,... | collective-permute-start | bytes 491528 | tf_op jit(solution)/shard_map/ppermute | solution.py:160
  37.9 12.0 %collective-permute-start.13 = (bf16[320,256]{1,0:T(8,128)(2,1)S(1)}, bf16[320,256]{1,0:T(8,128)(2,1)S(1)}, u32[]{:S(2)}, u32[]{:S(2)}) collective-permute-start(bf16[320,256]{1,0:T(8,128)(2,1)S(1)} %copy-done.27), channel_id=1, source_target_pairs={{0,4},{1,5},{2,6},{3,7},{4,0},{5,1},{6,2},{7,3},{8,12},{9,13},{10,... | collective-permute-start | bytes 491528 | tf_op jit(solution)/shard_map/ppermute | solution.py:160
  38.1 11.8 %collective-permute-start.14 = (bf16[320,256]{1,0:T(8,128)(2,1)S(1)}, bf16[320,256]{1,0:T(8,128)(2,1)S(1)}, u32[]{:S(2)}, u32[]{:S(2)}) collective-permute-start(bf16[320,256]{1,0:T(8,128)(2,1)S(1)} %copy-done.27), channel_id=1, source_target_pairs={{0,6},{1,7},{2,0},{3,1},{4,2},{5,3},{6,4},{7,5},{8,14},{9,15},{10,... | collective-permute-start | bytes 491528 | tf_op jit(solution)/shard_map/ppermute | solution.py:160
  50.2 14.9 %collective-permute-start.17 = (bf16[2,4,128,256]{3,2,1,0:T(8,128)(2,1)S(1)}, bf16[2,4,128,256]{3,2,1,0:T(8,128)(2,1)S(1)}, u32[]{:S(2)}, u32[]{:S(2)}) collective-permute-start(bf16[2,4,128,256]{3,2,1,0:T(8,128)(2,1)S(1)} %pad_maximum_fusion.2.rest_4_), channel_id=1, source_target_pairs={{0,16},{8,24},{16,0},{24,8},{1,17},{9,25},{17,1},{25,9},{2,18},{10... | collective-permute-start | bytes 1572872 | tf_op jit(solution)/shard_map/ppermute | solution.py:171
  51.8 13.4 %collective-permute-start.19 = (bf16[2,4,128,256]{3,2,1,0:T(8,128)(2,1)S(1)}, bf16[2,4,128,256]{3,2,1,0:T(8,128)(2,1)S(1)}, u32[]{:S(2)}, u32[]{:S(2)}) collective-permute-start(bf16[2,4,128,256]{3,2,1,0:T(8,128)(2,1)S(1)} %pad_maximum_fusion.2.rest_4_), channel_id=1, source_target_pairs={{0,8},{8,0},{16,24},{24,16},{1,9},{9,1},{17,25},{25,17},{2,10},{10... | collective-permute-start | bytes 1572872 | tf_op jit(solution)/shard_map/ppermute | solution.py:174
  52.1 17.0 %collective-permute-start.16 = (bf16[4,320,256]{2,1,0:T(8,128)(2,1)S(1)}, bf16[4,320,256]{2,1,0:T(8,128)(2,1)S(1)}, u32[]{:S(2)}, u32[]{:S(2)}) collective-permute-start(bf16[4,320,256]{2,1,0:T(8,128)(2,1)S(1)} %pad_maximum_fusion.1.rest_0_), channel_id=1, source_target_pairs={{0,1},{1,0},{2,3},{3,2},{4,5},{5,4},{6,7},{7,6},{8,9},{9,8},{10,11... | collective-permute-start | bytes 1966088 | tf_op jit(solution)/shard_map/ppermute | solution.py:160
  52.8 16.3 %collective-permute-start.18 = (bf16[4,320,256]{2,1,0:T(8,128)(2,1)S(1)}, bf16[4,320,256]{2,1,0:T(8,128)(2,1)S(1)}, u32[]{:S(2)}, u32[]{:S(2)}) collective-permute-start(bf16[4,320,256]{2,1,0:T(8,128)(2,1)S(1)} %pad_maximum_fusion.1.rest_0_), channel_id=1, source_target_pairs={{0,8},{8,0},{16,24},{24,16},{1,9},{9,1},{17,25},{25,17},{2,10},{10... | collective-permute-start | bytes 1966088 | tf_op jit(solution)/shard_map/ppermute | solution.py:174
  123.3 19.3 %collective-permute-start.24 = (bf16[4,256,256]{2,1,0:T(8,128)(2,1)S(1)}, bf16[4,256,256]{2,1,0:T(8,128)(2,1)S(1)}, u32[]{:S(2)}, u32[]{:S(2)}) collective-permute-start(bf16[4,256,256]{2,1,0:T(8,128)(2,1)S(1)} %slice.190), channel_id=1, source_target_pairs={{0,1},{1,0},{2,3},{3,2},{4,5},{5,4},{6,7},{7,6},{8,9},{9,8},{10,11... | collective-permute-start | bytes 1572872 | tf_op jit(solution)/shard_map/ppermute | solution.py:160
  125.3 17.4 %collective-permute-start.25 = (bf16[8,160,256]{2,1,0:T(8,128)(2,1)S(1)}, bf16[8,160,256]{2,1,0:T(8,128)(2,1)S(1)}, u32[]{:S(2)}, u32[]{:S(2)}) collective-permute-start(bf16[8,160,256]{2,1,0:T(8,128)(2,1)S(1)} %fusion.2), channel_id=1, source_target_pairs={{0,16},{8,24},{16,0},{24,8},{1,17},{9,25},{17,1},{25,9},{2,18},{10... | collective-permute-start | bytes 1966088 | tf_op jit(solution)/shard_map/ppermute | solution.py:171
  142.5 27.1 %collective-permute-start.26 = (bf16[8,96,256]{2,1,0:T(8,128)(2,1)}, bf16[8,96,256]{2,1,0:T(8,128)(2,1)S(1)}, u32[]{:S(2)}, u32[]{:S(2)}) collective-permute-start(bf16[8,96,256]{2,1,0:T(8,128)(2,1)} %get-tuple-element.244), channel_id=1, source_target_pairs={{0,8},{8,0},{16,24},{24,16},{1,9},{9,1},{17,25},{25,17},{2,10},{10... | collective-permute-start | bytes 1179656 | tf_op jit(solution)/shard_map/ppermute | solution.py:174
  143.5 26.3 %collective-permute-start.30 = (bf16[4,160,256]{2,1,0:T(8,128)(2,1)}, bf16[4,160,256]{2,1,0:T(8,128)(2,1)}, u32[]{:S(2)}, u32[]{:S(2)}) collective-permute-start(bf16[4,160,256]{2,1,0:T(8,128)(2,1)} %slice.191), channel_id=1, source_target_pairs={{0,1},{1,0},{2,3},{3,2},{4,5},{5,4},{6,7},{7,6},{8,9},{9,8},{10,11... | collective-permute-start | bytes 983048 | tf_op jit(solution)/shard_map/ppermute | solution.py:160
  146.7 23.1 %collective-permute-start.27 = (bf16[256,256]{1,0:T(8,128)(2,1)}, bf16[256,256]{1,0:T(8,128)(2,1)S(1)}, u32[]{:S(2)}, u32[]{:S(2)}) collective-permute-start(bf16[256,256]{1,0:T(8,128)(2,1)} %get-tuple-element.306), channel_id=1, source_target_pairs={{0,2},{1,3},{2,4},{3,5},{4,6},{5,7},{6,0},{7,1},{8,10},{9,11},{10,... | collective-permute-start | bytes 393224 | tf_op jit(solution)/shard_map/ppermute | solution.py:160
  150.7 19.1 %collective-permute-start.28 = (bf16[256,256]{1,0:T(8,128)(2,1)}, bf16[256,256]{1,0:T(8,128)(2,1)}, u32[]{:S(2)}, u32[]{:S(2)}) collective-permute-start(bf16[256,256]{1,0:T(8,128)(2,1)} %get-tuple-element.305), channel_id=1, source_target_pairs={{0,4},{1,5},{2,6},{3,7},{4,0},{5,1},{6,2},{7,3},{8,12},{9,13},{10,... | collective-permute-start | bytes 393224 | tf_op jit(solution)/shard_map/ppermute | solution.py:160
  151.8 18.0 %collective-permute-start.29 = (bf16[256,256]{1,0:T(8,128)(2,1)}, bf16[256,256]{1,0:T(8,128)(2,1)}, u32[]{:S(2)}, u32[]{:S(2)}) collective-permute-start(bf16[256,256]{1,0:T(8,128)(2,1)} %get-tuple-element.304), channel_id=1, source_target_pairs={{0,6},{1,7},{2,0},{3,1},{4,2},{5,3},{6,4},{7,5},{8,14},{9,15},{10,... | collective-permute-start | bytes 393224 | tf_op jit(solution)/shard_map/ppermute | solution.py:160
  171.3 15.3 %collective-permute-start.34 = (bf16[160,256]{1,0:T(8,128)(2,1)S(1)}, bf16[160,256]{1,0:T(8,128)(2,1)S(1)}, u32[]{:S(2)}, u32[]{:S(2)}) collective-permute-start(bf16[160,256]{1,0:T(8,128)(2,1)S(1)} %get-tuple-element.312), channel_id=1, source_target_pairs={{0,2},{1,3},{2,4},{3,5},{4,6},{5,7},{6,0},{7,1},{8,10},{9,11},{10,... | collective-permute-start | bytes 245768 | tf_op jit(solution)/shard_map/ppermute | solution.py:160
  172.1 14.4 %collective-permute-start.35 = (bf16[160,256]{1,0:T(8,128)(2,1)S(1)}, bf16[160,256]{1,0:T(8,128)(2,1)S(1)}, u32[]{:S(2)}, u32[]{:S(2)}) collective-permute-start(bf16[160,256]{1,0:T(8,128)(2,1)S(1)} %get-tuple-element.311), channel_id=1, source_target_pairs={{0,4},{1,5},{2,6},{3,7},{4,0},{5,1},{6,2},{7,3},{8,12},{9,13},{10,... | collective-permute-start | bytes 245768 | tf_op jit(solution)/shard_map/ppermute | solution.py:160
  173.9 12.6 %collective-permute-start.36 = (bf16[160,256]{1,0:T(8,128)(2,1)S(1)}, bf16[160,256]{1,0:T(8,128)(2,1)S(1)}, u32[]{:S(2)}, u32[]{:S(2)}) collective-permute-start(bf16[160,256]{1,0:T(8,128)(2,1)S(1)} %get-tuple-element.310), channel_id=1, source_target_pairs={{0,6},{1,7},{2,0},{3,1},{4,2},{5,3},{6,4},{7,5},{8,14},{9,15},{10,... | collective-permute-start | bytes 245768 | tf_op jit(solution)/shard_map/ppermute | solution.py:160
  179.4 11.4 %collective-permute-start.33 = (bf16[4,208,256]{2,1,0:T(8,128)(2,1)S(1)}, bf16[4,208,256]{2,1,0:T(8,128)(2,1)S(1)}, u32[]{:S(2)}, u32[]{:S(2)}) collective-permute-start(bf16[4,208,256]{2,1,0:T(8,128)(2,1)S(1)} %fusion.1), channel_id=1, source_target_pairs={{0,1},{1,0},{2,3},{3,2},{4,5},{5,4},{6,7},{7,6},{8,9},{9,8},{10,11... | collective-permute-start | bytes 1277960 | tf_op jit(solution)/shard_map/ppermute | solution.py:160
  190.9 10.9 %collective-permute-start.39 = (bf16[208,256]{1,0:T(8,128)(2,1)S(1)}, bf16[208,256]{1,0:T(8,128)(2,1)S(1)}, u32[]{:S(2)}, u32[]{:S(2)}) collective-permute-start(bf16[208,256]{1,0:T(8,128)(2,1)S(1)} %get-tuple-element.309), channel_id=1, source_target_pairs={{0,2},{1,3},{2,4},{3,5},{4,6},{5,7},{6,0},{7,1},{8,10},{9,11},{10,... | collective-permute-start | bytes 319496 | tf_op jit(solution)/shard_map/ppermute | solution.py:160
  (55 other events, 465.7 us)

commit v2 on v1

--- a/solution.py
+++ b/solution.py
@@ -184,6 +184,8 @@
 
 def call(kernel, me, grid, ins, outs, scratch, name, flops=0, moved=0, aliases=None, limit=32):
     def spec(block, index):
+        if block == "scalar":
+            return pl.BlockSpec(memory_space=pltpu.SMEM)
         if block is None:
             return pl.BlockSpec(memory_space=pltpu.VMEM if index is None else pl.ANY)
         return pl.BlockSpec(block, lambda *a: index(*a[:-1]))
@@ -199,7 +201,7 @@
         ),
         out_shape=[jax.ShapeDtypeStruct(s, d) for s, d, _, _ in outs],
         compiler_params=pltpu.CompilerParams(vmem_limit_bytes=limit * 2**20),
-        cost_estimate=pl.CostEstimate(flops=flops, bytes_accessed=moved, transcendentals=0),
+        cost_estimate=pl.CostEstimate(flops=flops // 1000, bytes_accessed=moved // 1000, transcendentals=0),
         input_output_aliases=aliases or {},
         name=name,
     )(me, *[a for a, _, _ in ins])
@@ -267,7 +269,7 @@
     )
 
 
-def attention_forward(me, half, x, memory, left_keys, left_values, masks, weights, places, part=0, parts=1, before=None):
+def attention_forward(me, half, x, memory, left_keys, left_values, lengths, masks, weights, places, part=0, parts=1, before=None):
     first = half == 0
     fresh = before is None
     spans = memory.shape[0] // MEM
@@ -280,7 +282,7 @@
     steps = spans // step_spans // parts
     start = part * steps
 
-    def kernel(me_ref, x_ref, mem_ref, lk_ref, lv_ref, mask_ref, *rest):
+    def kernel(me_ref, x_ref, mem_ref, lk_ref, lv_ref, len_ref, mask_ref, *rest):
         if fresh:
             own_ref, other_ref, *rest = rest
         else:
@@ -344,7 +346,7 @@
             work = {}
             units = [(g, p) for g in range(g0, g0 + 4) for p in range(2)]
             dead = {
-                g: mask_ref[g % 2] + dead_keys(me_ref, (start + pl.program_id(0)) * groups + g + 1)
+                g: mask_ref[g % 2] + dead_keys(len_ref, (start + pl.program_id(0)) * groups + g)
                 for g in range(g0, g0 + 4)
             }
             for g, p in units:
@@ -378,6 +380,7 @@
         (memory, *some((step_spans * MEM, D))),
         (left_keys, *some((step_spans * LEFT, HALF), half)),
         (left_values, *some((step_spans * LEFT, HALF), half)),
+        (lengths, "scalar", None),
         (masks, *whole((2, 2 * QROWS, KPAD))),
     ]
     outs = [
@@ -409,7 +412,7 @@
         outs,
         [pltpu.VMEM((groups, KPAD, HALF), BF16)] * 2,
         f"attention_forward_{half}_{part}",
-        limit=58,
+        limit=52,
         flops=2 * count * D * wide * 4 // parts,
         moved=2 * (count * D * 3 + spans * LEFT * D + spans * 4 * ROWS_SPAN * KPAD) // parts,
         aliases={1 + len(ins) - len(aliased) + k: k for k in range(len(aliased))},
@@ -702,7 +705,7 @@
             pltpu.VMEM((8, wide), F32),
         ],
         f"attention_backward_{half}",
-        limit=58,
+        limit=50,
         flops=2 * count * D * wide * 8,
         moved=2 * (count * D * 5 + spans * LEFT * D + spans * 4 * ROWS_SPAN * KPAD),
     )
@@ -752,46 +755,51 @@
     return a.astype(F32) + b.astype(F32)
 
 
-def update_ffn(me, up, down, ffn_in, ffn_in_m, ffn_in_v, ffn_out, ffn_out_m, ffn_out_v, places):
-    r, r2 = D // places.n, FF // places.n
-    half = FF // 2
-
-    def kernel(me_ref, own_ref, other_ref, own_down, other_down, wi, mi, vi, wo, mo, vo, *outs):
-        lower = me_ref[2] == 0
-
-        def halves(mine, sib):
-            return jnp.where(lower, mine, sib).astype(F32), jnp.where(lower, sib, mine).astype(F32)
-
-        def put(refs, at, grad, w, m, v, rate):
-            g_ref, f_ref, s_ref, n_ref, c_ref = refs
-            first, second, new = adamw(w[:, at], grad, m[:, at], v[:, at], rate)
-            g_ref[:, at] = grad
-            f_ref[:, at] = first
-            s_ref[:, at] = second
-            n_ref[:, at] = new
-            c_ref[:, at] = new.astype(BF16)
-
-        low, high = halves(own_ref[...], other_ref[...])
-        for k in range(4):
-            for base, part in ((0, low), (half, high)):
-                at = slice(base + k * HALF, base + (k + 1) * HALF)
-                put(outs[:5], at, part[k * r : (k + 1) * r], wi, mi, vi, RATE_FFN_IN)
-        low, high = halves(places.y_joined(me_ref, own_down), places.y_joined(me_ref, other_down))
-        for at, part in ((slice(0, HALF), low), (slice(HALF, D), high)):
-            put(outs[5:], at, part[r:], wo, mo, vo, RATE_FFN_OUT)
-
-    si, so = (r, FF), (r2, D)
+def update_rows(me, sums, rate, weight, first, second, name, joined):
+    shape = weight.shape
+
+    def kernel(me_ref, own_ref, other_ref, w, m, v, *outs):
+        for at, part in joined(me_ref, own_ref, other_ref):
+            part = part.astype(F32)
+            new = adamw(w[:, at], part, m[:, at], v[:, at], rate)
+            for ref, value in zip(outs, (part, *new, new[2].astype(BF16))):
+                ref[:, at] = value
+
     return call(
         kernel,
         me,
         (1,),
-        [resident(a) for a in (*up, *down)]
-        + [(a, *whole(a.shape)) for a in (ffn_in, ffn_in_m, ffn_in_v, ffn_out, ffn_out_m, ffn_out_v)],
-        [(s, t, *whole(s)) for s in (si, so) for t in (F32, F32, F32, F32, BF16)],
+        [resident(a) for a in sums] + [(a, *whole(shape)) for a in (weight, first, second)],
+        [(shape, t, *whole(shape)) for t in (F32, F32, F32, F32, BF16)],
         [],
-        "update_ffn",
-        moved=4 * 8 * (r * FF + r2 * D),
+        name,
+        moved=4 * 8 * shape[0] * shape[1],
     )
+
+
+def update_up(me, sums, ffn_in, ffn_in_m, ffn_in_v, places):
+    r = D // places.n
+
+    def joined(me_ref, own_ref, other_ref):
+        lower = me_ref[2] == 0
+        mine, sib = own_ref[...], other_ref[...]
+        for base, part in ((0, jnp.where(lower, mine, sib)), (FF // 2, jnp.where(lower, sib, mine))):
+            for k in range(4):
+                yield slice(base + k * HALF, base + (k + 1) * HALF), part[k * r : (k + 1) * r]
+
+    return update_rows(me, sums, RATE_FFN_IN, ffn_in, ffn_in_m, ffn_in_v, "update_up", joined)
+
+
+def update_down(me, sums, ffn_out, ffn_out_m, ffn_out_v, places):
+    r = D // places.n
+
+    def joined(me_ref, own_ref, other_ref):
+        lower = me_ref[2] == 0
+        mine, sib = [places.y_joined(me_ref, ref)[r:] for ref in (own_ref, other_ref)]
+        yield slice(0, HALF), jnp.where(lower, mine, sib)
+        yield slice(HALF, D), jnp.where(lower, sib, mine)
+
+    return update_rows(me, sums, RATE_FFN_OUT, ffn_out, ffn_out_m, ffn_out_v, "update_down", joined)
 
 
 def update_attention(me, rest, sums, attn_w, attn_m, attn_v, norm_params, norm_m, norm_v, places):
@@ -879,7 +887,7 @@
 ):
     X, Z = places.X, places.Z
     tie = lax.optimization_barrier
-    me = jnp.concatenate([places.me(), lengths])
+    me = places.me()
     masks = jnp.asarray(span_masks())
 
     def direct(value):
@@ -920,7 +928,7 @@
 
     def forward(token, half, x, weights, **part):
         return attention_forward(
-            token, half, x, memory, left_keys, left_values, masks, weights, places, **part
+            token, half, x, memory, left_keys, left_values, lengths, masks, weights, places, **part
         )
 
     low = forward(me, 0, frames, (first, places.other_core(first)), parts=2)
@@ -961,11 +969,13 @@
     got_up, got_down = send_z(up), send_x(down)
     got0 = places.other_core(send0)
     d1, keep1, send1, n1 = backward(me, 1, (qkv1, kvm1, p1, w_high, att1), [norm_two, n0])
-    me, d1, got0, got_up, got_down = tie((me, d1, got0, got_up, got_down))
+    me, d1, keep1, send1, got0, got_up, got_down = tie((me, d1, keep1, send1, got0, got_up, got_down))
     got1 = places.other_core(send1)
+    attn = jnp.concatenate([add(keep0, got0), add(keep1, got1)], axis=1)
+    attn, up, down, got_up, got_down = tie((attn, up, down, got_up, got_down))
+    attn = split(attn)
+    got = send_x(attn)
     up, down = collect(up[0], got_up).astype(BF16), collect(down[0], got_down)
-    attn = split(jnp.concatenate([add(keep0, got0), add(keep1, got1)], axis=1))
-    got = send_x(attn)
     got_down = send_z(down)
     up = places.sum_over_y(up)
     frames_part = functools.partial(
@@ -984,11 +994,15 @@
     me, input_grad, up, down, got = tie((me, input_grad, up, down, got))
     down = down, places.other_core(down)
     attn = places.sum_over_y(collect(attn[0], got).astype(BF16))
-    ffn = update_ffn(me, up, down, ffn_in, ffn_in_m, ffn_in_v, ffn_out, ffn_out_m, ffn_out_v, places)
+    ffn_up = update_up(me, up, ffn_in, ffn_in_m, ffn_in_v, places)
+    me, ffn_up, attn, down = tie((me, ffn_up, attn, down))
     attn = attn, places.other_core(attn)
+    ffn_down = update_down(me, down, ffn_out, ffn_out_m, ffn_out_v, places)
+    me, ffn_down = tie((me, ffn_down))
     attention = update_attention(
         me, down, attn, attn_w, attn_m, attn_v, norm_params, norm_m, norm_v, places
     )
+    ffn = *ffn_up, *ffn_down
     return (output, input_grad, *attention[:5], *ffn, *attention[5:])
 
 

time: 214 us -> 203 us (0.949)
  other arithmetic: 7.14 us -> 3.14 us
  local copies, waits for them, and re-layouts: 7.2 us -> 3.98 us
  waiting for transfers between devices: 18.1 us -> 15.7 us
    ppermute x27, waiting for transfers between devices: 8.92 us -> 5.07 us  [shift(): return lax.ppermute(value, 'fsdp', perm)]
    ppermute x13, waiting for transfers between devices: 5.56 us -> 8.59 us  [other_core(): return lax.ppermute(value, 'dp', [(d, d ^ 1) for d in range(self.dp)])]
    ppermute x2, starting transfers between devices: 3.17 us -> 0.84 us  [sum_over_y(): got = lax.ppermute(value, 'dp', [(d, d ^ 2 * step) for d in range(self.dp)])]
    pallas_call x11 -> x12, Pallas kernels: 130 us -> 129 us  [call(): pl.pallas_call(kernel, grid_spec=pltpu.PrefetchScalarGridSpec(num_scalar_...]
  transfers between devices with their start and end apart: 45 -> 45, of which waited for: 8 -> 9; matrix products, arithmetic and copies ran while one was open for 4% -> 1% of each run, Pallas kernels for 37% -> 39%
where the time goes in v2:
time: 203 us
  Pallas kernels  129 us (64%)
  starting transfers between devices  49.2 us (24%)
  waiting for transfers between devices  15.7 us (8%)
  local copies, waits for them, and re-layouts  3.98 us (2%)
  other arithmetic  3.14 us (2%)
    pallas_call x12, Pallas kernels, call(): pl.pallas_call(kernel, grid_spec=pltpu.PrefetchScalarGridSpec(num_scalar_...  129 us
    ppermute x27, starting transfers between devices, shift(): return lax.ppermute(value, 'fsdp', perm)  41.8 us
    ppermute x13, waiting for transfers between devices, other_core(): return lax.ppermute(value, 'dp', [(d, d ^ 1) for d in range(self.dp)])  8.59 us
    ppermute x27, waiting for transfers between devices, shift(): return lax.ppermute(value, 'fsdp', perm)  5.07 us
    ppermute x3, starting transfers between devices, shift_y(): lax.ppermute(value, 'dp', [(d, (d + 2 * dy) % dp) for d in range(dp)])  4.66 us
  transfers between devices with their start and end apart: 45, of which 9 were waited for; matrix products, arithmetic and copies ran while one was open for 1% of the time, Pallas kernels for 39%

profile of v2, /device:TPU:0, one launch (start us, length us, event | category | flops | bytes accessed | tf_op | source)
XLA Modules:
  0.0 203.0 jit_solution(9641381262453919438)
XLA Ops:
  2.4 3.1 %collective-permute-start = (bf16[112,256]{1,0:T(8,128)(2,1)S(1)}, bf16[112,256]{1,0:T(8,128)(2,1)S(1)}, u32[]{:S(2)}, u32[]{:S(2)}) collective-permute-start(bf16[112,256]{1,0:T(8,128)(2,1)S(1)} %fusion.13), channel_id=1, source_target_pairs={{0,2},{1,3},{2,4},{3,5},{4,6},{5,7},{6,0},{7,1},{8,10},{9,11},{10,... | collective-permute-start | bytes 172040 | tf_op jit(solution)/shard_map/ppermute | solution.py:160
  5.5 2.6 %collective-permute-start.1 = (bf16[112,256]{1,0:T(8,128)(2,1)S(1)}, bf16[112,256]{1,0:T(8,128)(2,1)S(1)}, u32[]{:S(2)}, u32[]{:S(2)}) collective-permute-start(bf16[112,256]{1,0:T(8,128)(2,1)S(1)} %fusion.13), channel_id=1, source_target_pairs={{0,4},{1,5},{2,6},{3,7},{4,0},{5,1},{6,2},{7,3},{8,12},{9,13},{10,... | collective-permute-start | bytes 172040 | tf_op jit(solution)/shard_map/ppermute | solution.py:160
  12.8 2.9 %collective-permute-start.6 = (bf16[112,256]{1,0:T(8,128)(2,1)S(1)}, bf16[112,256]{1,0:T(8,128)(2,1)S(1)}, u32[]{:S(2)}, u32[]{:S(2)}) collective-permute-start(bf16[112,256]{1,0:T(8,128)(2,1)S(1)} %fusion.13), channel_id=1, source_target_pairs={{0,7},{1,6},{2,1},{3,0},{4,3},{5,2},{6,5},{7,4},{8,15},{9,14},{10,... | collective-permute-start | bytes 172040 | tf_op jit(solution)/shard_map/ppermute | solution.py:160
  16.3 2.7 %pack_rest.1 = (bf16[224,256]{1,0:T(8,128)(2,1)}, bf16[320,256]{1,0:T(8,128)(2,1)}) custom-call(s32[4]{0:T(128)} %pad_add_fusion.me_ref, f32[4,64,512]{2,1,0:T(8,128)} %refs_4_.1, f32[64,2048]{1,0:T(8,128)} %w.2, f32[256,512]{1,0:T(8,128)} %w.3), custom_call_target="tpu_custom_call" | custom-call | bytes 1572 | tf_op jit(solution)/shard_map/pack_rest/pallas_call | solution.py:193
  19.3 2.9 %collective-permute-start.10 = (bf16[224,256]{1,0:T(8,128)(2,1)}, bf16[224,256]{1,0:T(8,128)(2,1)S(1)}, u32[]{:S(2)}, u32[]{:S(2)}) collective-permute-start(bf16[224,256]{1,0:T(8,128)(2,1)} %get-tuple-element.222), channel_id=1, source_target_pairs={{0,6},{1,7},{2,0},{3,1},{4,2},{5,3},{6,4},{7,5},{8,14},{9,15},{10,... | collective-permute-start | bytes 344072 | tf_op jit(solution)/shard_map/ppermute | solution.py:160
  23.9 8.6 %attention_forward_0_0.1 = (bf16[2560,768]{1,0:T(8,128)(2,1)}, bf16[512,512]{1,0:T(8,128)(2,1)S(1)}, bf16[2560,256]{1,0:T(8,128)(2,1)}, bf16[2,5120,256]{2,1,0:T...) custom-call(s32[4]{0:T(128)S(1)} %copy-done.20, ...), custom_call_target="tpu_custom_call" | custom-call | flops 4026531 | bytes 8519 | tf_op jit(solution)/shard_map/attention_forward_0_0/pallas_call | solution.py:193
  34.8 2.4 %collective-permute-start.12 = (bf16[320,256]{1,0:T(8,128)(2,1)S(1)}, bf16[320,256]{1,0:T(8,128)(2,1)S(1)}, u32[]{:S(2)}, u32[]{:S(2)}) collective-permute-start(bf16[320,256]{1,0:T(8,128)(2,1)S(1)} %copy-done.26), channel_id=1, source_target_pairs={{0,2},{1,3},{2,4},{3,5},{4,6},{5,7},{6,0},{7,1},{8,10},{9,11},{10,... | collective-permute-start | bytes 491528 | tf_op jit(solution)/shard_map/ppermute | solution.py:160
  40.7 8.8 %attention_forward_0_1.1 = (bf16[2560,768]{1,0:T(8,128)(2,1)}, bf16[512,512]{1,0:T(8,128)(2,1)S(1)}, bf16[2560,256]{1,0:T(8,128)(2,1)}, bf16[2,5120,256]{2,1,0:T...) custom-call(s32[4]{0:T(128)S(1)} %copy-done.20, ...), custom_call_target="tpu_custom_call", output_to_operand_aliasing={{0}: (9, {}), {1}: (10, {}), {2}: (11, {}), {3}: (12, {}), ... | custom-call | flops 4026531 | bytes 8519 | tf_op jit(solution)/shard_map/attention_forward_0_1/pallas_call | solution.py:193
  55.4 11.1 %attention_forward_1_0.1 = (bf16[2560,768]{1,0:T(8,128)(2,1)}, bf16[512,512]{1,0:T(8,128)(2,1)S(1)}, bf16[2560,256]{1,0:T(8,128)(2,1)}, bf16[2,5120,256]{2,1,0:T(8,128)(2,1)}, bf16[512,768]{1,0:T(8,128)(2,1)}) custom-call(s32[4]{0:T(128)S(1)} %copy-done.20, bf16[2560,512]{1,0:T(8,128)(2,1)} %get-tuple-element.228.x_ref, bf16[512,512]{1,0:T(8,128)(2,1)} %mem_ref.5, ...), custom_call_target="tpu_custom_call" | custom-call | flops 8053063 | bytes 17039 | tf_op jit(solution)/shard_map/attention_forward_1_0/pallas_call | solution.py:193
  67.1 2.3 %collective-permute-done.21.rest_7_ = bf16[2,4,128,256]{3,2,1,0:T(8,128)(2,1)S(1)} collective-permute-done((bf16[2,4,128,256]{3,2,1,0:T(8,128)(2,1)S(1)}, bf16[2,4,128,256]{3,2,1,0:T(8,128)(2,1)S(1)}, u32[]{:S(2)}, u32[]{:S(2)}) %collective-permute-start.21) | collective-permute-done | bytes 524320 | tf_op jit(solution)/shard_map/ppermute | solution.py:174
  69.5 48.3 %feed_forward.1 = (bf16[2560,512]{1,0:T(8,128)(2,1)}, f32[2560,512]{1,0:T(8,128)}, bf16[2560,512]{1,0:T(8,128)(2,1)}, f32[8,512]{1,0:T(8,128)S(1)}, bf16[8,256,2...) custom-call(s32[4]{0:T(128)S(1)} %copy-done.21, ...), custom_call_target="tpu_custom_call" | custom-call | flops 72477576 | bytes 20971 | tf_op jit(solution)/shard_map/feed_forward/pallas_call | solution.py:193
  118.4 2.7 %collective-permute-done.23 = bf16[2,8,160,256]{3,2,1,0:T(8,128)(2,1)S(1)} collective-permute-done((bf16[2,8,160,256]{3,2,1,0:T(8,128)(2,1)}, bf16[2,8,160,256]{3,2,1,0:T(8,128)(2,1)S(1)}, u32[]{:S(2)}, u32[]{:S(2)}) %collective-permute-start.23) | collective-permute-done | bytes 1310752 | tf_op jit(solution)/shard_map/ppermute | solution.py:174
  124.7 15.9 %attention_backward_0.1 = (bf16[2560,768]{1,0:T(8,128)(2,1)}, bf16[8,96,256]{2,1,0:T(8,128)(2,1)S(1)}, bf16[8,96,256]{2,1,0:T(8,128)(2,1)S(1)}, f32[8,512]{1,0:T(8,128)S(1)}) custom-call(s32[4]{0:T(128)S(1)} %copy-done.21, bf16[512,2560]{1,0:T(8,128)(2,1)} %get-tuple-element.252.xhat_ref, bf16[512,512]{1,0:T(8,128)(2,1)S(1)} %copy-done.9, ...), custom_call_target="tpu_custom_call" | custom-call | flops 16106127 | bytes 22282 | tf_op jit(solution)/shard_map/attention_backward_0/pallas_call | solution.py:193
  142.3 4.2 %collective-permute-start.27 = (bf16[256,256]{1,0:T(8,128)(2,1)S(1)}, bf16[256,256]{1,0:T(8,128)(2,1)S(1)}, u32[]{:S(2)}, u32[]{:S(2)}) collective-permute-start(bf16[256,256]{1,0:T(8,128)(2,1)S(1)} %get-tuple-element.354), channel_id=1, source_target_pairs={{0,2},{1,3},{2,4},{3,5},{4,6},{5,7},{6,0},{7,1},{8,10},{9,11},{10,... | collective-permute-start | bytes 393224 | tf_op jit(solution)/shard_map/ppermute | solution.py:160
  146.6 2.4 %collective-permute-start.29 = (bf16[256,256]{1,0:T(8,128)(2,1)S(1)}, bf16[256,256]{1,0:T(8,128)(2,1)S(1)}, u32[]{:S(2)}, u32[]{:S(2)}) collective-permute-start(bf16[256,256]{1,0:T(8,128)(2,1)S(1)} %get-tuple-element.352), channel_id=1, source_target_pairs={{0,6},{1,7},{2,0},{3,1},{4,2},{5,3},{6,4},{7,5},{8,14},{9,15},{10,... | collective-permute-start | bytes 393224 | tf_op jit(solution)/shard_map/ppermute | solution.py:160
  149.0 16.0 %attention_backward_1.1 = (bf16[2560,768]{1,0:T(8,128)(2,1)}, bf16[8,112,256]{2,1,0:T(8,128)(2,1)S(1)}, bf16[8,112,256]{2,1,0:T(8,128)(2,1)S(1)}, f32[8,512]{1,0:T(8,128)}) custom-call(s32[4]{0:T(128)S(1)} %copy-done.21, bf16[512,2560]{1,0:T(8,128)(2,1)} %get-tuple-element.252.xhat_ref, bf16[512,512]{1,0:T(8,128)(2,1)S(1)} %copy-done.9, ...), custom_call_target="tpu_custom_call" | custom-call | flops 16106127 | bytes 22282 | tf_op jit(solution)/shard_map/attention_backward_1/pallas_call | solution.py:193
  168.7 2.5 %collective-permute-start.35 = (bf16[160,256]{1,0:T(8,128)(2,1)S(1)}, bf16[160,256]{1,0:T(8,128)(2,1)S(1)}, u32[]{:S(2)}, u32[]{:S(2)}) collective-permute-start(bf16[160,256]{1,0:T(8,128)(2,1)S(1)} %get-tuple-element.359), channel_id=1, source_target_pairs={{0,4},{1,5},{2,6},{3,7},{4,0},{5,1},{6,2},{7,3},{8,12},{9,13},{10,... | collective-permute-start | bytes 245768 | tf_op jit(solution)/shard_map/ppermute | solution.py:160
  172.6 5.1 %frames_gradient_0.1.rest_0_ = f32[2560,512]{1,0:T(8,128)} custom-call(s32[4]{0:T(128)S(1)} %copy-done.21, bf16[2560,512]{1,0:T(8,128)(2,1)S(1)} %copy-done, f32[2560,512]{1,0:T(8,128)S(1)} %bitcast.98, bf16[2560,768]{1,0:T(8,128)(2,1)S(1)} %copy-done.1, bf16[2560,768]{1,0:T(8,128)(2,1)S(1)} %copy-done.2, bf16[512,768]{1,0:T(8,128)(2,1)S(1)} %copy-done.3, ...), custom_call_target="tpu_custom_call" | custom-call | flops 2013265 | bytes 10485 | tf_op jit(solution)/shard_map/frames_gradient_0/pallas_call | solution.py:193
  181.5 2.4 %collective-permute-start.40 = (bf16[208,256]{1,0:T(8,128)(2,1)S(1)}, bf16[208,256]{1,0:T(8,128)(2,1)S(1)}, u32[]{:S(2)}, u32[]{:S(2)}) collective-permute-start(bf16[208,256]{1,0:T(8,128)(2,1)S(1)} %get-tuple-element.356), channel_id=1, source_target_pairs={{0,4},{1,5},{2,6},{3,7},{4,0},{5,1},{6,2},{7,3},{8,12},{9,13},{10,... | collective-permute-start | bytes 319496 | tf_op jit(solution)/shard_map/ppermute | solution.py:160
  185.3 5.4 %frames_gradient_1.1 = f32[2560,512]{1,0:T(8,128)} custom-call(s32[4]{0:T(128)S(1)} %copy-done.21, bf16[2560,512]{1,0:T(8,128)(2,1)S(1)} %copy-done, f32[2560,512]{1,0:T(8,128)S(1)} %bitcast.98, bf16[2560,768]{1,0:T(8,128)(2,1)S(1)} %copy-done.1, bf16[2560,768]{1,0:T(8,128)(2,1)S(1)} %copy-done.2, ...), custom_call_target="tpu_custom_call", output_to_operand_aliasing={{}: (8, {})} | custom-call | flops 2013265 | bytes 10485 | tf_op jit(solution)/shard_map/frames_gradient_1/pallas_call | solution.py:193
  193.2 2.3 %update_up.1 = (f32[64,2048]{1,0:T(8,128)}, f32[64,2048]{1,0:T(8,128)}, f32[64,2048]{1,0:T(8,128)}, f32[64,2048]{1,0:T(8,128)}, bf16[64,2048]{1,0:T(8,128)(2,1)}) custom-call(s32[4]{0:T(128)S(1)} %copy-done.21, bf16[256,256]{1,0:T(8,128)(2,1)S(1)} %add_convert_fusion.own_ref, bf16[256,256]{1,0:T(8,128)(2,1)S(1)} %collective-permute-done.37.other_ref, ...), custom_call_target="tpu_custom_call" | custom-call | bytes 4194 | tf_op jit(solution)/shard_map/update_up/pallas_call | solution.py:193
  195.6 2.0 collective-permute-done.42
  197.7 2.3 %update_down.1 = (f32[256,512]{1,0:T(8,128)}, f32[256,512]{1,0:T(8,128)}, f32[256,512]{1,0:T(8,128)}, f32[256,512]{1,0:T(8,128)}, bf16[256,512]{1,0:T(8,128)(2,1)}) custom-call(s32[4]{0:T(128)S(1)} %copy-done.21, bf16[2,160,256]{2,1,0:T(8,128)(2,1)S(1)} %pad_maximum_fusion.5.own_ref.refs_0_, ...), custom_call_target="tpu_custom_call" | custom-call | bytes 4194 | tf_op jit(solution)/shard_map/update_down/pallas_call | solution.py:193
  200.1 2.7 %update_attention.1 = (f32[4,64,512]{2,1,0:T(8,128)}, f32[4,64,512]{2,1,0:T(8,128)}, f32[4,64,512]{2,1,0:T(8,128)}, f32[4,64,512]{2,1,0:T(8,128)}, bf16[4,64,512...) custom-call(s32[4]{0:T(128)S(1)} %copy-done.21, ...), custom_call_target="tpu_custom_call" | custom-call | bytes 4194 | tf_op jit(solution)/shard_map/update_attention/pallas_call | solution.py:193
  (181 shorter events, 39.4 us)
Async XLA Ops:
  8.0 11.0 %collective-permute-start.2 = (bf16[112,256]{1,0:T(8,128)(2,1)S(1)}, bf16[112,256]{1,0:T(8,128)(2,1)S(1)}, u32[]{:S(2)}, u32[]{:S(2)}) collective-permute-start(bf16[112,256]{1,0:T(8,128)(2,1)S(1)} %fusion.13), channel_id=1, source_target_pairs={{0,6},{1,7},{2,0},{3,1},{4,2},{5,3},{6,4},{7,5},{8,14},{9,15},{10,... | collective-permute-start | bytes 172040 | tf_op jit(solution)/shard_map/ppermute | solution.py:160
  19.3 13.2 %collective-permute-start.10 = (bf16[224,256]{1,0:T(8,128)(2,1)}, bf16[224,256]{1,0:T(8,128)(2,1)S(1)}, u32[]{:S(2)}, u32[]{:S(2)}) collective-permute-start(bf16[224,256]{1,0:T(8,128)(2,1)} %get-tuple-element.222), channel_id=1, source_target_pairs={{0,6},{1,7},{2,0},{3,1},{4,2},{5,3},{6,4},{7,5},{8,14},{9,15},{10,... | collective-permute-start | bytes 344072 | tf_op jit(solution)/shard_map/ppermute | solution.py:160
  22.2 10.4 %collective-permute-start.8 = (bf16[224,256]{1,0:T(8,128)(2,1)}, bf16[224,256]{1,0:T(8,128)(2,1)S(1)}, u32[]{:S(2)}, u32[]{:S(2)}) collective-permute-start(bf16[224,256]{1,0:T(8,128)(2,1)} %get-tuple-element.222), channel_id=1, source_target_pairs={{0,2},{1,3},{2,4},{3,5},{4,6},{5,7},{6,0},{7,1},{8,10},{9,11},{10,... | collective-permute-start | bytes 344072 | tf_op jit(solution)/shard_map/ppermute | solution.py:160
  22.2 11.8 %collective-permute-start.9 = (bf16[224,256]{1,0:T(8,128)(2,1)}, bf16[224,256]{1,0:T(8,128)(2,1)S(1)}, u32[]{:S(2)}, u32[]{:S(2)}) collective-permute-start(bf16[224,256]{1,0:T(8,128)(2,1)} %get-tuple-element.222), channel_id=1, source_target_pairs={{0,4},{1,5},{2,6},{3,7},{4,0},{5,1},{6,2},{7,3},{8,12},{9,13},{10,... | collective-permute-start | bytes 344072 | tf_op jit(solution)/shard_map/ppermute | solution.py:160
  34.1 16.2 %collective-permute-start.11 = (bf16[4,224,256]{2,1,0:T(8,128)(2,1)S(1)}, bf16[4,224,256]{2,1,0:T(8,128)(2,1)S(1)}, u32[]{:S(2)}, u32[]{:S(2)}) collective-permute-start(bf16[4,224,256]{2,1,0:T(8,128)(2,1)S(1)} %pad_maximum_fusion.3), channel_id=1, source_target_pairs={{0,1},{1,0},{2,3},{3,2},{4,5},{5,4},{6,7},{7,6},{8,9},{9,8},{10,11... | collective-permute-start | bytes 1376264 | tf_op jit(solution)/shard_map/ppermute | solution.py:160
  34.8 15.5 %collective-permute-start.12 = (bf16[320,256]{1,0:T(8,128)(2,1)S(1)}, bf16[320,256]{1,0:T(8,128)(2,1)S(1)}, u32[]{:S(2)}, u32[]{:S(2)}) collective-permute-start(bf16[320,256]{1,0:T(8,128)(2,1)S(1)} %copy-done.26), channel_id=1, source_target_pairs={{0,2},{1,3},{2,4},{3,5},{4,6},{5,7},{6,0},{7,1},{8,10},{9,11},{10,... | collective-permute-start | bytes 491528 | tf_op jit(solution)/shard_map/ppermute | solution.py:160
  37.2 13.1 %collective-permute-start.13 = (bf16[320,256]{1,0:T(8,128)(2,1)S(1)}, bf16[320,256]{1,0:T(8,128)(2,1)S(1)}, u32[]{:S(2)}, u32[]{:S(2)}) collective-permute-start(bf16[320,256]{1,0:T(8,128)(2,1)S(1)} %copy-done.26), channel_id=1, source_target_pairs={{0,4},{1,5},{2,6},{3,7},{4,0},{5,1},{6,2},{7,3},{8,12},{9,13},{10,... | collective-permute-start | bytes 491528 | tf_op jit(solution)/shard_map/ppermute | solution.py:160
  37.9 12.4 %collective-permute-start.14 = (bf16[320,256]{1,0:T(8,128)(2,1)S(1)}, bf16[320,256]{1,0:T(8,128)(2,1)S(1)}, u32[]{:S(2)}, u32[]{:S(2)}) collective-permute-start(bf16[320,256]{1,0:T(8,128)(2,1)S(1)} %copy-done.26), channel_id=1, source_target_pairs={{0,6},{1,7},{2,0},{3,1},{4,2},{5,3},{6,4},{7,5},{8,14},{9,15},{10,... | collective-permute-start | bytes 491528 | tf_op jit(solution)/shard_map/ppermute | solution.py:160
  50.4 16.1 %collective-permute-start.16 = (bf16[4,320,256]{2,1,0:T(8,128)(2,1)S(1)}, bf16[4,320,256]{2,1,0:T(8,128)(2,1)S(1)}, u32[]{:S(2)}, u32[]{:S(2)}) collective-permute-start(bf16[4,320,256]{2,1,0:T(8,128)(2,1)S(1)} %pad_maximum_fusion.1.rest_0_), channel_id=1, source_target_pairs={{0,1},{1,0},{2,3},{3,2},{4,5},{5,4},{6,7},{7,6},{8,9},{9,8},{10,11... | collective-permute-start | bytes 1966088 | tf_op jit(solution)/shard_map/ppermute | solution.py:160
  51.3 15.3 %collective-permute-start.18 = (bf16[4,320,256]{2,1,0:T(8,128)(2,1)S(1)}, bf16[4,320,256]{2,1,0:T(8,128)(2,1)S(1)}, u32[]{:S(2)}, u32[]{:S(2)}) collective-permute-start(bf16[4,320,256]{2,1,0:T(8,128)(2,1)S(1)} %pad_maximum_fusion.1.rest_0_), channel_id=1, source_target_pairs={{0,8},{8,0},{16,24},{24,16},{1,9},{9,1},{17,25},{25,17},{2,10},{10... | collective-permute-start | bytes 1966088 | tf_op jit(solution)/shard_map/ppermute | solution.py:174
  51.4 15.2 %collective-permute-start.17 = (bf16[2,4,128,256]{3,2,1,0:T(8,128)(2,1)S(1)}, bf16[2,4,128,256]{3,2,1,0:T(8,128)(2,1)S(1)}, u32[]{:S(2)}, u32[]{:S(2)}) collective-permute-start(bf16[2,4,128,256]{3,2,1,0:T(8,128)(2,1)S(1)} %pad_maximum_fusion.2.rest_4_), channel_id=1, source_target_pairs={{0,16},{8,24},{16,0},{24,8},{1,17},{9,25},{17,1},{25,9},{2,18},{10... | collective-permute-start | bytes 1572872 | tf_op jit(solution)/shard_map/ppermute | solution.py:171
  52.9 13.6 %collective-permute-start.19 = (bf16[2,4,128,256]{3,2,1,0:T(8,128)(2,1)S(1)}, bf16[2,4,128,256]{3,2,1,0:T(8,128)(2,1)S(1)}, u32[]{:S(2)}, u32[]{:S(2)}) collective-permute-start(bf16[2,4,128,256]{3,2,1,0:T(8,128)(2,1)S(1)} %pad_maximum_fusion.2.rest_4_), channel_id=1, source_target_pairs={{0,8},{8,0},{16,24},{24,16},{1,9},{9,1},{17,25},{25,17},{2,10},{10... | collective-permute-start | bytes 1572872 | tf_op jit(solution)/shard_map/ppermute | solution.py:174
  121.5 19.1 %collective-permute-start.25 = (bf16[8,160,256]{2,1,0:T(8,128)(2,1)S(1)}, bf16[8,160,256]{2,1,0:T(8,128)(2,1)S(1)}, u32[]{:S(2)}, u32[]{:S(2)}) collective-permute-start(bf16[8,160,256]{2,1,0:T(8,128)(2,1)S(1)} %fusion), channel_id=1, source_target_pairs={{0,16},{8,24},{16,0},{24,8},{1,17},{9,25},{17,1},{25,9},{2,18},{10... | collective-permute-start | bytes 1966088 | tf_op jit(solution)/shard_map/ppermute | solution.py:171
  123.2 17.4 %collective-permute-start.24 = (bf16[4,256,256]{2,1,0:T(8,128)(2,1)S(1)}, bf16[4,256,256]{2,1,0:T(8,128)(2,1)S(1)}, u32[]{:S(2)}, u32[]{:S(2)}) collective-permute-start(bf16[4,256,256]{2,1,0:T(8,128)(2,1)S(1)} %slice.171), channel_id=1, source_target_pairs={{0,1},{1,0},{2,3},{3,2},{4,5},{5,4},{6,7},{7,6},{8,9},{9,8},{10,11... | collective-permute-start | bytes 1572872 | tf_op jit(solution)/shard_map/ppermute | solution.py:160
  140.6 24.4 %collective-permute-start.26 = (bf16[8,96,256]{2,1,0:T(8,128)(2,1)S(1)}, bf16[8,96,256]{2,1,0:T(8,128)(2,1)S(1)}, u32[]{:S(2)}, u32[]{:S(2)}) collective-permute-start(bf16[8,96,256]{2,1,0:T(8,128)(2,1)S(1)} %get-tuple-element.270), channel_id=1, source_target_pairs={{0,8},{8,0},{16,24},{24,16},{1,9},{9,1},{17,25},{25,17},{2,10},{10... | collective-permute-start | bytes 1179656 | tf_op jit(solution)/shard_map/ppermute | solution.py:174
  140.8 24.2 %collective-permute-start.30 = (bf16[4,160,256]{2,1,0:T(8,128)(2,1)S(1)}, bf16[4,160,256]{2,1,0:T(8,128)(2,1)S(1)}, u32[]{:S(2)}, u32[]{:S(2)}) collective-permute-start(bf16[4,160,256]{2,1,0:T(8,128)(2,1)S(1)} %slice.173), channel_id=1, source_target_pairs={{0,1},{1,0},{2,3},{3,2},{4,5},{5,4},{6,7},{7,6},{8,9},{9,8},{10,11... | collective-permute-start | bytes 983048 | tf_op jit(solution)/shard_map/ppermute | solution.py:160
  142.3 22.7 %collective-permute-start.27 = (bf16[256,256]{1,0:T(8,128)(2,1)S(1)}, bf16[256,256]{1,0:T(8,128)(2,1)S(1)}, u32[]{:S(2)}, u32[]{:S(2)}) collective-permute-start(bf16[256,256]{1,0:T(8,128)(2,1)S(1)} %get-tuple-element.354), channel_id=1, source_target_pairs={{0,2},{1,3},{2,4},{3,5},{4,6},{5,7},{6,0},{7,1},{8,10},{9,11},{10,... | collective-permute-start | bytes 393224 | tf_op jit(solution)/shard_map/ppermute | solution.py:160
  146.6 18.5 %collective-permute-start.28 = (bf16[256,256]{1,0:T(8,128)(2,1)S(1)}, bf16[256,256]{1,0:T(8,128)(2,1)S(1)}, u32[]{:S(2)}, u32[]{:S(2)}) collective-permute-start(bf16[256,256]{1,0:T(8,128)(2,1)S(1)} %get-tuple-element.353), channel_id=1, source_target_pairs={{0,4},{1,5},{2,6},{3,7},{4,0},{5,1},{6,2},{7,3},{8,12},{9,13},{10,... | collective-permute-start | bytes 393224 | tf_op jit(solution)/shard_map/ppermute | solution.py:160
  146.6 18.5 %collective-permute-start.29 = (bf16[256,256]{1,0:T(8,128)(2,1)S(1)}, bf16[256,256]{1,0:T(8,128)(2,1)S(1)}, u32[]{:S(2)}, u32[]{:S(2)}) collective-permute-start(bf16[256,256]{1,0:T(8,128)(2,1)S(1)} %get-tuple-element.352), channel_id=1, source_target_pairs={{0,6},{1,7},{2,0},{3,1},{4,2},{5,3},{6,4},{7,5},{8,14},{9,15},{10,... | collective-permute-start | bytes 393224 | tf_op jit(solution)/shard_map/ppermute | solution.py:160
  167.3 10.5 %collective-permute-start.32 = (bf16[256,256]{1,0:T(8,128)(2,1)S(1)}, bf16[256,256]{1,0:T(8,128)(2,1)S(1)}, u32[]{:S(2)}, u32[]{:S(2)}) collective-permute-start(bf16[256,256]{1,0:T(8,128)(2,1)S(1)} %fusion.3), channel_id=1, source_target_pairs={{0,16},{8,24},{16,0},{24,8},{1,17},{9,25},{17,1},{25,9},{2,18},{10... | collective-permute-start | bytes 393224 | tf_op jit(solution)/shard_map/ppermute | solution.py:179
  167.7 11.6 %collective-permute-start.33 = (bf16[4,208,256]{2,1,0:T(8,128)(2,1)S(1)}, bf16[4,208,256]{2,1,0:T(8,128)(2,1)S(1)}, u32[]{:S(2)}, u32[]{:S(2)}) collective-permute-start(bf16[4,208,256]{2,1,0:T(8,128)(2,1)S(1)} %slice.172), channel_id=1, source_target_pairs={{0,1},{1,0},{2,3},{3,2},{4,5},{5,4},{6,7},{7,6},{8,9},{9,8},{10,11... | collective-permute-start | bytes 1277960 | tf_op jit(solution)/shard_map/ppermute | solution.py:160
  179.4 11.3 %collective-permute-start.38 = (bf16[160,256]{1,0:T(8,128)(2,1)S(1)}, bf16[160,256]{1,0:T(8,128)(2,1)S(1)}, u32[]{:S(2)}, u32[]{:S(2)}) collective-permute-start(bf16[160,256]{1,0:T(8,128)(2,1)S(1)} %fusion.11), channel_id=1, source_target_pairs={{0,16},{8,24},{16,0},{24,8},{1,17},{9,25},{17,1},{25,9},{2,18},{10... | collective-permute-start | bytes 245768 | tf_op jit(solution)/shard_map/ppermute | solution.py:171
  181.2 11.5 %collective-permute-start.37 = (bf16[256,256]{1,0:T(8,128)(2,1)S(1)}, bf16[256,256]{1,0:T(8,128)(2,1)S(1)}, u32[]{:S(2)}, u32[]{:S(2)}) collective-permute-start(bf16[256,256]{1,0:T(8,128)(2,1)S(1)} %add_convert_fusion.own_ref), channel_id=1, source_target_pairs={{0,8},{8,0},{16,24},{24,16},{1,9},{9,1},{17,25},{25,17},{2,10},{10... | collective-permute-start | bytes 393224 | tf_op jit(solution)/shard_map/ppermute | solution.py:174
  181.5 11.3 %collective-permute-start.40 = (bf16[208,256]{1,0:T(8,128)(2,1)S(1)}, bf16[208,256]{1,0:T(8,128)(2,1)S(1)}, u32[]{:S(2)}, u32[]{:S(2)}) collective-permute-start(bf16[208,256]{1,0:T(8,128)(2,1)S(1)} %get-tuple-element.356), channel_id=1, source_target_pairs={{0,4},{1,5},{2,6},{3,7},{4,0},{5,1},{6,2},{7,3},{8,12},{9,13},{10,... | collective-permute-start | bytes 319496 | tf_op jit(solution)/shard_map/ppermute | solution.py:160
  (51 other events, 419.1 us)

commit v3 on v2

--- a/solution.py
+++ b/solution.py
@@ -147,6 +147,14 @@
         dx = lax.rem(f % self.X + self.X - me_ref[1], self.X)
         return dx * self.Z + dz
 
+    def slot_halving(self, me_ref, f):
+        dx = lax.rem(f % self.X + self.X - me_ref[1], self.X)
+        return dx * self.Z + lax.bitwise_xor(me_ref[0], jnp.int32(f // self.X))
+
+    def swap_z(self, value, step):
+        X = self.X
+        return lax.ppermute(value, "fsdp", [(f, (f // X ^ step) * X + f % X) for f in range(self.n)])
+
     def slot_from(self, me_ref, f):
         dz = lax.rem(me_ref[0] + self.Z - f // self.X, self.Z)
         dx = lax.rem(me_ref[1] + self.X - f % self.X, self.X)
@@ -188,6 +196,8 @@
             return pl.BlockSpec(memory_space=pltpu.SMEM)
         if block is None:
             return pl.BlockSpec(memory_space=pltpu.VMEM if index is None else pl.ANY)
+        if getattr(index, "by_device", False):
+            return pl.BlockSpec(block, lambda *a: index(a[-1]))
         return pl.BlockSpec(block, lambda *a: index(*a[:-1]))
 
     return pl.pallas_call(
@@ -207,6 +217,12 @@
     )(me, *[a for a, _, _ in ins])
 
 
+def placed(shape, index):
+    place = functools.partial(index)
+    place.by_device = True
+    return shape, place
+
+
 def resident(array):
     return array, None, None
 
@@ -232,24 +248,15 @@
     r, r2 = D // places.n, FF // places.n
     h, q = r // 2, r2 // places.dp
 
-    def kernel(me_ref, w_ref, in_ref, out_w_ref, second_ref, up_ref):
-        lower = me_ref[2] == 0
+    def kernel(me_ref, w_ref, wo_ref, in_ref, out_w_ref, second_ref, up_ref):
         for k in range(3):
-            w = w_ref[k, :, HALF:]
-            second_ref[k * h : (k + 1) * h, :] = jnp.where(lower, w[:h], w[h:]).astype(BF16)
-        member = me_ref[3] * 2 + me_ref[2]
-        w = out_w_ref[pl.ds(pl.multiple_of(member * q, q), q), :].astype(BF16)
+            second_ref[k * h : (k + 1) * h, :] = w_ref[k].astype(BF16)
+        w = out_w_ref[...].astype(BF16)
         second_ref[3 * h : 3 * h + q, :] = w[:, :HALF]
         second_ref[3 * h + q :, :] = w[:, HALF:]
-        half = FF // 2
         for k in range(4):
-            up_ref[k * r : (k + 1) * r, :] = jnp.where(
-                lower,
-                in_ref[:, k * HALF : (k + 1) * HALF],
-                in_ref[:, half + k * HALF : half + (k + 1) * HALF],
-            ).astype(BF16)
-        w = w_ref[3]
-        up_ref[4 * r :, :] = jnp.where(lower, w[:, :HALF], w[:, HALF:]).astype(BF16)
+            up_ref[k * r : (k + 1) * r, :] = in_ref[:, k * HALF : (k + 1) * HALF].astype(BF16)
+        up_ref[4 * r :, :] = wo_ref[0].astype(BF16)
 
     shapes = (3 * h + 2 * q, HALF), (5 * r, HALF)
     return call(
@@ -257,9 +264,10 @@
         me,
         (1,),
         [
-            (attn_w, *whole((4, r, D))),
-            (ffn_in, *whole((r, FF))),
-            (ffn_out, *whole((r2, D))),
+            (attn_w, *placed((3, h, HALF), lambda me_ref: (0, me_ref[2], 1))),
+            (attn_w, *placed((1, r, HALF), lambda me_ref: (3, 0, me_ref[2]))),
+            (ffn_in, *placed((r, FF // 2), lambda me_ref: (0, me_ref[2]))),
+            (ffn_out, *placed((q, D), lambda me_ref: (me_ref[3] * 2 + me_ref[2], 0))),
         ],
         [(shape, BF16, *whole(shape)) for shape in shapes],
         [],
@@ -412,7 +420,7 @@
         outs,
         [pltpu.VMEM((groups, KPAD, HALF), BF16)] * 2,
         f"attention_forward_{half}_{part}",
-        limit=52,
+        limit=48,
         flops=2 * count * D * wide * 4 // parts,
         moved=2 * (count * D * 3 + spans * LEFT * D + spans * 4 * ROWS_SPAN * KPAD) // parts,
         aliases={1 + len(ins) - len(aliased) + k: k for k in range(len(aliased))},
@@ -507,6 +515,7 @@
         def _():
             for f in range(n):
                 slot = places.slot_to(me_ref, f)
+                halving = places.slot_halving(me_ref, f)
 
                 def sides(low, high):
                     low, high = low.astype(BF16), high.astype(BF16)
@@ -515,7 +524,7 @@
                 here = slice(f * r, (f + 1) * r)
                 for k in range(4):
                     at = slice(k * r, (k + 1) * r)
-                    keep_up[slot, at, :], send_up[slot, at, :] = sides(
+                    keep_up[halving, at, :], send_up[halving, at, :] = sides(
                         acc1[here, k * HALF : (k + 1) * HALF],
                         acc1[here, FF // 2 + k * HALF : FF // 2 + (k + 1) * HALF],
                     )
@@ -555,7 +564,7 @@
             pltpu.VMEM((D, D), F32),
         ],
         "feed_forward",
-        limit=46,
+        limit=42,
         flops=2 * count * D * (6 * FF + 3 * D) * 2,
         moved=2 * count * D * 8,
     )
@@ -705,7 +714,7 @@
             pltpu.VMEM((8, wide), F32),
         ],
         f"attention_backward_{half}",
-        limit=50,
+        limit=46,
         flops=2 * count * D * wide * 8,
         moved=2 * (count * D * 5 + spans * LEFT * D + spans * 4 * ROWS_SPAN * KPAD),
     )
@@ -740,6 +749,7 @@
         [((count, D), F32, *block((rows, D)))],
         [],
         f"frames_gradient_{part}",
+        limit=32,
         flops=count * D * 3 * D,
         moved=count * D * 8,
         aliases={len(ins): 0} if part else None,
@@ -966,7 +976,8 @@
     d0, keep0, send0, n0 = backward(me, 0, (qkv0, kvm0, p0, w_low, att0))
     me, d0, got_up, got_down = tie((me, d0, got_up, got_down))
     up, down = collect(up[0], got_up), split(collect(down[0], got_down))
-    got_up, got_down = send_z(up), send_x(down)
+    half = places.Z // 2
+    got_up, got_down = [places.swap_z(up[half:].astype(BF16), half)], send_x(down)
     got0 = places.other_core(send0)
     d1, keep1, send1, n1 = backward(me, 1, (qkv1, kvm1, p1, w_high, att1), [norm_two, n0])
     me, d1, keep1, send1, got0, got_up, got_down = tie((me, d1, keep1, send1, got0, got_up, got_down))
@@ -975,9 +986,12 @@
     attn, up, down, got_up, got_down = tie((attn, up, down, got_up, got_down))
     attn = split(attn)
     got = send_x(attn)
-    up, down = collect(up[0], got_up).astype(BF16), collect(down[0], got_down)
+    up, down = collect(up[:half], got_up), collect(down[0], got_down)
     got_down = send_z(down)
-    up = places.sum_over_y(up)
+    while half > 2:
+        half //= 2
+        up = add(up[:half], places.swap_z(up[half:].astype(BF16), half))
+    up = up[0], places.swap_z(up[1].astype(BF16), 1)
     frames_part = functools.partial(
         frames_gradient, frames=frames, grad_residual=grad_residual, grads=(d0, d1),
         weights=(w_low, w_high), norm=norm,
@@ -987,12 +1001,18 @@
     me, input_grad, up, got, got_down = tie((me, input_grad, up, got, got_down))
     attn = collect(attn[0], got)
     got = send_z(attn)
-    up = up, places.other_core(up)
+    up = add(*up).astype(BF16)
     down = collect(down[0], got_down).astype(BF16)
-    down = jnp.stack([down if dy == 0 else places.shift_y(down, dy) for dy in range(places.Y)])
+    if places.Y == 2:
+        both = places.shift_y(jnp.concatenate([up, down], axis=0), 1)
+        up, both = add(up, both[: up.shape[0]]).astype(BF16), both[up.shape[0] :]
+        down = jnp.stack([down, both])
+    else:
+        up = places.sum_over_y(up)
+        down = jnp.stack([down if dy == 0 else places.shift_y(down, dy) for dy in range(places.Y)])
     input_grad = frames_part(me, part=1, before=input_grad)
     me, input_grad, up, down, got = tie((me, input_grad, up, down, got))
-    down = down, places.other_core(down)
+    up, down = (up, places.other_core(up)), (down, places.other_core(down))
     attn = places.sum_over_y(collect(attn[0], got).astype(BF16))
     ffn_up = update_up(me, up, ffn_in, ffn_in_m, ffn_in_v, places)
     me, ffn_up, attn, down = tie((me, ffn_up, attn, down))

time: 203 us -> 202 us (level)
  waiting for transfers between devices: 15.7 us -> 19.5 us
  starting transfers between devices: 49.2 us -> 46.9 us
    ppermute x27 -> x24, starting transfers between devices: 41.8 us -> 34.7 us  [shift(): return lax.ppermute(value, 'fsdp', perm)]
    ppermute x0 -> x2, starting transfers between devices: none -> 5.17 us  [swap_z(): lax.ppermute(value, 'fsdp', [(f, (f // X ^ step) * X + f % X) for f in ra...]
    ppermute x27 -> x24, waiting for transfers between devices: 5.07 us -> 7.3 us  [shift(): return lax.ppermute(value, 'fsdp', perm)]
  transfers between devices with their start and end apart: 45 -> 43, of which waited for: 9 -> 12; matrix products, arithmetic and copies ran while one was open for 1% -> 1% of each run, Pallas kernels for 39% -> 38%
where the time goes in v3:
time: 202 us
  Pallas kernels  128 us (63%)
  starting transfers between devices  46.9 us (23%)
  waiting for transfers between devices  19.5 us (10%)
  local copies, waits for them, and re-layouts  3.13 us (2%)
  other arithmetic  3.09 us (2%)
    pallas_call x12, Pallas kernels, call(): pl.pallas_call(kernel, grid_spec=pltpu.PrefetchScalarGridSpec(num_scalar_...  128 us
    ppermute x24, starting transfers between devices, shift(): return lax.ppermute(value, 'fsdp', perm)  34.7 us
    ppermute x13, waiting for transfers between devices, other_core(): return lax.ppermute(value, 'dp', [(d, d ^ 1) for d in range(self.dp)])  8.67 us
    ppermute x24, waiting for transfers between devices, shift(): return lax.ppermute(value, 'fsdp', perm)  7.3 us
    ppermute x2, starting transfers between devices, swap_z(): lax.ppermute(value, 'fsdp', [(f, (f // X ^ step) * X + f % X) for f in ra...  5.17 us
  transfers between devices with their start and end apart: 43, of which 12 were waited for; matrix products, arithmetic and copies ran while one was open for 1% of the time, Pallas kernels for 38%

profile of v3, /device:TPU:0, one launch (start us, length us, event | category | flops | bytes accessed | tf_op | source)
XLA Modules:
  0.0 201.8 jit_solution(4076715370824810498)
XLA Ops:
  2.4 3.1 %collective-permute-start = (bf16[112,256]{1,0:T(8,128)(2,1)S(1)}, bf16[112,256]{1,0:T(8,128)(2,1)S(1)}, u32[]{:S(2)}, u32[]{:S(2)}) collective-permute-start(bf16[112,256]{1,0:T(8,128)(2,1)S(1)} %fusion.11), channel_id=1, source_target_pairs={{0,2},{1,3},{2,4},{3,5},{4,6},{5,7},{6,0},{7,1},{8,10},{9,11},{10,... | collective-permute-start | bytes 172040 | tf_op jit(solution)/shard_map/ppermute | solution.py:168
  5.5 2.6 %collective-permute-start.1 = (bf16[112,256]{1,0:T(8,128)(2,1)S(1)}, bf16[112,256]{1,0:T(8,128)(2,1)S(1)}, u32[]{:S(2)}, u32[]{:S(2)}) collective-permute-start(bf16[112,256]{1,0:T(8,128)(2,1)S(1)} %fusion.11), channel_id=1, source_target_pairs={{0,4},{1,5},{2,6},{3,7},{4,0},{5,1},{6,2},{7,3},{8,12},{9,13},{10,... | collective-permute-start | bytes 172040 | tf_op jit(solution)/shard_map/ppermute | solution.py:168
  12.8 2.9 %collective-permute-start.6 = (bf16[112,256]{1,0:T(8,128)(2,1)S(1)}, bf16[112,256]{1,0:T(8,128)(2,1)S(1)}, u32[]{:S(2)}, u32[]{:S(2)}) collective-permute-start(bf16[112,256]{1,0:T(8,128)(2,1)S(1)} %fusion.11), channel_id=1, source_target_pairs={{0,7},{1,6},{2,1},{3,0},{4,3},{5,2},{6,5},{7,4},{8,15},{9,14},{10,... | collective-permute-start | bytes 172040 | tf_op jit(solution)/shard_map/ppermute | solution.py:168
  16.4 2.6 %pack_rest.1 = (bf16[224,256]{1,0:T(8,128)(2,1)}, bf16[320,256]{1,0:T(8,128)(2,1)}) custom-call(s32[4]{0:T(128)} %pad_add_fusion.me_ref, f32[4,64,512]{2,1,0:T(8,128)} %refs_4_.1, f32[4,64,512]{2,1,0:T(8,128)} %refs_4_.1, f32[64,2048]{1,0:T(8,128)} %w.2, f32[256,512]{1,0:T(8,128)} %w.3), custom_call_target="tpu_custom_call" | custom-call | bytes 1572 | tf_op jit(solution)/shard_map/pack_rest/pallas_call | solution.py:203
  19.3 3.0 %collective-permute-start.10 = (bf16[224,256]{1,0:T(8,128)(2,1)}, bf16[224,256]{1,0:T(8,128)(2,1)S(1)}, u32[]{:S(2)}, u32[]{:S(2)}) collective-permute-start(bf16[224,256]{1,0:T(8,128)(2,1)} %get-tuple-element.218), channel_id=1, source_target_pairs={{0,6},{1,7},{2,0},{3,1},{4,2},{5,3},{6,4},{7,5},{8,14},{9,15},{10,... | collective-permute-start | bytes 344072 | tf_op jit(solution)/shard_map/ppermute | solution.py:168
  23.2 8.3 %attention_forward_0_0.1 = (bf16[2560,768]{1,0:T(8,128)(2,1)}, bf16[512,512]{1,0:T(8,128)(2,1)S(1)}, bf16[2560,256]{1,0:T(8,128)(2,1)S(1)}, bf16[2,5120,256]{2,1...) custom-call(s32[4]{0:T(128)S(1)} %copy-done.18, ...), custom_call_target="tpu_custom_call" | custom-call | flops 4026531 | bytes 8519 | tf_op jit(solution)/shard_map/attention_forward_0_0/pallas_call | solution.py:203
  31.5 2.5 %collective-permute-done.9 = bf16[224,256]{1,0:T(8,128)(2,1)S(1)} collective-permute-done((bf16[224,256]{1,0:T(8,128)(2,1)}, bf16[224,256]{1,0:T(8,128)(2,1)S(1)}, u32[]{:S(2)}, u32[]{:S(2)}) %collective-permute-start.9) | collective-permute-done | bytes 114720 | tf_op jit(solution)/shard_map/ppermute | solution.py:168
  38.7 8.5 %attention_forward_0_1.1 = (bf16[2560,768]{1,0:T(8,128)(2,1)}, bf16[512,512]{1,0:T(8,128)(2,1)S(1)}, bf16[2560,256]{1,0:T(8,128)(2,1)S(1)}, bf16[2,5120,256]{2,1...) custom-call(s32[4]{0:T(128)S(1)} %copy-done.18, ...), custom_call_target="tpu_custom_call", output_to_operand_aliasing={{0}: (9, {}), {1}: (10, {}), {2}: (11, {}), {3}: (12, {}), ... | custom-call | flops 4026531 | bytes 8519 | tf_op jit(solution)/shard_map/attention_forward_0_1/pallas_call | solution.py:203
  55.0 10.7 %attention_forward_1_0.1 = (bf16[2560,768]{1,0:T(8,128)(2,1)}, bf16[512,512]{1,0:T(8,128)(2,1)S(1)}, bf16[2560,256]{1,0:T(8,128)(2,1)S(1)}, bf16[2,5120,256]{2,1,0:T(8,128)(2,1)}, bf16[512,768]{1,0:T(8,128)(2,1)S(1)}) custom-call(s32[4]{0:T(128)S(1)} %copy-done.18, bf16[2560,512]{1,0:T(8,128)(2,1)} %get-tuple-element.224.x_ref, ...), custom_call_target="tpu_custom_call" | custom-call | flops 8053063 | bytes 17039 | tf_op jit(solution)/shard_map/attention_forward_1_0/pallas_call | solution.py:203
  67.1 2.3 %collective-permute-done.21.rest_7_ = bf16[2,4,128,256]{3,2,1,0:T(8,128)(2,1)S(1)} collective-permute-done((bf16[2,4,128,256]{3,2,1,0:T(8,128)(2,1)S(1)}, bf16[2,4,128,256]{3,2,1,0:T(8,128)(2,1)S(1)}, u32[]{:S(2)}, u32[]{:S(2)}) %collective-permute-start.21) | collective-permute-done | bytes 524320 | tf_op jit(solution)/shard_map/ppermute | solution.py:182
  69.4 47.7 %feed_forward.1 = (bf16[2560,512]{1,0:T(8,128)(2,1)}, f32[2560,512]{1,0:T(8,128)}, bf16[2560,512]{1,0:T(8,128)(2,1)}, f32[8,512]{1,0:T(8,128)S(1)}, bf16[8,256,2...) custom-call(s32[4]{0:T(128)S(1)} %copy-done.18, ...), custom_call_target="tpu_custom_call" | custom-call | flops 72477576 | bytes 20971 | tf_op jit(solution)/shard_map/feed_forward/pallas_call | solution.py:203
  117.6 2.5 %collective-permute-done.23 = bf16[2,8,160,256]{3,2,1,0:T(8,128)(2,1)S(1)} collective-permute-done((bf16[2,8,160,256]{3,2,1,0:T(8,128)(2,1)S(1)}, bf16[2,8,160,256]{3,2,1,0:T(8,128)(2,1)S(1)}, u32[]{:S(2)}, u32[]{:S(2)}) %collective-permute-start.23) | collective-permute-done | bytes 1310752 | tf_op jit(solution)/shard_map/ppermute | solution.py:182
  123.4 15.9 %attention_backward_0.1 = (bf16[2560,768]{1,0:T(8,128)(2,1)}, bf16[8,96,256]{2,1,0:T(8,128)(2,1)S(1)}, bf16[8,96,256]{2,1,0:T(8,128)(2,1)S(1)}, f32[8,512]{1,0:T(8,128)S(1)}) custom-call(s32[4]{0:T(128)S(1)} %copy-done.18, bf16[512,2560]{1,0:T(8,128)(2,1)S(1)} %copy-done.1, bf16[512,512]{1,0:T(8,128)(2,1)S(1)} %get-tuple-element.249.mem_ref, ...), custom_call_target="tpu_custom_call" | custom-call | flops 16106127 | bytes 22282 | tf_op jit(solution)/shard_map/attention_backward_0/pallas_call | solution.py:203
  140.4 3.1 %collective-permute-start.27 = (bf16[2,256,256]{2,1,0:T(8,128)(2,1)S(1)}, bf16[2,256,256]{2,1,0:T(8,128)(2,1)S(1)}, u32[]{:S(2)}, u32[]{:S(2)}) collective-permute-start(bf16[2,256,256]{2,1,0:T(8,128)(2,1)S(1)} %slice.187), channel_id=1, source_target_pairs={{0,4},{1,5},{2,6},{3,7},{4,0},{5,1},{6,2},{7,3},{8,12},{9,13},{10,... | collective-permute-start | bytes 786440 | tf_op jit(solution)/shard_map/ppermute | solution.py:156
  143.5 16.0 %attention_backward_1.1 = (bf16[2560,768]{1,0:T(8,128)(2,1)}, bf16[8,112,256]{2,1,0:T(8,128)(2,1)S(1)}, bf16[8,112,256]{2,1,0:T(8,128)(2,1)S(1)}, f32[8,512]{1,0:T(8,128)}) custom-call(s32[4]{0:T(128)S(1)} %copy-done.18, bf16[512,2560]{1,0:T(8,128)(2,1)S(1)} %copy-done.1, bf16[512,512]{1,0:T(8,128)(2,1)S(1)} %get-tuple-element.249.mem_ref, ...), custom_call_target="tpu_custom_call" | custom-call | flops 16106127 | bytes 22282 | tf_op jit(solution)/shard_map/attention_backward_1/pallas_call | solution.py:203
  163.3 2.5 %collective-permute-start.33 = (bf16[160,256]{1,0:T(8,128)(2,1)S(1)}, bf16[160,256]{1,0:T(8,128)(2,1)S(1)}, u32[]{:S(2)}, u32[]{:S(2)}) collective-permute-start(bf16[160,256]{1,0:T(8,128)(2,1)S(1)} %get-tuple-element.346), channel_id=1, source_target_pairs={{0,4},{1,5},{2,6},{3,7},{4,0},{5,1},{6,2},{7,3},{8,12},{9,13},{10,... | collective-permute-start | bytes 245768 | tf_op jit(solution)/shard_map/ppermute | solution.py:168
  169.4 5.2 %frames_gradient_0.1.rest_0_ = f32[2560,512]{1,0:T(8,128)} custom-call(s32[4]{0:T(128)S(1)} %copy-done.18, bf16[2560,512]{1,0:T(8,128)(2,1)S(1)} %copy-done, f32[2560,512]{1,0:T(8,128)S(1)} %bitcast.88, bf16[2560,768]{1,0:T(8,128)(2,1)S(1)} %copy-done.2, bf16[2560,768]{1,0:T(8,128)(2,1)S(1)} %copy-done.3, ...), custom_call_target="tpu_custom_call" | custom-call | flops 2013265 | bytes 10485 | tf_op jit(solution)/shard_map/frames_gradient_0/pallas_call | solution.py:203
  174.8 2.6 %collective-permute-done.31 = bf16[4,208,256]{2,1,0:T(8,128)(2,1)S(1)} collective-permute-done((bf16[4,208,256]{2,1,0:T(8,128)(2,1)S(1)}, bf16[4,208,256]{2,1,0:T(8,128)(2,1)S(1)}, u32[]{:S(2)}, u32[]{:S(2)}) %collective-permute-start.31) | collective-permute-done | bytes 426016 | tf_op jit(solution)/shard_map/ppermute | solution.py:168
  181.0 2.3 %collective-permute-start.38 = (bf16[208,256]{1,0:T(8,128)(2,1)S(1)}, bf16[208,256]{1,0:T(8,128)(2,1)S(1)}, u32[]{:S(2)}, u32[]{:S(2)}) collective-permute-start(bf16[208,256]{1,0:T(8,128)(2,1)S(1)} %get-tuple-element.342), channel_id=1, source_target_pairs={{0,6},{1,7},{2,0},{3,1},{4,2},{5,3},{6,4},{7,5},{8,14},{9,15},{10,... | collective-permute-start | bytes 319496 | tf_op jit(solution)/shard_map/ppermute | solution.py:168
  183.4 5.4 %frames_gradient_1.1 = f32[2560,512]{1,0:T(8,128)} custom-call(s32[4]{0:T(128)S(1)} %copy-done.18, bf16[2560,512]{1,0:T(8,128)(2,1)S(1)} %copy-done, f32[2560,512]{1,0:T(8,128)S(1)} %bitcast.88, bf16[2560,768]{1,0:T(8,128)(2,1)S(1)} %copy-done.2, bf16[2560,768]{1,0:T(8,128)(2,1)S(1)} %copy-done.3, ...), custom_call_target="tpu_custom_call", output_to_operand_aliasing={{}: (8, {})} | custom-call | flops 2013265 | bytes 10485 | tf_op jit(solution)/shard_map/frames_gradient_1/pallas_call | solution.py:203
  190.8 3.3 %collective-permute-done.40 = bf16[208,256]{1,0:T(8,128)(2,1)S(1)} collective-permute-done((bf16[208,256]{1,0:T(8,128)(2,1)S(1)}, bf16[208,256]{1,0:T(8,128)(2,1)S(1)}, u32[]{:S(2)}, u32[]{:S(2)}) %collective-permute-start.40) | collective-permute-done | bytes 106528 | tf_op jit(solution)/shard_map/ppermute | solution.py:187
  194.2 2.3 %update_up.1 = (f32[64,2048]{1,0:T(8,128)}, f32[64,2048]{1,0:T(8,128)}, f32[64,2048]{1,0:T(8,128)}, f32[64,2048]{1,0:T(8,128)}, bf16[64,2048]{1,0:T(8,128)(2,1)}) custom-call(s32[4]{0:T(128)S(1)} %copy-done.18, bf16[256,256]{1,0:T(8,128)(2,1)S(1)} %add_convert_fusion.own_ref, bf16[256,256]{1,0:T(8,128)(2,1)S(1)} %collective-permute-done.39.other_ref, ...), custom_call_target="tpu_custom_call" | custom-call | bytes 4194 | tf_op jit(solution)/shard_map/update_up/pallas_call | solution.py:203
  196.5 2.3 %update_down.1 = (f32[256,512]{1,0:T(8,128)}, f32[256,512]{1,0:T(8,128)}, f32[256,512]{1,0:T(8,128)}, f32[256,512]{1,0:T(8,128)}, bf16[256,512]{1,0:T(8,128)(2,1)}) custom-call(s32[4]{0:T(128)S(1)} %copy-done.18, bf16[2,160,256]{2,1,0:T(8,128)(2,1)S(1)} %pad_maximum_fusion.6.own_ref.refs_0_, ...), custom_call_target="tpu_custom_call" | custom-call | bytes 4194 | tf_op jit(solution)/shard_map/update_down/pallas_call | solution.py:203
  198.9 2.7 %update_attention.1 = (f32[4,64,512]{2,1,0:T(8,128)}, f32[4,64,512]{2,1,0:T(8,128)}, f32[4,64,512]{2,1,0:T(8,128)}, f32[4,64,512]{2,1,0:T(8,128)}, bf16[4,64,512...) custom-call(s32[4]{0:T(128)S(1)} %copy-done.18, ...), custom_call_target="tpu_custom_call" | custom-call | bytes 4194 | tf_op jit(solution)/shard_map/update_attention/pallas_call | solution.py:203
  (180 shorter events, 39.8 us)
Async XLA Ops:
  2.4 9.2 %collective-permute-start = (bf16[112,256]{1,0:T(8,128)(2,1)S(1)}, bf16[112,256]{1,0:T(8,128)(2,1)S(1)}, u32[]{:S(2)}, u32[]{:S(2)}) collective-permute-start(bf16[112,256]{1,0:T(8,128)(2,1)S(1)} %fusion.11), channel_id=1, source_target_pairs={{0,2},{1,3},{2,4},{3,5},{4,6},{5,7},{6,0},{7,1},{8,10},{9,11},{10,... | collective-permute-start | bytes 172040 | tf_op jit(solution)/shard_map/ppermute | solution.py:168
  8.1 10.9 %collective-permute-start.2 = (bf16[112,256]{1,0:T(8,128)(2,1)S(1)}, bf16[112,256]{1,0:T(8,128)(2,1)S(1)}, u32[]{:S(2)}, u32[]{:S(2)}) collective-permute-start(bf16[112,256]{1,0:T(8,128)(2,1)S(1)} %fusion.11), channel_id=1, source_target_pairs={{0,6},{1,7},{2,0},{3,1},{4,2},{5,3},{6,4},{7,5},{8,14},{9,15},{10,... | collective-permute-start | bytes 172040 | tf_op jit(solution)/shard_map/ppermute | solution.py:168
  9.4 9.5 %collective-permute-start.3 = (bf16[112,256]{1,0:T(8,128)(2,1)S(1)}, bf16[112,256]{1,0:T(8,128)(2,1)S(1)}, u32[]{:S(2)}, u32[]{:S(2)}) collective-permute-start(bf16[112,256]{1,0:T(8,128)(2,1)S(1)} %fusion.11), channel_id=1, source_target_pairs={{0,1},{1,0},{2,3},{3,2},{4,5},{5,4},{6,7},{7,6},{8,9},{9,8},{10,11... | collective-permute-start | bytes 172040 | tf_op jit(solution)/shard_map/ppermute | solution.py:168
  19.3 12.2 %collective-permute-start.10 = (bf16[224,256]{1,0:T(8,128)(2,1)}, bf16[224,256]{1,0:T(8,128)(2,1)S(1)}, u32[]{:S(2)}, u32[]{:S(2)}) collective-permute-start(bf16[224,256]{1,0:T(8,128)(2,1)} %get-tuple-element.218), channel_id=1, source_target_pairs={{0,6},{1,7},{2,0},{3,1},{4,2},{5,3},{6,4},{7,5},{8,14},{9,15},{10,... | collective-permute-start | bytes 344072 | tf_op jit(solution)/shard_map/ppermute | solution.py:168
  22.2 9.3 %collective-permute-start.8 = (bf16[224,256]{1,0:T(8,128)(2,1)}, bf16[224,256]{1,0:T(8,128)(2,1)S(1)}, u32[]{:S(2)}, u32[]{:S(2)}) collective-permute-start(bf16[224,256]{1,0:T(8,128)(2,1)} %get-tuple-element.218), channel_id=1, source_target_pairs={{0,2},{1,3},{2,4},{3,5},{4,6},{5,7},{6,0},{7,1},{8,10},{9,11},{10,... | collective-permute-start | bytes 344072 | tf_op jit(solution)/shard_map/ppermute | solution.py:168
  22.2 11.8 %collective-permute-start.9 = (bf16[224,256]{1,0:T(8,128)(2,1)}, bf16[224,256]{1,0:T(8,128)(2,1)S(1)}, u32[]{:S(2)}, u32[]{:S(2)}) collective-permute-start(bf16[224,256]{1,0:T(8,128)(2,1)} %get-tuple-element.218), channel_id=1, source_target_pairs={{0,4},{1,5},{2,6},{3,7},{4,0},{5,1},{6,2},{7,3},{8,12},{9,13},{10,... | collective-permute-start | bytes 344072 | tf_op jit(solution)/shard_map/ppermute | solution.py:168
  34.1 14.8 %collective-permute-start.11 = (bf16[4,224,256]{2,1,0:T(8,128)(2,1)S(1)}, bf16[4,224,256]{2,1,0:T(8,128)(2,1)S(1)}, u32[]{:S(2)}, u32[]{:S(2)}) collective-permute-start(bf16[4,224,256]{2,1,0:T(8,128)(2,1)S(1)} %pad_maximum_fusion.3), channel_id=1, source_target_pairs={{0,1},{1,0},{2,3},{3,2},{4,5},{5,4},{6,7},{7,6},{8,9},{9,8},{10,11... | collective-permute-start | bytes 1376264 | tf_op jit(solution)/shard_map/ppermute | solution.py:168
  34.9 12.4 %collective-permute-start.12 = (bf16[320,256]{1,0:T(8,128)(2,1)S(1)}, bf16[320,256]{1,0:T(8,128)(2,1)S(1)}, u32[]{:S(2)}, u32[]{:S(2)}) collective-permute-start(bf16[320,256]{1,0:T(8,128)(2,1)S(1)} %copy-done.25), channel_id=1, source_target_pairs={{0,2},{1,3},{2,4},{3,5},{4,6},{5,7},{6,0},{7,1},{8,10},{9,11},{10,... | collective-permute-start | bytes 491528 | tf_op jit(solution)/shard_map/ppermute | solution.py:168
  36.4 12.6 %collective-permute-start.13 = (bf16[320,256]{1,0:T(8,128)(2,1)S(1)}, bf16[320,256]{1,0:T(8,128)(2,1)S(1)}, u32[]{:S(2)}, u32[]{:S(2)}) collective-permute-start(bf16[320,256]{1,0:T(8,128)(2,1)S(1)} %copy-done.25), channel_id=1, source_target_pairs={{0,4},{1,5},{2,6},{3,7},{4,0},{5,1},{6,2},{7,3},{8,12},{9,13},{10,... | collective-permute-start | bytes 491528 | tf_op jit(solution)/shard_map/ppermute | solution.py:168
  37.9 11.0 %collective-permute-start.14 = (bf16[320,256]{1,0:T(8,128)(2,1)S(1)}, bf16[320,256]{1,0:T(8,128)(2,1)S(1)}, u32[]{:S(2)}, u32[]{:S(2)}) collective-permute-start(bf16[320,256]{1,0:T(8,128)(2,1)S(1)} %copy-done.25), channel_id=1, source_target_pairs={{0,6},{1,7},{2,0},{3,1},{4,2},{5,3},{6,4},{7,5},{8,14},{9,15},{10,... | collective-permute-start | bytes 491528 | tf_op jit(solution)/shard_map/ppermute | solution.py:168
  49.0 17.4 %collective-permute-start.16 = (bf16[4,320,256]{2,1,0:T(8,128)(2,1)S(1)}, bf16[4,320,256]{2,1,0:T(8,128)(2,1)S(1)}, u32[]{:S(2)}, u32[]{:S(2)}) collective-permute-start(bf16[4,320,256]{2,1,0:T(8,128)(2,1)S(1)} %pad_maximum_fusion.1.rest_0_), channel_id=1, source_target_pairs={{0,1},{1,0},{2,3},{3,2},{4,5},{5,4},{6,7},{7,6},{8,9},{9,8},{10,11... | collective-permute-start | bytes 1966088 | tf_op jit(solution)/shard_map/ppermute | solution.py:168
  50.8 15.6 %collective-permute-start.18 = (bf16[4,320,256]{2,1,0:T(8,128)(2,1)S(1)}, bf16[4,320,256]{2,1,0:T(8,128)(2,1)S(1)}, u32[]{:S(2)}, u32[]{:S(2)}) collective-permute-start(bf16[4,320,256]{2,1,0:T(8,128)(2,1)S(1)} %pad_maximum_fusion.1.rest_0_), channel_id=1, source_target_pairs={{0,8},{8,0},{16,24},{24,16},{1,9},{9,1},{17,25},{25,17},{2,10},{10... | collective-permute-start | bytes 1966088 | tf_op jit(solution)/shard_map/ppermute | solution.py:182
  50.9 15.5 %collective-permute-start.17 = (bf16[2,4,128,256]{3,2,1,0:T(8,128)(2,1)S(1)}, bf16[2,4,128,256]{3,2,1,0:T(8,128)(2,1)S(1)}, u32[]{:S(2)}, u32[]{:S(2)}) collective-permute-start(bf16[2,4,128,256]{3,2,1,0:T(8,128)(2,1)S(1)} %pad_maximum_fusion.2.rest_4_), channel_id=1, source_target_pairs={{0,16},{8,24},{16,0},{24,8},{1,17},{9,25},{17,1},{25,9},{2,18},{10... | collective-permute-start | bytes 1572872 | tf_op jit(solution)/shard_map/ppermute | solution.py:179
  52.5 13.9 %collective-permute-start.19 = (bf16[2,4,128,256]{3,2,1,0:T(8,128)(2,1)S(1)}, bf16[2,4,128,256]{3,2,1,0:T(8,128)(2,1)S(1)}, u32[]{:S(2)}, u32[]{:S(2)}) collective-permute-start(bf16[2,4,128,256]{3,2,1,0:T(8,128)(2,1)S(1)} %pad_maximum_fusion.2.rest_4_), channel_id=1, source_target_pairs={{0,8},{8,0},{16,24},{24,16},{1,9},{9,1},{17,25},{25,17},{2,10},{10... | collective-permute-start | bytes 1572872 | tf_op jit(solution)/shard_map/ppermute | solution.py:182
  120.6 19.0 %collective-permute-start.25 = (bf16[8,160,256]{2,1,0:T(8,128)(2,1)S(1)}, bf16[8,160,256]{2,1,0:T(8,128)(2,1)S(1)}, u32[]{:S(2)}, u32[]{:S(2)}) collective-permute-start(bf16[8,160,256]{2,1,0:T(8,128)(2,1)S(1)} %fusion), channel_id=1, source_target_pairs={{0,16},{8,24},{16,0},{24,8},{1,17},{9,25},{17,1},{25,9},{2,18},{10... | collective-permute-start | bytes 1966088 | tf_op jit(solution)/shard_map/ppermute | solution.py:179
  122.0 17.6 %collective-permute-start.24 = (bf16[4,256,256]{2,1,0:T(8,128)(2,1)S(1)}, bf16[4,256,256]{2,1,0:T(8,128)(2,1)S(1)}, u32[]{:S(2)}, u32[]{:S(2)}) collective-permute-start(bf16[4,256,256]{2,1,0:T(8,128)(2,1)S(1)} %slice.184), channel_id=1, source_target_pairs={{0,1},{1,0},{2,3},{3,2},{4,5},{5,4},{6,7},{7,6},{8,9},{9,8},{10,11... | collective-permute-start | bytes 1572872 | tf_op jit(solution)/shard_map/ppermute | solution.py:168
  139.3 20.2 %collective-permute-start.26 = (bf16[8,96,256]{2,1,0:T(8,128)(2,1)S(1)}, bf16[8,96,256]{2,1,0:T(8,128)(2,1)S(1)}, u32[]{:S(2)}, u32[]{:S(2)}) collective-permute-start(bf16[8,96,256]{2,1,0:T(8,128)(2,1)S(1)} %get-tuple-element.266), channel_id=1, source_target_pairs={{0,8},{8,0},{16,24},{24,16},{1,9},{9,1},{17,25},{25,17},{2,10},{10... | collective-permute-start | bytes 1179656 | tf_op jit(solution)/shard_map/ppermute | solution.py:182
  139.8 19.8 %collective-permute-start.28 = (bf16[4,160,256]{2,1,0:T(8,128)(2,1)S(1)}, bf16[4,160,256]{2,1,0:T(8,128)(2,1)S(1)}, u32[]{:S(2)}, u32[]{:S(2)}) collective-permute-start(bf16[4,160,256]{2,1,0:T(8,128)(2,1)S(1)} %slice.186), channel_id=1, source_target_pairs={{0,1},{1,0},{2,3},{3,2},{4,5},{5,4},{6,7},{7,6},{8,9},{9,8},{10,11... | collective-permute-start | bytes 983048 | tf_op jit(solution)/shard_map/ppermute | solution.py:168
  140.4 19.1 %collective-permute-start.27 = (bf16[2,256,256]{2,1,0:T(8,128)(2,1)S(1)}, bf16[2,256,256]{2,1,0:T(8,128)(2,1)S(1)}, u32[]{:S(2)}, u32[]{:S(2)}) collective-permute-start(bf16[2,256,256]{2,1,0:T(8,128)(2,1)S(1)} %slice.187), channel_id=1, source_target_pairs={{0,4},{1,5},{2,6},{3,7},{4,0},{5,1},{6,2},{7,3},{8,12},{9,13},{10,... | collective-permute-start | bytes 786440 | tf_op jit(solution)/shard_map/ppermute | solution.py:156
  161.9 12.7 %collective-permute-start.32 = (bf16[160,256]{1,0:T(8,128)(2,1)S(1)}, bf16[160,256]{1,0:T(8,128)(2,1)S(1)}, u32[]{:S(2)}, u32[]{:S(2)}) collective-permute-start(bf16[160,256]{1,0:T(8,128)(2,1)S(1)} %get-tuple-element.347), channel_id=1, source_target_pairs={{0,2},{1,3},{2,4},{3,5},{4,6},{5,7},{6,0},{7,1},{8,10},{9,11},{10,... | collective-permute-start | bytes 245768 | tf_op jit(solution)/shard_map/ppermute | solution.py:168
  163.3 11.2 %collective-permute-start.33 = (bf16[160,256]{1,0:T(8,128)(2,1)S(1)}, bf16[160,256]{1,0:T(8,128)(2,1)S(1)}, u32[]{:S(2)}, u32[]{:S(2)}) collective-permute-start(bf16[160,256]{1,0:T(8,128)(2,1)S(1)} %get-tuple-element.346), channel_id=1, source_target_pairs={{0,4},{1,5},{2,6},{3,7},{4,0},{5,1},{6,2},{7,3},{8,12},{9,13},{10,... | collective-permute-start | bytes 245768 | tf_op jit(solution)/shard_map/ppermute | solution.py:168
  165.9 11.5 %collective-permute-start.31 = (bf16[4,208,256]{2,1,0:T(8,128)(2,1)S(1)}, bf16[4,208,256]{2,1,0:T(8,128)(2,1)S(1)}, u32[]{:S(2)}, u32[]{:S(2)}) collective-permute-start(bf16[4,208,256]{2,1,0:T(8,128)(2,1)S(1)} %slice.185), channel_id=1, source_target_pairs={{0,1},{1,0},{2,3},{3,2},{4,5},{5,4},{6,7},{7,6},{8,9},{9,8},{10,11... | collective-permute-start | bytes 1277960 | tf_op jit(solution)/shard_map/ppermute | solution.py:168
  177.5 11.3 %collective-permute-start.35 = (bf16[416,256]{1,0:T(8,128)(2,1)S(1)}, bf16[416,256]{1,0:T(8,128)(2,1)S(1)}, u32[]{:S(2)}, u32[]{:S(2)}) collective-permute-start(bf16[416,256]{1,0:T(8,128)(2,1)S(1)} %pad_maximum_fusion.5), channel_id=1, source_target_pairs={{0,16},{8,24},{16,0},{24,8},{1,17},{9,25},{17,1},{25,9},{2,18},{10... | collective-permute-start | bytes 638984 | tf_op jit(solution)/shard_map/ppermute | solution.py:179
  178.8 10.2 %collective-permute-start.36 = (bf16[208,256]{1,0:T(8,128)(2,1)S(1)}, bf16[208,256]{1,0:T(8,128)(2,1)S(1)}, u32[]{:S(2)}, u32[]{:S(2)}) collective-permute-start(bf16[208,256]{1,0:T(8,128)(2,1)S(1)} %get-tuple-element.344), channel_id=1, source_target_pairs={{0,2},{1,3},{2,4},{3,5},{4,6},{5,7},{6,0},{7,1},{8,10},{9,11},{10,... | collective-permute-start | bytes 319496 | tf_op jit(solution)/shard_map/ppermute | solution.py:168
  (48 other events, 438.8 us)

commit v4 on v3

--- a/solution.py
+++ b/solution.py
@@ -309,8 +309,9 @@
 
         @pl.when(pl.program_id(0) == 0)
         def _():
-            ks[...] = jnp.zeros_like(ks)
-            vs[...] = jnp.zeros_like(vs)
+            rest_rows = MROWS + QROWS + LWIN
+            for dest in (ks, vs):
+                dest[:, rest_rows:, :] = jnp.zeros((groups, KPAD - rest_rows, HALF), BF16)
             lower = me_ref[2] == 0
             if first and fresh:
                 norm_ref[...] = jnp.zeros_like(norm_ref)
@@ -591,8 +592,9 @@
 
         @pl.when(i == 0)
         def _():
-            ks[...] = jnp.zeros_like(ks)
-            vs[...] = jnp.zeros_like(vs)
+            rest_rows = MROWS + QROWS + LWIN
+            for dest in (ks, vs):
+                dest[:, rest_rows:, :] = jnp.zeros((groups, KPAD - rest_rows, HALF), BF16)
             acc[...] = jnp.zeros_like(acc)
             accm[...] = jnp.zeros_like(accm)
             sums[...] = jnp.zeros_like(sums)

time: 202 us -> 202 us (level)
  no operation moved by 1% of the time
where the time goes in v4:
time: 202 us
  Pallas kernels  127 us (63%)
  starting transfers between devices  46.7 us (23%)
  waiting for transfers between devices  19.9 us (10%)
  local copies, waits for them, and re-layouts  3.15 us (2%)
  other arithmetic  3.09 us (2%)
    pallas_call x12, Pallas kernels, call(): pl.pallas_call(kernel, grid_spec=pltpu.PrefetchScalarGridSpec(num_scalar_...  127 us
    ppermute x24, starting transfers between devices, shift(): return lax.ppermute(value, 'fsdp', perm)  34.5 us
    ppermute x13, waiting for transfers between devices, other_core(): return lax.ppermute(value, 'dp', [(d, d ^ 1) for d in range(self.dp)])  8.67 us
    ppermute x24, waiting for transfers between devices, shift(): return lax.ppermute(value, 'fsdp', perm)  7.69 us
    ppermute x2, starting transfers between devices, swap_z(): lax.ppermute(value, 'fsdp', [(f, (f // X ^ step) * X + f % X) for f in ra...  5.15 us
  transfers between devices with their start and end apart: 43, of which 12 were waited for; matrix products, arithmetic and copies ran while one was open for 1% of the time, Pallas kernels for 38%

profile of v4, /device:TPU:0, one launch (start us, length us, event | category | flops | bytes accessed | tf_op | source)
XLA Modules:
  0.0 201.5 jit_solution(4663136495146863996)
XLA Ops:
  2.4 3.1 %collective-permute-start = (bf16[112,256]{1,0:T(8,128)(2,1)S(1)}, bf16[112,256]{1,0:T(8,128)(2,1)S(1)}, u32[]{:S(2)}, u32[]{:S(2)}) collective-permute-start(bf16[112,256]{1,0:T(8,128)(2,1)S(1)} %fusion.11), channel_id=1, source_target_pairs={{0,2},{1,3},{2,4},{3,5},{4,6},{5,7},{6,0},{7,1},{8,10},{9,11},{10,... | collective-permute-start | bytes 172040 | tf_op jit(solution)/shard_map/ppermute | solution.py:168
  5.5 2.6 %collective-permute-start.1 = (bf16[112,256]{1,0:T(8,128)(2,1)S(1)}, bf16[112,256]{1,0:T(8,128)(2,1)S(1)}, u32[]{:S(2)}, u32[]{:S(2)}) collective-permute-start(bf16[112,256]{1,0:T(8,128)(2,1)S(1)} %fusion.11), channel_id=1, source_target_pairs={{0,4},{1,5},{2,6},{3,7},{4,0},{5,1},{6,2},{7,3},{8,12},{9,13},{10,... | collective-permute-start | bytes 172040 | tf_op jit(solution)/shard_map/ppermute | solution.py:168
  12.8 2.9 %collective-permute-start.6 = (bf16[112,256]{1,0:T(8,128)(2,1)S(1)}, bf16[112,256]{1,0:T(8,128)(2,1)S(1)}, u32[]{:S(2)}, u32[]{:S(2)}) collective-permute-start(bf16[112,256]{1,0:T(8,128)(2,1)S(1)} %fusion.11), channel_id=1, source_target_pairs={{0,7},{1,6},{2,1},{3,0},{4,3},{5,2},{6,5},{7,4},{8,15},{9,14},{10,... | collective-permute-start | bytes 172040 | tf_op jit(solution)/shard_map/ppermute | solution.py:168
  16.4 2.6 %pack_rest.1 = (bf16[224,256]{1,0:T(8,128)(2,1)}, bf16[320,256]{1,0:T(8,128)(2,1)}) custom-call(s32[4]{0:T(128)} %pad_add_fusion.me_ref, f32[4,64,512]{2,1,0:T(8,128)} %refs_4_.1, f32[4,64,512]{2,1,0:T(8,128)} %refs_4_.1, f32[64,2048]{1,0:T(8,128)} %w.2, f32[256,512]{1,0:T(8,128)} %w.3), custom_call_target="tpu_custom_call" | custom-call | bytes 1572 | tf_op jit(solution)/shard_map/pack_rest/pallas_call | solution.py:203
  19.3 3.0 %collective-permute-start.10 = (bf16[224,256]{1,0:T(8,128)(2,1)}, bf16[224,256]{1,0:T(8,128)(2,1)S(1)}, u32[]{:S(2)}, u32[]{:S(2)}) collective-permute-start(bf16[224,256]{1,0:T(8,128)(2,1)} %get-tuple-element.218), channel_id=1, source_target_pairs={{0,6},{1,7},{2,0},{3,1},{4,2},{5,3},{6,4},{7,5},{8,14},{9,15},{10,... | collective-permute-start | bytes 344072 | tf_op jit(solution)/shard_map/ppermute | solution.py:168
  23.2 8.2 %attention_forward_0_0.1 = (bf16[2560,768]{1,0:T(8,128)(2,1)}, bf16[512,512]{1,0:T(8,128)(2,1)S(1)}, bf16[2560,256]{1,0:T(8,128)(2,1)S(1)}, bf16[2,5120,256]{2,1...) custom-call(s32[4]{0:T(128)S(1)} %copy-done.18, ...), custom_call_target="tpu_custom_call" | custom-call | flops 4026531 | bytes 8519 | tf_op jit(solution)/shard_map/attention_forward_0_0/pallas_call | solution.py:203
  31.5 2.6 %collective-permute-done.9 = bf16[224,256]{1,0:T(8,128)(2,1)S(1)} collective-permute-done((bf16[224,256]{1,0:T(8,128)(2,1)}, bf16[224,256]{1,0:T(8,128)(2,1)S(1)}, u32[]{:S(2)}, u32[]{:S(2)}) %collective-permute-start.9) | collective-permute-done | bytes 114720 | tf_op jit(solution)/shard_map/ppermute | solution.py:168
  38.7 8.3 %attention_forward_0_1.1 = (bf16[2560,768]{1,0:T(8,128)(2,1)}, bf16[512,512]{1,0:T(8,128)(2,1)S(1)}, bf16[2560,256]{1,0:T(8,128)(2,1)S(1)}, bf16[2,5120,256]{2,1...) custom-call(s32[4]{0:T(128)S(1)} %copy-done.18, ...), custom_call_target="tpu_custom_call", output_to_operand_aliasing={{0}: (9, {}), {1}: (10, {}), {2}: (11, {}), {3}: (12, {}), ... | custom-call | flops 4026531 | bytes 8519 | tf_op jit(solution)/shard_map/attention_forward_0_1/pallas_call | solution.py:203
  55.0 10.5 %attention_forward_1_0.1 = (bf16[2560,768]{1,0:T(8,128)(2,1)}, bf16[512,512]{1,0:T(8,128)(2,1)S(1)}, bf16[2560,256]{1,0:T(8,128)(2,1)S(1)}, bf16[2,5120,256]{2,1,0:T(8,128)(2,1)}, bf16[512,768]{1,0:T(8,128)(2,1)S(1)}) custom-call(s32[4]{0:T(128)S(1)} %copy-done.18, bf16[2560,512]{1,0:T(8,128)(2,1)} %get-tuple-element.224.x_ref, ...), custom_call_target="tpu_custom_call" | custom-call | flops 8053063 | bytes 17039 | tf_op jit(solution)/shard_map/attention_forward_1_0/pallas_call | solution.py:203
  66.9 2.3 %collective-permute-done.21.rest_7_ = bf16[2,4,128,256]{3,2,1,0:T(8,128)(2,1)S(1)} collective-permute-done((bf16[2,4,128,256]{3,2,1,0:T(8,128)(2,1)S(1)}, bf16[2,4,128,256]{3,2,1,0:T(8,128)(2,1)S(1)}, u32[]{:S(2)}, u32[]{:S(2)}) %collective-permute-start.21) | collective-permute-done | bytes 524320 | tf_op jit(solution)/shard_map/ppermute | solution.py:182
  69.3 47.7 %feed_forward.1 = (bf16[2560,512]{1,0:T(8,128)(2,1)}, f32[2560,512]{1,0:T(8,128)}, bf16[2560,512]{1,0:T(8,128)(2,1)}, f32[8,512]{1,0:T(8,128)S(1)}, bf16[8,256,2...) custom-call(s32[4]{0:T(128)S(1)} %copy-done.18, ...), custom_call_target="tpu_custom_call" | custom-call | flops 72477576 | bytes 20971 | tf_op jit(solution)/shard_map/feed_forward/pallas_call | solution.py:203
  117.5 2.5 %collective-permute-done.23 = bf16[2,8,160,256]{3,2,1,0:T(8,128)(2,1)S(1)} collective-permute-done((bf16[2,8,160,256]{3,2,1,0:T(8,128)(2,1)S(1)}, bf16[2,8,160,256]{3,2,1,0:T(8,128)(2,1)S(1)}, u32[]{:S(2)}, u32[]{:S(2)}) %collective-permute-start.23) | collective-permute-done | bytes 1310752 | tf_op jit(solution)/shard_map/ppermute | solution.py:182
  123.3 15.8 %attention_backward_0.1 = (bf16[2560,768]{1,0:T(8,128)(2,1)}, bf16[8,96,256]{2,1,0:T(8,128)(2,1)S(1)}, bf16[8,96,256]{2,1,0:T(8,128)(2,1)S(1)}, f32[8,512]{1,0:T(8,128)S(1)}) custom-call(s32[4]{0:T(128)S(1)} %copy-done.18, bf16[512,2560]{1,0:T(8,128)(2,1)S(1)} %copy-done.1, bf16[512,512]{1,0:T(8,128)(2,1)S(1)} %get-tuple-element.249.mem_ref, ...), custom_call_target="tpu_custom_call" | custom-call | flops 16106127 | bytes 22282 | tf_op jit(solution)/shard_map/attention_backward_0/pallas_call | solution.py:203
  140.2 3.1 %collective-permute-start.27 = (bf16[2,256,256]{2,1,0:T(8,128)(2,1)S(1)}, bf16[2,256,256]{2,1,0:T(8,128)(2,1)S(1)}, u32[]{:S(2)}, u32[]{:S(2)}) collective-permute-start(bf16[2,256,256]{2,1,0:T(8,128)(2,1)S(1)} %slice.187), channel_id=1, source_target_pairs={{0,4},{1,5},{2,6},{3,7},{4,0},{5,1},{6,2},{7,3},{8,12},{9,13},{10,... | collective-permute-start | bytes 786440 | tf_op jit(solution)/shard_map/ppermute | solution.py:156
  143.3 15.9 %attention_backward_1.1 = (bf16[2560,768]{1,0:T(8,128)(2,1)}, bf16[8,112,256]{2,1,0:T(8,128)(2,1)S(1)}, bf16[8,112,256]{2,1,0:T(8,128)(2,1)S(1)}, f32[8,512]{1,0:T(8,128)}) custom-call(s32[4]{0:T(128)S(1)} %copy-done.18, bf16[512,2560]{1,0:T(8,128)(2,1)S(1)} %copy-done.1, bf16[512,512]{1,0:T(8,128)(2,1)S(1)} %get-tuple-element.249.mem_ref, ...), custom_call_target="tpu_custom_call" | custom-call | flops 16106127 | bytes 22282 | tf_op jit(solution)/shard_map/attention_backward_1/pallas_call | solution.py:203
  163.0 2.4 %collective-permute-start.33 = (bf16[160,256]{1,0:T(8,128)(2,1)S(1)}, bf16[160,256]{1,0:T(8,128)(2,1)S(1)}, u32[]{:S(2)}, u32[]{:S(2)}) collective-permute-start(bf16[160,256]{1,0:T(8,128)(2,1)S(1)} %get-tuple-element.346), channel_id=1, source_target_pairs={{0,4},{1,5},{2,6},{3,7},{4,0},{5,1},{6,2},{7,3},{8,12},{9,13},{10,... | collective-permute-start | bytes 245768 | tf_op jit(solution)/shard_map/ppermute | solution.py:168
  169.0 5.2 %frames_gradient_0.1.rest_0_ = f32[2560,512]{1,0:T(8,128)} custom-call(s32[4]{0:T(128)S(1)} %copy-done.18, bf16[2560,512]{1,0:T(8,128)(2,1)S(1)} %copy-done, f32[2560,512]{1,0:T(8,128)S(1)} %bitcast.88, bf16[2560,768]{1,0:T(8,128)(2,1)S(1)} %copy-done.2, bf16[2560,768]{1,0:T(8,128)(2,1)S(1)} %copy-done.3, ...), custom_call_target="tpu_custom_call" | custom-call | flops 2013265 | bytes 10485 | tf_op jit(solution)/shard_map/frames_gradient_0/pallas_call | solution.py:203
  174.4 2.7 %collective-permute-done.31 = bf16[4,208,256]{2,1,0:T(8,128)(2,1)S(1)} collective-permute-done((bf16[4,208,256]{2,1,0:T(8,128)(2,1)S(1)}, bf16[4,208,256]{2,1,0:T(8,128)(2,1)S(1)}, u32[]{:S(2)}, u32[]{:S(2)}) %collective-permute-start.31) | collective-permute-done | bytes 426016 | tf_op jit(solution)/shard_map/ppermute | solution.py:168
  180.8 2.2 %collective-permute-start.38 = (bf16[208,256]{1,0:T(8,128)(2,1)S(1)}, bf16[208,256]{1,0:T(8,128)(2,1)S(1)}, u32[]{:S(2)}, u32[]{:S(2)}) collective-permute-start(bf16[208,256]{1,0:T(8,128)(2,1)S(1)} %get-tuple-element.342), channel_id=1, source_target_pairs={{0,6},{1,7},{2,0},{3,1},{4,2},{5,3},{6,4},{7,5},{8,14},{9,15},{10,... | collective-permute-start | bytes 319496 | tf_op jit(solution)/shard_map/ppermute | solution.py:168
  183.0 5.4 %frames_gradient_1.1 = f32[2560,512]{1,0:T(8,128)} custom-call(s32[4]{0:T(128)S(1)} %copy-done.18, bf16[2560,512]{1,0:T(8,128)(2,1)S(1)} %copy-done, f32[2560,512]{1,0:T(8,128)S(1)} %bitcast.88, bf16[2560,768]{1,0:T(8,128)(2,1)S(1)} %copy-done.2, bf16[2560,768]{1,0:T(8,128)(2,1)S(1)} %copy-done.3, ...), custom_call_target="tpu_custom_call", output_to_operand_aliasing={{}: (8, {})} | custom-call | flops 2013265 | bytes 10485 | tf_op jit(solution)/shard_map/frames_gradient_1/pallas_call | solution.py:203
  190.5 3.3 %collective-permute-done.40 = bf16[208,256]{1,0:T(8,128)(2,1)S(1)} collective-permute-done((bf16[208,256]{1,0:T(8,128)(2,1)S(1)}, bf16[208,256]{1,0:T(8,128)(2,1)S(1)}, u32[]{:S(2)}, u32[]{:S(2)}) %collective-permute-start.40) | collective-permute-done | bytes 106528 | tf_op jit(solution)/shard_map/ppermute | solution.py:187
  193.8 2.3 %update_up.1 = (f32[64,2048]{1,0:T(8,128)}, f32[64,2048]{1,0:T(8,128)}, f32[64,2048]{1,0:T(8,128)}, f32[64,2048]{1,0:T(8,128)}, bf16[64,2048]{1,0:T(8,128)(2,1)}) custom-call(s32[4]{0:T(128)S(1)} %copy-done.18, bf16[256,256]{1,0:T(8,128)(2,1)S(1)} %add_convert_fusion.own_ref, bf16[256,256]{1,0:T(8,128)(2,1)S(1)} %collective-permute-done.39.other_ref, ...), custom_call_target="tpu_custom_call" | custom-call | bytes 4194 | tf_op jit(solution)/shard_map/update_up/pallas_call | solution.py:203
  196.2 2.3 %update_down.1 = (f32[256,512]{1,0:T(8,128)}, f32[256,512]{1,0:T(8,128)}, f32[256,512]{1,0:T(8,128)}, f32[256,512]{1,0:T(8,128)}, bf16[256,512]{1,0:T(8,128)(2,1)}) custom-call(s32[4]{0:T(128)S(1)} %copy-done.18, bf16[2,160,256]{2,1,0:T(8,128)(2,1)S(1)} %pad_maximum_fusion.6.own_ref.refs_0_, ...), custom_call_target="tpu_custom_call" | custom-call | bytes 4194 | tf_op jit(solution)/shard_map/update_down/pallas_call | solution.py:203
  198.6 2.7 %update_attention.1 = (f32[4,64,512]{2,1,0:T(8,128)}, f32[4,64,512]{2,1,0:T(8,128)}, f32[4,64,512]{2,1,0:T(8,128)}, f32[4,64,512]{2,1,0:T(8,128)}, bf16[4,64,512...) custom-call(s32[4]{0:T(128)S(1)} %copy-done.18, ...), custom_call_target="tpu_custom_call" | custom-call | bytes 4194 | tf_op jit(solution)/shard_map/update_attention/pallas_call | solution.py:203
  (180 shorter events, 40.1 us)
Async XLA Ops:
  2.4 9.2 %collective-permute-start = (bf16[112,256]{1,0:T(8,128)(2,1)S(1)}, bf16[112,256]{1,0:T(8,128)(2,1)S(1)}, u32[]{:S(2)}, u32[]{:S(2)}) collective-permute-start(bf16[112,256]{1,0:T(8,128)(2,1)S(1)} %fusion.11), channel_id=1, source_target_pairs={{0,2},{1,3},{2,4},{3,5},{4,6},{5,7},{6,0},{7,1},{8,10},{9,11},{10,... | collective-permute-start | bytes 172040 | tf_op jit(solution)/shard_map/ppermute | solution.py:168
  8.1 10.9 %collective-permute-start.2 = (bf16[112,256]{1,0:T(8,128)(2,1)S(1)}, bf16[112,256]{1,0:T(8,128)(2,1)S(1)}, u32[]{:S(2)}, u32[]{:S(2)}) collective-permute-start(bf16[112,256]{1,0:T(8,128)(2,1)S(1)} %fusion.11), channel_id=1, source_target_pairs={{0,6},{1,7},{2,0},{3,1},{4,2},{5,3},{6,4},{7,5},{8,14},{9,15},{10,... | collective-permute-start | bytes 172040 | tf_op jit(solution)/shard_map/ppermute | solution.py:168
  9.4 9.5 %collective-permute-start.3 = (bf16[112,256]{1,0:T(8,128)(2,1)S(1)}, bf16[112,256]{1,0:T(8,128)(2,1)S(1)}, u32[]{:S(2)}, u32[]{:S(2)}) collective-permute-start(bf16[112,256]{1,0:T(8,128)(2,1)S(1)} %fusion.11), channel_id=1, source_target_pairs={{0,1},{1,0},{2,3},{3,2},{4,5},{5,4},{6,7},{7,6},{8,9},{9,8},{10,11... | collective-permute-start | bytes 172040 | tf_op jit(solution)/shard_map/ppermute | solution.py:168
  19.3 12.2 %collective-permute-start.10 = (bf16[224,256]{1,0:T(8,128)(2,1)}, bf16[224,256]{1,0:T(8,128)(2,1)S(1)}, u32[]{:S(2)}, u32[]{:S(2)}) collective-permute-start(bf16[224,256]{1,0:T(8,128)(2,1)} %get-tuple-element.218), channel_id=1, source_target_pairs={{0,6},{1,7},{2,0},{3,1},{4,2},{5,3},{6,4},{7,5},{8,14},{9,15},{10,... | collective-permute-start | bytes 344072 | tf_op jit(solution)/shard_map/ppermute | solution.py:168
  22.2 9.2 %collective-permute-start.8 = (bf16[224,256]{1,0:T(8,128)(2,1)}, bf16[224,256]{1,0:T(8,128)(2,1)S(1)}, u32[]{:S(2)}, u32[]{:S(2)}) collective-permute-start(bf16[224,256]{1,0:T(8,128)(2,1)} %get-tuple-element.218), channel_id=1, source_target_pairs={{0,2},{1,3},{2,4},{3,5},{4,6},{5,7},{6,0},{7,1},{8,10},{9,11},{10,... | collective-permute-start | bytes 344072 | tf_op jit(solution)/shard_map/ppermute | solution.py:168
  22.2 11.8 %collective-permute-start.9 = (bf16[224,256]{1,0:T(8,128)(2,1)}, bf16[224,256]{1,0:T(8,128)(2,1)S(1)}, u32[]{:S(2)}, u32[]{:S(2)}) collective-permute-start(bf16[224,256]{1,0:T(8,128)(2,1)} %get-tuple-element.218), channel_id=1, source_target_pairs={{0,4},{1,5},{2,6},{3,7},{4,0},{5,1},{6,2},{7,3},{8,12},{9,13},{10,... | collective-permute-start | bytes 344072 | tf_op jit(solution)/shard_map/ppermute | solution.py:168
  34.1 14.8 %collective-permute-start.11 = (bf16[4,224,256]{2,1,0:T(8,128)(2,1)S(1)}, bf16[4,224,256]{2,1,0:T(8,128)(2,1)S(1)}, u32[]{:S(2)}, u32[]{:S(2)}) collective-permute-start(bf16[4,224,256]{2,1,0:T(8,128)(2,1)S(1)} %pad_maximum_fusion.3), channel_id=1, source_target_pairs={{0,1},{1,0},{2,3},{3,2},{4,5},{5,4},{6,7},{7,6},{8,9},{9,8},{10,11... | collective-permute-start | bytes 1376264 | tf_op jit(solution)/shard_map/ppermute | solution.py:168
  34.9 12.2 %collective-permute-start.12 = (bf16[320,256]{1,0:T(8,128)(2,1)S(1)}, bf16[320,256]{1,0:T(8,128)(2,1)S(1)}, u32[]{:S(2)}, u32[]{:S(2)}) collective-permute-start(bf16[320,256]{1,0:T(8,128)(2,1)S(1)} %copy-done.25), channel_id=1, source_target_pairs={{0,2},{1,3},{2,4},{3,5},{4,6},{5,7},{6,0},{7,1},{8,10},{9,11},{10,... | collective-permute-start | bytes 491528 | tf_op jit(solution)/shard_map/ppermute | solution.py:168
  36.3 12.6 %collective-permute-start.13 = (bf16[320,256]{1,0:T(8,128)(2,1)S(1)}, bf16[320,256]{1,0:T(8,128)(2,1)S(1)}, u32[]{:S(2)}, u32[]{:S(2)}) collective-permute-start(bf16[320,256]{1,0:T(8,128)(2,1)S(1)} %copy-done.25), channel_id=1, source_target_pairs={{0,4},{1,5},{2,6},{3,7},{4,0},{5,1},{6,2},{7,3},{8,12},{9,13},{10,... | collective-permute-start | bytes 491528 | tf_op jit(solution)/shard_map/ppermute | solution.py:168
  37.9 11.0 %collective-permute-start.14 = (bf16[320,256]{1,0:T(8,128)(2,1)S(1)}, bf16[320,256]{1,0:T(8,128)(2,1)S(1)}, u32[]{:S(2)}, u32[]{:S(2)}) collective-permute-start(bf16[320,256]{1,0:T(8,128)(2,1)S(1)} %copy-done.25), channel_id=1, source_target_pairs={{0,6},{1,7},{2,0},{3,1},{4,2},{5,3},{6,4},{7,5},{8,14},{9,15},{10,... | collective-permute-start | bytes 491528 | tf_op jit(solution)/shard_map/ppermute | solution.py:168
  49.0 17.3 %collective-permute-start.16 = (bf16[4,320,256]{2,1,0:T(8,128)(2,1)S(1)}, bf16[4,320,256]{2,1,0:T(8,128)(2,1)S(1)}, u32[]{:S(2)}, u32[]{:S(2)}) collective-permute-start(bf16[4,320,256]{2,1,0:T(8,128)(2,1)S(1)} %pad_maximum_fusion.1.rest_0_), channel_id=1, source_target_pairs={{0,1},{1,0},{2,3},{3,2},{4,5},{5,4},{6,7},{7,6},{8,9},{9,8},{10,11... | collective-permute-start | bytes 1966088 | tf_op jit(solution)/shard_map/ppermute | solution.py:168
  50.8 15.5 %collective-permute-start.18 = (bf16[4,320,256]{2,1,0:T(8,128)(2,1)S(1)}, bf16[4,320,256]{2,1,0:T(8,128)(2,1)S(1)}, u32[]{:S(2)}, u32[]{:S(2)}) collective-permute-start(bf16[4,320,256]{2,1,0:T(8,128)(2,1)S(1)} %pad_maximum_fusion.1.rest_0_), channel_id=1, source_target_pairs={{0,8},{8,0},{16,24},{24,16},{1,9},{9,1},{17,25},{25,17},{2,10},{10... | collective-permute-start | bytes 1966088 | tf_op jit(solution)/shard_map/ppermute | solution.py:182
  50.9 15.4 %collective-permute-start.17 = (bf16[2,4,128,256]{3,2,1,0:T(8,128)(2,1)S(1)}, bf16[2,4,128,256]{3,2,1,0:T(8,128)(2,1)S(1)}, u32[]{:S(2)}, u32[]{:S(2)}) collective-permute-start(bf16[2,4,128,256]{3,2,1,0:T(8,128)(2,1)S(1)} %pad_maximum_fusion.2.rest_4_), channel_id=1, source_target_pairs={{0,16},{8,24},{16,0},{24,8},{1,17},{9,25},{17,1},{25,9},{2,18},{10... | collective-permute-start | bytes 1572872 | tf_op jit(solution)/shard_map/ppermute | solution.py:179
  52.5 13.8 %collective-permute-start.19 = (bf16[2,4,128,256]{3,2,1,0:T(8,128)(2,1)S(1)}, bf16[2,4,128,256]{3,2,1,0:T(8,128)(2,1)S(1)}, u32[]{:S(2)}, u32[]{:S(2)}) collective-permute-start(bf16[2,4,128,256]{3,2,1,0:T(8,128)(2,1)S(1)} %pad_maximum_fusion.2.rest_4_), channel_id=1, source_target_pairs={{0,8},{8,0},{16,24},{24,16},{1,9},{9,1},{17,25},{25,17},{2,10},{10... | collective-permute-start | bytes 1572872 | tf_op jit(solution)/shard_map/ppermute | solution.py:182
  120.4 18.9 %collective-permute-start.25 = (bf16[8,160,256]{2,1,0:T(8,128)(2,1)S(1)}, bf16[8,160,256]{2,1,0:T(8,128)(2,1)S(1)}, u32[]{:S(2)}, u32[]{:S(2)}) collective-permute-start(bf16[8,160,256]{2,1,0:T(8,128)(2,1)S(1)} %fusion), channel_id=1, source_target_pairs={{0,16},{8,24},{16,0},{24,8},{1,17},{9,25},{17,1},{25,9},{2,18},{10... | collective-permute-start | bytes 1966088 | tf_op jit(solution)/shard_map/ppermute | solution.py:179
  121.9 17.5 %collective-permute-start.24 = (bf16[4,256,256]{2,1,0:T(8,128)(2,1)S(1)}, bf16[4,256,256]{2,1,0:T(8,128)(2,1)S(1)}, u32[]{:S(2)}, u32[]{:S(2)}) collective-permute-start(bf16[4,256,256]{2,1,0:T(8,128)(2,1)S(1)} %slice.184), channel_id=1, source_target_pairs={{0,1},{1,0},{2,3},{3,2},{4,5},{5,4},{6,7},{7,6},{8,9},{9,8},{10,11... | collective-permute-start | bytes 1572872 | tf_op jit(solution)/shard_map/ppermute | solution.py:168
  139.1 20.1 %collective-permute-start.26 = (bf16[8,96,256]{2,1,0:T(8,128)(2,1)S(1)}, bf16[8,96,256]{2,1,0:T(8,128)(2,1)S(1)}, u32[]{:S(2)}, u32[]{:S(2)}) collective-permute-start(bf16[8,96,256]{2,1,0:T(8,128)(2,1)S(1)} %get-tuple-element.266), channel_id=1, source_target_pairs={{0,8},{8,0},{16,24},{24,16},{1,9},{9,1},{17,25},{25,17},{2,10},{10... | collective-permute-start | bytes 1179656 | tf_op jit(solution)/shard_map/ppermute | solution.py:182
  139.5 19.6 %collective-permute-start.28 = (bf16[4,160,256]{2,1,0:T(8,128)(2,1)S(1)}, bf16[4,160,256]{2,1,0:T(8,128)(2,1)S(1)}, u32[]{:S(2)}, u32[]{:S(2)}) collective-permute-start(bf16[4,160,256]{2,1,0:T(8,128)(2,1)S(1)} %slice.186), channel_id=1, source_target_pairs={{0,1},{1,0},{2,3},{3,2},{4,5},{5,4},{6,7},{7,6},{8,9},{9,8},{10,11... | collective-permute-start | bytes 983048 | tf_op jit(solution)/shard_map/ppermute | solution.py:168
  140.2 19.0 %collective-permute-start.27 = (bf16[2,256,256]{2,1,0:T(8,128)(2,1)S(1)}, bf16[2,256,256]{2,1,0:T(8,128)(2,1)S(1)}, u32[]{:S(2)}, u32[]{:S(2)}) collective-permute-start(bf16[2,256,256]{2,1,0:T(8,128)(2,1)S(1)} %slice.187), channel_id=1, source_target_pairs={{0,4},{1,5},{2,6},{3,7},{4,0},{5,1},{6,2},{7,3},{8,12},{9,13},{10,... | collective-permute-start | bytes 786440 | tf_op jit(solution)/shard_map/ppermute | solution.py:156
  161.5 12.7 %collective-permute-start.32 = (bf16[160,256]{1,0:T(8,128)(2,1)S(1)}, bf16[160,256]{1,0:T(8,128)(2,1)S(1)}, u32[]{:S(2)}, u32[]{:S(2)}) collective-permute-start(bf16[160,256]{1,0:T(8,128)(2,1)S(1)} %get-tuple-element.347), channel_id=1, source_target_pairs={{0,2},{1,3},{2,4},{3,5},{4,6},{5,7},{6,0},{7,1},{8,10},{9,11},{10,... | collective-permute-start | bytes 245768 | tf_op jit(solution)/shard_map/ppermute | solution.py:168
  163.0 11.1 %collective-permute-start.33 = (bf16[160,256]{1,0:T(8,128)(2,1)S(1)}, bf16[160,256]{1,0:T(8,128)(2,1)S(1)}, u32[]{:S(2)}, u32[]{:S(2)}) collective-permute-start(bf16[160,256]{1,0:T(8,128)(2,1)S(1)} %get-tuple-element.346), channel_id=1, source_target_pairs={{0,4},{1,5},{2,6},{3,7},{4,0},{5,1},{6,2},{7,3},{8,12},{9,13},{10,... | collective-permute-start | bytes 245768 | tf_op jit(solution)/shard_map/ppermute | solution.py:168
  165.5 11.6 %collective-permute-start.31 = (bf16[4,208,256]{2,1,0:T(8,128)(2,1)S(1)}, bf16[4,208,256]{2,1,0:T(8,128)(2,1)S(1)}, u32[]{:S(2)}, u32[]{:S(2)}) collective-permute-start(bf16[4,208,256]{2,1,0:T(8,128)(2,1)S(1)} %slice.185), channel_id=1, source_target_pairs={{0,1},{1,0},{2,3},{3,2},{4,5},{5,4},{6,7},{7,6},{8,9},{9,8},{10,11... | collective-permute-start | bytes 1277960 | tf_op jit(solution)/shard_map/ppermute | solution.py:168
  177.2 11.2 %collective-permute-start.35 = (bf16[416,256]{1,0:T(8,128)(2,1)S(1)}, bf16[416,256]{1,0:T(8,128)(2,1)S(1)}, u32[]{:S(2)}, u32[]{:S(2)}) collective-permute-start(bf16[416,256]{1,0:T(8,128)(2,1)S(1)} %pad_maximum_fusion.5), channel_id=1, source_target_pairs={{0,16},{8,24},{16,0},{24,8},{1,17},{9,25},{17,1},{25,9},{2,18},{10... | collective-permute-start | bytes 638984 | tf_op jit(solution)/shard_map/ppermute | solution.py:179
  178.5 10.1 %collective-permute-start.36 = (bf16[208,256]{1,0:T(8,128)(2,1)S(1)}, bf16[208,256]{1,0:T(8,128)(2,1)S(1)}, u32[]{:S(2)}, u32[]{:S(2)}) collective-permute-start(bf16[208,256]{1,0:T(8,128)(2,1)S(1)} %get-tuple-element.344), channel_id=1, source_target_pairs={{0,2},{1,3},{2,4},{3,5},{4,6},{5,7},{6,0},{7,1},{8,10},{9,11},{10,... | collective-permute-start | bytes 319496 | tf_op jit(solution)/shard_map/ppermute | solution.py:168
  (48 other events, 438.8 us)
